TPU v7x, 32 devices: a whole 2x2x4 slice. The times are simulated.
32 devices in a mesh: dp: 8 (over y, x, core), mp: 4 (over z).
Axes of the slice: x: 2, y: 2, z: 4, core: 2. Of those that a mesh axis runs over, the one named last changes fastest.
Arguments:
- tokens: bfloat16 [25600, 512], P('dp'), may hold values from -6 to 6
- cotangent: bfloat16 [25600, 512], P('dp'), may hold values from -6 to 6
- group_windows: int32 [8], P('dp'), may hold values from 16 to 32, as said below
- offset_index: int32 [100, 100], replicated, may hold values from 0 to 360, as said below
- first_gain: bfloat16 [512], replicated, may hold values from 0.099609375 to 1.8984375
- first_shift: bfloat16 [512], replicated, may hold values from -3 to 3
- triple_weight: bfloat16 [512, 3, 512], P(None, None, 'mp'), may hold values from -0.25 to 0.25
- query_value_bias: bfloat16 [2, 512], P(None, 'mp'), may hold values from -3 to 3
- bias_table: bfloat16 [361, 16], P(None, 'mp'), may hold values from -4 to 4
- output_weight: bfloat16 [512, 512], P('mp'), may hold values from -1 to 1
- output_bias: bfloat16 [512], replicated, may hold values from -3 to 3
- second_gain: bfloat16 [512], replicated, may hold values from 0.099609375 to 1.8984375
- second_shift: bfloat16 [512], replicated, may hold values from -3 to 3
- expand_weight: bfloat16 [512, 2048], P(None, 'mp'), may hold values from -0.25 to 0.25
- expand_bias: bfloat16 [2048], P('mp'), may hold values from -3 to 3
- shrink_weight: bfloat16 [2048, 512], P('mp'), may hold values from -0.125 to 0.125
- shrink_bias: bfloat16 [512], replicated, may hold values from -3 to 3
Outputs:
- block_output: bfloat16 [25600, 512], P('dp')
- grad_tokens: bfloat16 [25600, 512], P('dp')
- grad_first_gain: float32 [512], replicated
- grad_first_shift: float32 [512], replicated
- grad_triple_weight: float32 [512, 3, 512], P(None, None, 'mp')
- grad_query_value_bias: float32 [2, 512], P(None, 'mp')
- grad_bias_table: float32 [361, 16], P(None, 'mp')
- grad_output_weight: float32 [512, 512], P('mp')
- grad_output_bias: float32 [512], replicated
- grad_second_gain: float32 [512], replicated
- grad_second_shift: float32 [512], replicated
- grad_expand_weight: float32 [512, 2048], P(None, 'mp')
- grad_expand_bias: float32 [2048], P('mp')
- grad_shrink_weight: float32 [2048, 512], P('mp')
- grad_shrink_bias: float32 [512], replicated
Inputs may be any that keep to these rules, and one draw needn't show every extreme that they name: `group_windows`: entry g counts the windows of group g of dp; they fill its first window slots and the other slots of the 32 are empty; in every draw some group has all 32 filled. `offset_index`: entry [i, j] names the bias table row of the offset between positions i and j of a 10 x 10 window, positions row-major; equal offsets share a row and different offsets have different rows.
All inputs are finite; a program needn't handle non-finite values.
Results may differ from a plain program's by a relative error of at most 0.022.
Values may be sent and summed in bfloat16 or wider, within the bound.
A program may use at most 128 MiB of HBM per device.

v0:
```python
import jax
import jax.numpy as jnp
from jax import lax
from jax.sharding import PartitionSpec as P

AREA = 100


EPSILON = 1e-05
HALF_ROOT = 0.7071067811865476
DENSITY = 0.3989422804014327


def normalize(values):
    centered = values - jnp.mean(values, axis=-1, keepdims=True)
    inv_std = lax.rsqrt(jnp.mean(centered * centered, axis=-1, keepdims=True) + EPSILON)
    return (centered * inv_std, inv_std)


def norm_back(grad_hat, normed_hat, inv_std):
    return inv_std * (
        grad_hat
        - jnp.mean(grad_hat, axis=-1, keepdims=True)
        - normed_hat * jnp.mean(grad_hat * normed_hat, axis=-1, keepdims=True)
    )


def gelu_slope(hidden):
    return (
        0.5 * (1.0 + lax.erf(hidden * HALF_ROOT))
        + hidden * jnp.exp(-0.5 * hidden * hidden) * DENSITY
    )


def row_sums(values):
    return jnp.sum(values.astype(jnp.float32), axis=0)


def attention_scores(queries, key_rows, relative, score_scale):
    raw_scores = jnp.einsum(
        "wqhe,wkhe->whqk", queries, key_rows, preferred_element_type=jnp.float32
    )
    return raw_scores * score_scale + relative[None]


def local(
    tokens,
    cotangent,
    group_windows,
    offset_index,
    first_gain,
    first_shift,
    triple_weight,
    query_value_bias,
    bias_table,
    output_weight,
    output_bias,
    second_gain,
    second_shift,
    expand_weight,
    expand_bias,
    shrink_weight,
    shrink_bias,
):
    total_rows = tokens.shape[0]
    local_width = triple_weight.shape[2]
    local_heads = bias_table.shape[1]
    head_size = local_width // local_heads
    windows = total_rows // AREA
    score_scale = head_size ** (-0.5)
    head_shape = (windows, AREA, local_heads, head_size)
    window_slot = lax.broadcasted_iota(jnp.int32, (total_rows, 1), 0) // AREA
    live_mask = (window_slot < group_windows[0]).astype(jnp.float32)
    table_rows = bias_table.shape[0]
    lookup = (
        offset_index.reshape(AREA * AREA, 1) == lax.broadcasted_iota(jnp.int32, (1, table_rows), 1)
    ).astype(jnp.float32)
    relative = jnp.dot(lookup.astype(jnp.bfloat16), bias_table, preferred_element_type=jnp.float32)
    relative = jnp.transpose(relative.reshape(AREA, AREA, local_heads), (2, 0, 1))
    gain_first = first_gain.astype(jnp.float32)
    shift_first = first_shift.astype(jnp.float32)
    gain_second = second_gain.astype(jnp.float32)
    shift_second = second_shift.astype(jnp.float32)
    tokens_wide = tokens.astype(jnp.float32)
    first_hat, first_inv = normalize(tokens_wide)
    first_normed = (first_hat * gain_first + shift_first).astype(jnp.bfloat16)
    triple = jnp.einsum(
        "rd,dce->rce", first_normed, triple_weight, preferred_element_type=jnp.float32
    )
    bias_wide = query_value_bias.astype(jnp.float32)
    queries = (triple[:, 0] + bias_wide[0]).astype(jnp.bfloat16).reshape(head_shape)
    key_rows = triple[:, 1].astype(jnp.bfloat16).reshape(head_shape)
    value_rows = (triple[:, 2] + bias_wide[1]).astype(jnp.bfloat16).reshape(head_shape)
    scores = attention_scores(queries, key_rows, relative, score_scale)
    row_top = jnp.max(scores, axis=-1, keepdims=True)
    log_total = row_top + jnp.log(jnp.sum(jnp.exp(scores - row_top), axis=-1, keepdims=True))
    probs_low = jnp.exp(scores - log_total).astype(jnp.bfloat16)
    mixed = jnp.einsum("whqk,wkhe->wqhe", probs_low, value_rows, preferred_element_type=jnp.float32)
    mixed = mixed.reshape(total_rows, local_width).astype(jnp.bfloat16)
    branch_term = jnp.dot(mixed, output_weight, preferred_element_type=jnp.float32)
    middle = (
        tokens_wide
        + lax.psum(branch_term.astype(jnp.bfloat16), "mp").astype(jnp.float32)
        + output_bias.astype(jnp.float32)
    )
    second_hat, second_inv = normalize(middle)
    second_normed = (second_hat * gain_second + shift_second).astype(jnp.bfloat16)
    hidden = jnp.dot(
        second_normed, expand_weight, preferred_element_type=jnp.float32
    ) + expand_bias.astype(jnp.float32)
    active = jax.nn.gelu(hidden, approximate=False).astype(jnp.bfloat16)
    shrink_term = jnp.dot(active, shrink_weight, preferred_element_type=jnp.float32)
    grad_result = cotangent.astype(jnp.float32) * live_mask
    result = (
        middle
        + lax.psum(shrink_term.astype(jnp.bfloat16), "mp").astype(jnp.float32)
        + shrink_bias.astype(jnp.float32)
    )
    result = result * live_mask
    grad_low = grad_result.astype(jnp.bfloat16)
    grad_shrink_weight = jnp.einsum(
        "rf,rd->fd", active, grad_low, preferred_element_type=jnp.float32
    )
    grad_shrink_bias = row_sums(grad_low)
    grad_active = jnp.einsum(
        "rd,fd->rf", grad_low, shrink_weight, preferred_element_type=jnp.float32
    )
    grad_hidden = (grad_active * gelu_slope(hidden)).astype(jnp.bfloat16)
    grad_expand_weight = jnp.einsum(
        "rd,rf->df", second_normed, grad_hidden, preferred_element_type=jnp.float32
    )
    grad_expand_bias = row_sums(grad_hidden)
    second_back = jnp.einsum(
        "rf,df->rd", grad_hidden, expand_weight, preferred_element_type=jnp.float32
    )
    grad_second = lax.psum(second_back.astype(jnp.bfloat16), "mp").astype(jnp.float32)
    grad_middle = grad_result + norm_back(grad_second * gain_second, second_hat, second_inv)
    grad_branch = grad_middle.astype(jnp.bfloat16)
    second_gain_term = jnp.sum(grad_second * second_hat, axis=0)
    second_shift_term = jnp.sum(grad_second, axis=0)
    grad_output_weight = jnp.einsum(
        "rc,rd->cd", mixed, grad_branch, preferred_element_type=jnp.float32
    )
    grad_output_bias = row_sums(grad_branch)
    grad_mixed = jnp.einsum(
        "rd,cd->rc", grad_branch, output_weight, preferred_element_type=jnp.float32
    )
    grad_mixed = grad_mixed.astype(jnp.bfloat16).reshape(head_shape)
    grad_value = jnp.einsum(
        "whqk,wqhe->wkhe", probs_low, grad_mixed, preferred_element_type=jnp.float32
    ).astype(jnp.bfloat16)
    attn_probs = jnp.exp(attention_scores(queries, key_rows, relative, score_scale) - log_total)
    grad_probs = jnp.einsum(
        "wqhe,wkhe->whqk", grad_mixed, value_rows, preferred_element_type=jnp.float32
    )
    grad_scores = (
        attn_probs * (grad_probs - jnp.sum(attn_probs * grad_probs, axis=-1, keepdims=True))
    ).astype(jnp.bfloat16)
    grad_query = (
        jnp.einsum("whqk,wkhe->wqhe", grad_scores, key_rows, preferred_element_type=jnp.float32)
        * score_scale
    ).astype(jnp.bfloat16)
    grad_key = (
        jnp.einsum("whqk,wqhe->wkhe", grad_scores, queries, preferred_element_type=jnp.float32)
        * score_scale
    ).astype(jnp.bfloat16)
    score_totals = jnp.sum(grad_scores.astype(jnp.float32), axis=0)
    score_totals = jnp.transpose(score_totals, (1, 2, 0)).reshape(AREA * AREA, local_heads)
    grad_bias_table = jnp.dot(lookup.T, score_totals, precision=lax.Precision.HIGHEST)
    grad_triple = jnp.stack(
        [
            grad_query.reshape(total_rows, local_width),
            grad_key.reshape(total_rows, local_width),
            grad_value.reshape(total_rows, local_width),
        ],
        axis=1,
    )
    grad_triple_weight = jnp.einsum(
        "rd,rce->dce", first_normed, grad_triple, preferred_element_type=jnp.float32
    )
    grad_query_value_bias = jnp.stack([row_sums(grad_triple[:, 0]), row_sums(grad_triple[:, 2])])
    first_back = jnp.einsum(
        "rce,dce->rd", grad_triple, triple_weight, preferred_element_type=jnp.float32
    )
    grad_first = lax.psum(first_back.astype(jnp.bfloat16), "mp").astype(jnp.float32)
    grad_input = grad_middle + norm_back(grad_first * gain_first, first_hat, first_inv)
    first_gain_term = jnp.sum(grad_first * first_hat, axis=0)
    first_shift_term = jnp.sum(grad_first, axis=0)
    block_output = result.astype(jnp.bfloat16)
    grad_tokens = grad_input.astype(jnp.bfloat16)
    summed = (
        lax.psum(first_gain_term.astype(jnp.bfloat16), "dp").astype(jnp.float32),
        lax.psum(first_shift_term.astype(jnp.bfloat16), "dp").astype(jnp.float32),
        lax.psum(grad_triple_weight.astype(jnp.bfloat16), "dp").astype(jnp.float32),
        lax.psum(grad_query_value_bias.astype(jnp.bfloat16), "dp").astype(jnp.float32),
        lax.psum(grad_bias_table.astype(jnp.bfloat16), "dp").astype(jnp.float32),
        lax.psum(grad_output_weight.astype(jnp.bfloat16), "dp").astype(jnp.float32),
        lax.psum(grad_output_bias.astype(jnp.bfloat16), "dp").astype(jnp.float32),
        lax.psum(second_gain_term.astype(jnp.bfloat16), "dp").astype(jnp.float32),
        lax.psum(second_shift_term.astype(jnp.bfloat16), "dp").astype(jnp.float32),
        lax.psum(grad_expand_weight.astype(jnp.bfloat16), "dp").astype(jnp.float32),
        lax.psum(grad_expand_bias.astype(jnp.bfloat16), "dp").astype(jnp.float32),
        lax.psum(grad_shrink_weight.astype(jnp.bfloat16), "dp").astype(jnp.float32),
        lax.psum(grad_shrink_bias.astype(jnp.bfloat16), "dp").astype(jnp.float32),
    )
    return (
        block_output,
        grad_tokens,
        summed[0],
        summed[1],
        summed[2],
        summed[3],
        summed[4],
        summed[5],
        summed[6],
        summed[7],
        summed[8],
        summed[9],
        summed[10],
        summed[11],
        summed[12],
    )


def solution(mesh):
    in_specs = (
        P("dp", None),
        P("dp", None),
        P("dp"),
        P(),
        P(),
        P(),
        P(None, None, "mp"),
        P(None, "mp"),
        P(None, "mp"),
        P("mp", None),
        P(),
        P(),
        P(),
        P(None, "mp"),
        P("mp"),
        P("mp", None),
        P(),
    )
    out_specs = (
        P("dp", None),
        P("dp", None),
        P(),
        P(),
        P(None, None, "mp"),
        P(None, "mp"),
        P(None, "mp"),
        P("mp", None),
        P(),
        P(),
        P(),
        P(None, "mp"),
        P("mp"),
        P("mp", None),
        P(),
    )
    return jax.shard_map(local, mesh=mesh, in_specs=in_specs, out_specs=out_specs, check_vma=False)
```

profile of v0, /device:TPU:0, one launch (start us, length us, event | category | flops | bytes accessed | tf_op | source)
XLA Modules:
  0.0 764.0 jit_solution(16358423675704268554)
XLA Ops:
  9.1 2.4 convert_reduce_fusion
  11.5 3.2 fusion.20
  25.6 3.9 convert_element_type.228
  29.6 6.3 squeeze.11
  35.9 2.7 copy.69
  38.5 6.1 squeeze.10
  48.7 2.8 fusion.45
  59.0 2.7 convolution_convert_fusion.2
  63.0 127.0 %all-reduce.8.cloned.1.call-done = bf16[3200,512]{1,0:T(8,128)(2,1)} async-done(((bf16[3200,512]{1,0:T(8,128)(2,1)}), bf16[3200,512]{1,0:T(8,128)(2,1)}) %all-reduce.8.cloned.1.call-update) | async-done | bytes 3276816 | tf_op jit(solution)/shard_map/psum | solution.py:103
  190.0 4.2 fusion.48
  198.9 17.0 %fusion.31 = (bf16[3200,512]{1,0:T(8,128)(2,1)}, f32[3200,512]{1,0:T(8,128)S(1)}) fusion(f32[512]{0:T(512)S(1)} %convert_element_type.241, bf16[3200,512]{1,0:T(8,128)(2,1)S(1)} %add_convert_fusion, bf16[512,512]{1,0:T(8,128)(2,1)S(1)} %copy-done), kind=kOutput, calls=%fused_computation.50 | convolution fusion | flops 1785856000 | bytes 13633536 | tf_op jit(solution)/shard_map/dot_general | solution.py:108
  215.9 5.0 fusion.85
  222.6 3.7 convolution_convert_fusion
  226.4 5.8 convolution_convert_fusion.7
  232.2 2.8 convolution_convert_fusion.6
  235.0 115.8 %all-reduce.10.cloned.1.call-done = bf16[3200,512]{1,0:T(8,128)(2,1)} async-done(((bf16[3200,512]{1,0:T(8,128)(2,1)}), bf16[3200,512]{1,0:T(8,128)(2,1)}) %all-reduce.10.cloned.1.call-update) | async-done | bytes 3276816 | tf_op jit(solution)/shard_map/psum | solution.py:136
  350.8 8.9 %fusion.25 = (bf16[512]{0:T(512)(128)(2,1)S(1)}, f32[3200]{0:T(1024)S(1)}, f32[3200]{0:T(1024)S(1)}) fusion(bf16[3200,512]{1,0:T(8,128)(2,1)} %all-reduce.10.cloned.1.call-done, f32[3200]{0:T(1024)S(1)} %add_rsqrt_fusion, f32[3200]{0:T(1024)S(1)} %broadcast_multiply_fusion.4, f32[512]{0:T(512)S(1)} %convert_element_type.237, ...), kind=kLoop, calls=%fused_computation.44 | loop fusion | flops 21292288 | bytes 9886720 | tf_op jit(solution)/shard_map/reduce_sum | solution.py:139
  359.7 8.1 %convert_reduce_fusion.2 = (bf16[512]{0:T(512)(128)(2,1)S(1)}, f32[3200,512]{1,0:T(8,128)S(1)}, bf16[512]{0:T(512)(128)(2,1)S(1)}, bf16[512]{0:T(512)(128)(2,1)S(1)}) fusion(f32[3200]{0:T(1024)S(1)} %get-tuple-element.60, f32[3200]{0:T(1024)S(1)} %broadcast_multiply_fusion.4, f32[512]{0:T(512)S(1)} %convert_element_type.237, ...), kind=kLoop, calls=%fused_computation.137 | loop fusion | flops 32766464 | bytes 19731968 | tf_op jit(solution)/shard_map/reduce_sum | solution.py:36
  374.9 5.8 reshape.150
  380.7 5.4 fusion.83
  386.1 3.5 multiply_reduce_fusion
  389.7 2.8 convert_reduce_fusion.1
  392.5 2.8 fusion.52
  409.6 6.0 convolution_convert_fusion.8
  415.8 5.7 convolution_convert_fusion.1
  421.5 3.6 bitcast_convert_fusion
  426.3 5.1 fusion.53
  431.4 42.8 %all-reduce.12.cloned.1.call-done = (bf16[512,3,128]{2,0,1:T(8,128)(2,1)}, bf16[128,512]{1,0:T(8,128)(2,1)}, bf16[512,512]{1,0:T(8,128)(2,1)}, bf16[512,512]{1,0:T(8,128)(2,1)}) async-done(((bf16[512,3,128]{2,0,1:T(8,128)(2,1)}, bf16[128,512]{1,0:T(8,128)(2,1)}, bf16[512,512]{1,0:T(8,128)(2,1)}, bf16[512,512]{1,0:T(8,128)(2,1)}), (bf16[512,3,128]{2,0,1:T(8,128)(2,1)}, bf16[128,512]{1,0:T(8,128)(2,1)}, ...) | async-done | bytes 1572880 | tf_op jit(solution)/shard_map/psum | solution.py:194
  482.1 226.2 %all-reduce.14.cloned.1.call-done = (bf16[3200,512]{1,0:T(8,128)(2,1)}, bf16[3200,512]{1,0:T(8,128)(2,1)}) async-done(((bf16[3200,512]{1,0:T(8,128)(2,1)}, bf16[3200,512]{1,0:T(8,128)(2,1)}), (bf16[3200,512]{1,0:T(8,128)(2,1)}, bf16[3200,512]{1,0:T(8,128)(2,1)})) %all-reduce.14.cloned.1.call-update) | async-done | bytes 6553616 | tf_op jit(solution)/shard_map/psum | solution.py:116
  708.3 6.6 fusion.27
  717.3 24.0 %all-reduce = (bf16[512]{0:T(512)(128)(2,1)S(1)}, bf16[512]{0:T(512)(128)(2,1)S(1)}, bf16[2,128]{1,0:T(2,128)(2,1)S(1)}, bf16[361,4]{0,1:T(4,128)(2,1)S(1)}, bf1...) all-reduce(bf16[512]{0:T(512)(128)(2,1)S(1)} %get-tuple-element.17,, ...), channel_id=1, replica_groups=mesh['dp'=8,'mp'=4] {'dp'}, use_global_device_ids=true, to_apply=%region_16.17 | all-reduce | flops 5284 | bytes 21136 | tf_op jit(solution)/shard_map/psum | solution.py:192
  746.5 10.8 %fusion.19 = (bf16[3200,512]{1,0:T(8,128)(2,1)}, bf16[3200,512]{1,0:T(8,128)(2,1)}) fusion(f32[3200,512]{1,0:T(8,128)} %copy-done.8, bf16[3200,512]{1,0:T(8,128)(2,1)} %param.17, bf16[3200,512]{1,0:T(8,128)(2,1)} %get-tuple-element.37, f32[3200]{0:T(1024)S(1)} %broadcast_multiply_fusion, f32[3200]{0:T(1024)S(1)} %broadcast_multiply_fusion.1, ...), kind=kLoop, calls=%fused_computation.38 | loop fusion | flops 31129600 | bytes 26284544 | tf_op jit(solution)/shard_map/convert_element_type | solution.py:190
  (154 shorter events, 69.0 us)
Async XLA Ops:
  7.2 191.7 %copy-start = (bf16[512,512]{1,0:T(8,128)(2,1)S(1)}, bf16[512,512]{1,0:T(8,128)(2,1)}, u32[]{:S(2)}) copy-start(bf16[512,512]{1,0:T(8,128)(2,1)} %param.30) | copy-start | bytes 1572868
  7.2 7.5 copy-start.30
  7.2 182.7 %all-reduce.8.cloned.1.call-start = ((), (), s32[]{:S(2)}) async-start(), calls=%async_computation | async-start | bytes 6553600 | tf_op jit(solution)/shard_map/psum | solution.py:103
  7.3 7.5 copy-start.2
  29.5 19.2 %copy-start.11 = (bf16[32,100,4,32]{1,0,3,2:T(8,128)(2,1)}, bf16[32,100,4,32]{1,0,3,2:T(8,128)(2,1)S(1)}, u32[]{:S(2)}) copy-start(bf16[32,100,4,32]{1,0,3,2:T(8,128)(2,1)S(1)} %convert_element_type.228) | copy-start | bytes 2457604
  46.5 5.1 copy-start.15
  48.7 5.1 copy-start.13
  53.8 5.2 copy-start.22
  57.0 5.9 copy-start.24
  57.0 5.9 copy-start.25
  57.0 5.9 copy-start.26
  57.0 5.9 copy-start.27
  61.8 289.0 %all-reduce.10.cloned.1.call-start = ((), (), s32[]{:S(2)}) async-start(), calls=%async_computation.1 | async-start | bytes 6553600 | tf_op jit(solution)/shard_map/psum | solution.py:136
  198.9 17.0 %copy-start.19 = (bf16[3200,512]{1,0:T(8,128)(2,1)}, bf16[3200,512]{1,0:T(8,128)(2,1)S(1)}, u32[]{:S(2)}) copy-start(bf16[3200,512]{1,0:T(8,128)(2,1)S(1)} %add_convert_fusion) | copy-start | bytes 9830404
  198.9 17.0 %copy-start.17 = (bf16[3200,512]{1,0:T(8,128)(2,1)S(1)}, bf16[3200,512]{1,0:T(8,128)(2,1)}, u32[]{:S(2)}) copy-start(bf16[3200,512]{1,0:T(8,128)(2,1)} %param.18) | copy-start | bytes 9830404
  198.9 17.0 %copy-start.29 = (bf16[512,512]{1,0:T(8,128)(2,1)S(1)}, bf16[512,512]{1,0:T(8,128)(2,1)}, u32[]{:S(2)}) copy-start(bf16[512,512]{1,0:T(8,128)(2,1)} %param.32) | copy-start | bytes 1572868
  226.3 247.9 %all-reduce.12.cloned.1.call-start = ((), (), s32[]{:S(2)}) async-start(), calls=%async_computation.2 | async-start | bytes 3145728 | tf_op jit(solution)/shard_map/psum | solution.py:194
  226.4 5.8 copy-start.18
  226.4 5.8 copy-start.34
  350.8 8.9 %copy-start.4 = (bf16[3200,512]{1,0:T(8,128)(2,1)S(1)}, bf16[3200,512]{1,0:T(8,128)(2,1)}, u32[]{:S(2)}) copy-start(bf16[3200,512]{1,0:T(8,128)(2,1)} %param.17) | copy-start | bytes 9830404
  350.8 8.9 %copy-start.7 = (bf16[3200,512]{1,0:T(8,128)(2,1)S(1)}, bf16[3200,512]{1,0:T(8,128)(2,1)}, u32[]{:S(2)}) copy-start(bf16[3200,512]{1,0:T(8,128)(2,1)} %all-reduce.8.cloned.1.call-done) | copy-start | bytes 9830404
  350.8 8.9 %copy-start.9 = (bf16[3200,512]{1,0:T(8,128)(2,1)S(1)}, bf16[3200,512]{1,0:T(8,128)(2,1)}, u32[]{:S(2)}) copy-start(bf16[3200,512]{1,0:T(8,128)(2,1)} %all-reduce.10.cloned.1.call-done) | copy-start | bytes 9830404
  372.5 13.6 %slice-start = ((s8[6815744]{0:T(1024)(128)(4,1)}), s8[2621440]{0:T(1024)(128)(4,1)S(1)}, s32[]{:S(2)}) async-start(s8[6815744]{0:T(1024)(128)(4,1)} %bitcast.70), calls=%async_computation.4 | async-start | bytes 5242880
  380.7 5.4 slice-start.1
  380.7 5.4 copy-start.10
  380.7 5.4 copy-start.14
  389.7 5.7 copy-start.12
  415.7 5.8 copy-start.20
  415.7 5.8 copy-start.21
  415.7 292.6 %all-reduce.14.cloned.1.call-start = ((), (), s32[]{:S(2)}) async-start(), calls=%async_computation.3 | async-start | bytes 13107200 | tf_op jit(solution)/shard_map/psum | solution.py:116
  415.7 5.7 copy-start.31
  746.5 10.8 %copy-start.1 = (bf16[512,512]{1,0:T(8,128)(2,1)S(1)}, bf16[512,512]{1,0:T(8,128)(2,1)}, u32[]{:S(2)}) copy-start(bf16[512,512]{1,0:T(8,128)(2,1)} %param.30) | copy-start | bytes 1572868
  (10 other events, 29.5 us)
Sparse Core Ops, SparseCore 0:
  61.9 128.0 all-reduce.7
  226.4 124.3 all-reduce.9
  415.8 58.3 all-reduce.11
  477.2 231.0 all-reduce.13
where the time goes:
time: 770 us; the launch traced here: 764 us
  waiting for transfers between devices  512 us (66%)
  matrix products  83.9 us (11%)
  other arithmetic  74.7 us (10%)
  local copies, waits for them, and re-layouts  53.7 us (7%)
  blocking collectives  24 us (3%)
  between operations  15.2 us (2%)
    psum x1, waiting for transfers between devices, local(): lax.psum(shrink_term.astype(jnp.bfloat16), 'mp').astype(jnp.float32)  226 us
    psum x1, waiting for transfers between devices, local(): lax.psum(branch_term.astype(jnp.bfloat16), 'mp').astype(jnp.float32)  127 us
    psum x1, waiting for transfers between devices, local(): lax.psum(second_back.astype(jnp.bfloat16), 'mp').astype(jnp.float32)  116 us
    psum x1, waiting for transfers between devices, local(): lax.psum(grad_triple_weight.astype(jnp.bfloat16), 'dp').astype(jnp.float32)  42.8 us
    psum x1, blocking collectives, local(): lax.psum(first_gain_term.astype(jnp.bfloat16), 'dp').astype(jnp.float32)  24 us
    dot_general x1, matrix products, local(): jnp.dot(second_normed, expand_weight, preferred_element_type=jnp.float32)  17 us
  transfers between devices with their start and end apart: 4, of which 4 were waited for; matrix products, arithmetic and copies ran while one was open for 4% of the time, Pallas kernels for 0%

commit v1 on v0

--- a/solution.py
+++ b/solution.py
@@ -62,14 +62,26 @@
     shrink_weight,
     shrink_bias,
 ):
-    total_rows = tokens.shape[0]
+    mp_size = lax.axis_size("mp")
+    mp_index = lax.axis_index("mp")
+    total_rows = tokens.shape[0] // mp_size
+    first_row = mp_index * total_rows
+    tokens = lax.dynamic_slice_in_dim(tokens, first_row, total_rows, 0)
+    cotangent = lax.dynamic_slice_in_dim(cotangent, first_row, total_rows, 0)
+    triple_weight = lax.all_gather(triple_weight, "mp", axis=2, tiled=True)
+    query_value_bias = lax.all_gather(query_value_bias, "mp", axis=1, tiled=True)
+    bias_table = lax.all_gather(bias_table, "mp", axis=1, tiled=True)
+    output_weight = lax.all_gather(output_weight, "mp", axis=0, tiled=True)
+    expand_weight = lax.all_gather(expand_weight, "mp", axis=1, tiled=True)
+    expand_bias = lax.all_gather(expand_bias, "mp", axis=0, tiled=True)
+    shrink_weight = lax.all_gather(shrink_weight, "mp", axis=0, tiled=True)
     local_width = triple_weight.shape[2]
     local_heads = bias_table.shape[1]
     head_size = local_width // local_heads
     windows = total_rows // AREA
     score_scale = head_size ** (-0.5)
     head_shape = (windows, AREA, local_heads, head_size)
-    window_slot = lax.broadcasted_iota(jnp.int32, (total_rows, 1), 0) // AREA
+    window_slot = (first_row + lax.broadcasted_iota(jnp.int32, (total_rows, 1), 0)) // AREA
     live_mask = (window_slot < group_windows[0]).astype(jnp.float32)
     table_rows = bias_table.shape[0]
     lookup = (
@@ -100,7 +112,7 @@
     branch_term = jnp.dot(mixed, output_weight, preferred_element_type=jnp.float32)
     middle = (
         tokens_wide
-        + lax.psum(branch_term.astype(jnp.bfloat16), "mp").astype(jnp.float32)
+        + branch_term
         + output_bias.astype(jnp.float32)
     )
     second_hat, second_inv = normalize(middle)
@@ -113,7 +125,7 @@
     grad_result = cotangent.astype(jnp.float32) * live_mask
     result = (
         middle
-        + lax.psum(shrink_term.astype(jnp.bfloat16), "mp").astype(jnp.float32)
+        + shrink_term
         + shrink_bias.astype(jnp.float32)
     )
     result = result * live_mask
@@ -133,7 +145,7 @@
     second_back = jnp.einsum(
         "rf,df->rd", grad_hidden, expand_weight, preferred_element_type=jnp.float32
     )
-    grad_second = lax.psum(second_back.astype(jnp.bfloat16), "mp").astype(jnp.float32)
+    grad_second = second_back
     grad_middle = grad_result + norm_back(grad_second * gain_second, second_hat, second_inv)
     grad_branch = grad_middle.astype(jnp.bfloat16)
     second_gain_term = jnp.sum(grad_second * second_hat, axis=0)
@@ -182,26 +194,34 @@
     first_back = jnp.einsum(
         "rce,dce->rd", grad_triple, triple_weight, preferred_element_type=jnp.float32
     )
-    grad_first = lax.psum(first_back.astype(jnp.bfloat16), "mp").astype(jnp.float32)
+    grad_first = first_back
     grad_input = grad_middle + norm_back(grad_first * gain_first, first_hat, first_inv)
     first_gain_term = jnp.sum(grad_first * first_hat, axis=0)
     first_shift_term = jnp.sum(grad_first, axis=0)
-    block_output = result.astype(jnp.bfloat16)
-    grad_tokens = grad_input.astype(jnp.bfloat16)
+    block_output = lax.all_gather(result.astype(jnp.bfloat16), "mp", axis=0, tiled=True)
+    grad_tokens = lax.all_gather(grad_input.astype(jnp.bfloat16), "mp", axis=0, tiled=True)
+
+    def total(value, axis=None):
+        value = value.astype(jnp.bfloat16)
+        if axis is None:
+            return lax.psum(value, ("mp", "dp")).astype(jnp.float32)
+        value = lax.psum_scatter(value, "mp", scatter_dimension=axis, tiled=True)
+        return lax.psum(value, "dp").astype(jnp.float32)
+
     summed = (
-        lax.psum(first_gain_term.astype(jnp.bfloat16), "dp").astype(jnp.float32),
-        lax.psum(first_shift_term.astype(jnp.bfloat16), "dp").astype(jnp.float32),
-        lax.psum(grad_triple_weight.astype(jnp.bfloat16), "dp").astype(jnp.float32),
-        lax.psum(grad_query_value_bias.astype(jnp.bfloat16), "dp").astype(jnp.float32),
-        lax.psum(grad_bias_table.astype(jnp.bfloat16), "dp").astype(jnp.float32),
-        lax.psum(grad_output_weight.astype(jnp.bfloat16), "dp").astype(jnp.float32),
-        lax.psum(grad_output_bias.astype(jnp.bfloat16), "dp").astype(jnp.float32),
-        lax.psum(second_gain_term.astype(jnp.bfloat16), "dp").astype(jnp.float32),
-        lax.psum(second_shift_term.astype(jnp.bfloat16), "dp").astype(jnp.float32),
-        lax.psum(grad_expand_weight.astype(jnp.bfloat16), "dp").astype(jnp.float32),
-        lax.psum(grad_expand_bias.astype(jnp.bfloat16), "dp").astype(jnp.float32),
-        lax.psum(grad_shrink_weight.astype(jnp.bfloat16), "dp").astype(jnp.float32),
-        lax.psum(grad_shrink_bias.astype(jnp.bfloat16), "dp").astype(jnp.float32),
+        total(first_gain_term),
+        total(first_shift_term),
+        total(grad_triple_weight, 2),
+        total(grad_query_value_bias, 1),
+        total(grad_bias_table, 1),
+        total(grad_output_weight, 0),
+        total(grad_output_bias),
+        total(second_gain_term),
+        total(second_shift_term),
+        total(grad_expand_weight, 1),
+        total(grad_expand_bias, 0),
+        total(grad_shrink_weight, 0),
+        total(grad_shrink_bias),
     )
     return (
         block_output,

time: 770 us -> 593 us (0.77)
  waiting for transfers between devices: 512 us -> 264 us
  blocking collectives: 24 us -> 130 us
  other arithmetic: 74.7 us -> 33.8 us
    psum x4 -> x1, waiting for transfers between devices: 512 us -> 62.6 us  [total(): return lax.psum(value, 'dp').astype(jnp.float32)]
    reduce_scatter x0 -> x3, waiting for transfers between devices: none -> 110 us  [total(): value = lax.psum_scatter(value, 'mp', scatter_dimension=axis, tiled=True)]
    all_gather x0 -> x5, waiting for transfers between devices: none -> 82.1 us  [the longest x1 66.4 us: local(): lax.all_gather(grad_input.astype(jnp.bfloat16), 'mp', axis=0, tiled=True)]
    all_gather x0 -> x4, blocking collectives: none -> 59.4 us  [the longest x1 18.9 us: local(): output_weight = lax.all_gather(output_weight, 'mp', axis=0, tiled=True)]
    psum x1 -> x2, blocking collectives: 24 us -> 52.5 us  [the longest x1 39.7 us: total(): return lax.psum(value, ('mp', 'dp')).astype(jnp.float32)]
    unnamed x0 -> x1, blocking collectives: none -> 18.4 us
    reduce_sum x3 -> x0, other arithmetic: 17.9 us -> none  [the longest x1 8.86 us: local(): second_gain_term = jnp.sum(grad_second * second_hat, axis=0)]
    unnamed x76 -> x105, local copies, waits for them, and re-layouts: 4.11 us -> 19.2 us
  transfers between devices with their start and end apart: 4 -> 11, of which waited for: 4 -> 8; matrix products, arithmetic and copies ran while one was open for 4% -> 18% of each run, Pallas kernels for 0% -> 0%
where the time goes in v1:
time: 593 us; the launch traced here: 588 us
  waiting for transfers between devices  264 us (45%)
  blocking collectives  130 us (22%)
  matrix products  86.5 us (15%)
  local copies, waits for them, and re-layouts  55.4 us (9%)
  other arithmetic  33.8 us (6%)
  between operations  17 us (3%)
    reduce_scatter x3, waiting for transfers between devices, total(): value = lax.psum_scatter(value, 'mp', scatter_dimension=axis, tiled=True)  110 us
    all_gather x1, waiting for transfers between devices, local(): lax.all_gather(grad_input.astype(jnp.bfloat16), 'mp', axis=0, tiled=True)  66.4 us
    psum x1, waiting for transfers between devices, total(): return lax.psum(value, 'dp').astype(jnp.float32)  62.6 us
    psum x1, blocking collectives, total(): return lax.psum(value, ('mp', 'dp')).astype(jnp.float32)  39.7 us
    dot_general x1, matrix products, local(): jnp.dot(second_normed, expand_weight, preferred_element_type=jnp.float32)  19.3 us
    unnamed x105, local copies, waits for them, and re-layouts  19.2 us
    all_gather x1, blocking collectives, local(): output_weight = lax.all_gather(output_weight, 'mp', axis=0, tiled=True)  18.9 us
    unnamed x1, blocking collectives  18.4 us
  transfers between devices with their start and end apart: 11, of which 8 were waited for; matrix products, arithmetic and copies ran while one was open for 18% of the time, Pallas kernels for 0%

profile of v1, /device:TPU:0, one launch (start us, length us, event | category | flops | bytes accessed | tf_op | source)
XLA Modules:
  0.0 587.8 jit_solution(14676501665583845716)
XLA Ops:
  12.9 12.8 %all_gather.28 = bf16[2,512]{1,0:T(2,128)(2,1)S(1)} all-gather(bf16[2,128]{1,0:T(2,128)(2,1)} %param.24), channel_id=1, replica_groups=mesh['dp'=8,'mp'=4] {'mp'}, dimensions={1}, use_global_device_ids=true | all-gather | bytes 2560 | tf_op jit(solution)/shard_map/all_gather | solution.py:72
  30.0 13.5 %all-gather.1 = bf16[4,1,512]{2,1,0:T(2,128)(2,1)S(1)} all-gather(bf16[1,1,512]{2,1,0:T(2,128)(2,1)S(1)} %reshape.152), channel_id=1, replica_groups=mesh['dp'=8,'mp'=4] {'mp'}, dimensions={0}, use_global_device_ids=true | all-gather | bytes 5120 | tf_op jit(solution)/shard_map/all_gather | solution.py:76
  43.7 14.2 %all-gather = bf16[4,4,361]{2,1,0:T(4,128)(2,1)S(1)} all-gather(bf16[1,4,361]{2,1,0:T(4,128)(2,1)} %bitcast.95), channel_id=1, replica_groups=mesh['dp'=8,'mp'=4] {'mp'}, dimensions={0}, use_global_device_ids=true | all-gather | bytes 14440 | tf_op jit(solution)/shard_map/all_gather | solution.py:73
  58.1 18.9 %all_gather.30 = bf16[512,512]{1,0:T(8,128)(2,1)} all-gather(bf16[128,512]{1,0:T(8,128)(2,1)S(1)} %copy-done.21), channel_id=1, replica_groups=mesh['dp'=8,'mp'=4] {'mp'}, dimensions={0}, use_global_device_ids=true | all-gather | bytes 655360 | tf_op jit(solution)/shard_map/all_gather | solution.py:74
  80.1 3.2 fusion.58
  87.4 3.1 copy.68
  90.5 3.3 squeeze.11
  96.5 3.3 squeeze.10
  113.9 19.3 %fusion.6 = (bf16[800,2048]{1,0:T(8,128)(2,1)}, f32[800,2048]{1,0:T(8,128)}) fusion(f32[2048]{0:T(1024)S(1)} %bitcast.93, bf16[512,2048]{1,0:T(8,128)(2,1)} %all-gather.10.cloned.1.call-done, f32[800,512]{1,0:T(8,128)S(1)} %get-tuple-element.50, f32[512]{0:T(512)S(1)} %convert_element_type.217, f32[512]{0:T(512)S(1)} %convert_element_type.216, ...), kind=kOutput, calls=%fused_computation.16 | convolution fusion | flops 1787904000 | bytes 13584640 | tf_op jit(solution)/shard_map/dot_general | solution.py:120
  133.2 12.6 %all-gather.12.cloned.1.call-done = bf16[2048,512]{1,0:T(8,128)(2,1)} async-done(((bf16[512,512]{1,0:T(8,128)(2,1)}), bf16[2048,512]{1,0:T(8,128)(2,1)}) %all-gather.12.cloned.1.call-update) | async-done | bytes 2097168 | tf_op jit(solution)/shard_map/all_gather | solution.py:77
  145.8 7.4 %fusion.79 = (bf16[2048]{0:T(1024)(128)(2,1)}, bf16[800,2048]{1,0:T(8,128)(2,1)S(1)}) fusion(f32[800,2048]{1,0:T(8,128)} %get-tuple-element.52, f32[2048]{0:T(1024)S(1)} %bitcast.94, bf16[2048,512]{1,0:T(8,128)(2,1)} %all-gather.12.cloned.1.call-done, f32[800]{0:T(1024)S(1)} %fusion.61, bf16[3200,512]{1,0:T(8,128)(2,1)} %param.18, s32[]{:T(128)S(6)} %select_n.14), kind=kOutput, calls=%fused_computation.136 | convolution fusion | flops 1698609152 | bytes 12762244 | tf_op jit(solution)/shard_map/rd,fd->rf/dot_general | solution.py:137
  163.5 3.3 reshape.148
  166.9 6.0 %fusion.77 = (bf16[16,32]{1,0:T(8,128)(2,1)}, bf16[8,100,16,32]{1,3,2,0:T(8,128)(2,1)S(1)}) fusion(f32[8,16,100,100]{2,3,1,0:T(8,128)} %copy-done, f32[8,16,100]{2,1,0:T(8,128)S(1)} %log_add_fusion, f32[16,100,100]{1,2,0:T(8,128)S(1)} %copy.72, bf16[8,100,16,32]{1,0,3,2:T(8,128)(2,1)} %reshape.148), kind=kOutput, calls=%fused_computation.134 | convolution fusion | flops 87858688 | bytes 7450624 | tf_op jit(solution)/shard_map/whqk,wqhe->wkhe/dot_general | solution.py:161
  175.8 3.9 convert_reduce_fusion
  193.5 3.6 convolution_convert_fusion.2
  197.1 3.0 copy.96
  200.1 3.4 copy.100
  205.2 6.1 %convolution_convert_fusion = bf16[2048,512]{1,0:T(8,128)(2,1)} fusion(bf16[800,2048]{1,0:T(8,128)(2,1)} %get-tuple-element.51, f32[800]{0:T(1024)S(1)} %copy-done.31, bf16[3200,512]{1,0:T(8,128)(2,1)} %param.18, s32[]{:T(128)S(6)} %select_n.14), kind=kOutput, calls=%fused_computation.40 | convolution fusion | flops 1679998976 | bytes 6196356 | tf_op jit(solution)/shard_map/rf,rd->fd/dot_general | solution.py:133
  211.4 5.9 convolution_convert_fusion.1
  218.5 5.4 multiply_convert_fusion.3
  224.2 4.3 fusion.35
  231.3 6.7 %reduce-scatter.16.cloned.1.call-done = bf16[128,1536]{1,0:T(8,128)(2,1)} async-done(((bf16[512,1536]{1,0:T(8,128)(2,1)}), bf16[128,1536]{1,0:T(8,128)(2,1)}) %reduce-scatter.16.cloned.1.call-update) | async-done | bytes 393232
  240.7 20.6 %reduce-scatter.10.cloned.1.call-done = bf16[128,512]{1,0:T(8,128)(2,1)} async-done(((bf16[512,512]{1,0:T(8,128)(2,1)}), bf16[128,512]{1,0:T(8,128)(2,1)}) %reduce-scatter.10.cloned.1.call-update) | async-done | bytes 131088 | tf_op jit(solution)/shard_map/reduce_scatter | solution.py:208
  261.3 44.3 %reduce-scatter.14.cloned.1.call-done = bf16[512,512]{1,0:T(8,128)(2,1)} async-done(((bf16[2048,512]{1,0:T(8,128)(2,1)}), bf16[512,512]{1,0:T(8,128)(2,1)}) %reduce-scatter.14.cloned.1.call-update) | async-done | bytes 524304 | tf_op jit(solution)/shard_map/reduce_scatter | solution.py:208
  305.6 45.6 %reduce-scatter.12.cloned.1.call-done = bf16[512,512]{1,0:T(8,128)(2,1)} async-done(((bf16[512,2048]{1,0:T(8,128)(2,1)}), bf16[512,512]{1,0:T(8,128)(2,1)}) %reduce-scatter.12.cloned.1.call-update) | async-done | bytes 524304 | tf_op jit(solution)/shard_map/reduce_scatter | solution.py:208
  353.8 39.7 %all-reduce.2 = (bf16[512]{0:T(512)(128)(2,1)S(1)}, bf16[512]{0:T(512)(128)(2,1)S(1)}, bf16[512]{0:T(512)(128)(2,1)S(1)}, bf16[512]{0:T(512)(128)(2,1)S(1)}, bf1...) all-reduce(bf16[512]{0:T(512)(128)(2,1)S(1)} %get-tuple-element.15,, ...), channel_id=1, replica_groups=mesh['dp'=8,'mp'=4] {'mp','dp'}, use_global_device_ids=true, to_apply=%region_12.13 | all-reduce | flops 3072 | bytes 12288 | tf_op jit(solution)/shard_map/psum | solution.py:207
  397.0 5.1 fusion.44
  402.1 18.4 %all-reduce.5 = (bf16[361,16]{0,1:T(8,128)(2,1)S(1)}, bf16[2048]{0:T(1024)(128)(2,1)S(1)}) all-reduce(bf16[361,16]{0,1:T(8,128)(2,1)S(1)} %fusion.44, bf16[2048]{0:T(1024)(128)(2,1)S(1)} %copy-done.36), channel_id=4, replica_groups=mesh['dp'=8,'mp'=4] {'mp'}, use_global_device_ids=true, to_apply=%region_22.23.clone | all-reduce | flops 7824 | bytes 31296
  421.4 12.8 %all-reduce.3 = (bf16[2,128]{1,0:T(2,128)(2,1)S(1)}, bf16[361,4]{0,1:T(4,128)(2,1)S(1)}, bf16[512]{0:T(512)(128)(2,1)S(1)}) all-reduce(bf16[2,128]{1,0:T(2,128)(2,1)S(1)} %copy.99, bf16[361,4]{0,1:T(4,128)(2,1)S(1)} %constant_dynamic-slice_fusion, bf16[512]{0:T(512)(128)(2,1)S(1)} %dynamic-slice.3), channel_id=1, replica_groups=mesh['dp'=8,'mp'=4] {'dp'}, use_global_device_ids=true, to_apply=%region_20.21 | all-reduce | flops 2212 | bytes 8848 | tf_op jit(solution)/shard_map/psum | solution.py:209
  436.0 3.1 all-gather.14.cloned.1.call-done
  439.1 66.4 %all-gather.16.cloned.1.call-done = bf16[3200,512]{1,0:T(8,128)(2,1)} async-done(((bf16[800,512]{1,0:T(8,128)(2,1)}), bf16[3200,512]{1,0:T(8,128)(2,1)}) %all-gather.16.cloned.1.call-update) | async-done | bytes 3276816 | tf_op jit(solution)/shard_map/all_gather | solution.py:202
  505.6 62.6 %all-reduce.8.cloned.1.call-done = (bf16[512,3,128]{2,0,1:T(8,128)(2,1)}, bf16[128,512]{1,0:T(8,128)(2,1)}, bf16[512,512]{1,0:T(8,128)(2,1)}, bf16[512,512]{1,0:T(8,128)(2,1)}) async-done(((bf16[512,3,128]{2,0,1:T(8,128)(2,1)}, bf16[128,512]{1,0:T(8,128)(2,1)}, bf16[512,512]{1,0:T(8,128)(2,1)}, bf16[512,512]{1,0:T(8,128)(2,1)}), (bf16[512,3,128]{2,0,1:T(8,128)(2,1)}, bf16[128,512]{1,0:T(8,128)(2,1)}, ...) | async-done | bytes 1572880 | tf_op jit(solution)/shard_map/psum | solution.py:209
  (205 shorter events, 89.1 us)
Async XLA Ops:
  7.2 50.7 %copy-start.22 = (s32[100,100]{1,0:T(8,128)S(1)}, s32[100,100]{1,0:T(8,128)}, u32[]{:S(2)}) copy-start(s32[100,100]{1,0:T(8,128)} %param.20) | copy-start | bytes 120004
  7.2 50.8 %copy-start.21 = (bf16[128,512]{1,0:T(8,128)(2,1)S(1)}, bf16[128,512]{1,0:T(8,128)(2,1)}, u32[]{:S(2)}) copy-start(bf16[128,512]{1,0:T(8,128)(2,1)} %param.26) | copy-start | bytes 393220
  7.2 72.8 %all-gather.8.cloned.1.call-start = ((), (), s32[]{:S(2)}) async-start(), calls=%async_computation.5 | async-start | bytes 1966080 | tf_op jit(solution)/shard_map/all_gather | solution.py:71
  7.9 105.9 %all-gather.10.cloned.1.call-start = ((), (), s32[]{:S(2)}) async-start(), calls=%async_computation.6 | async-start | bytes 2621440 | tf_op jit(solution)/shard_map/all_gather | solution.py:75
  8.7 137.1 %all-gather.12.cloned.1.call-start = ((), (), s32[]{:S(2)}) async-start(), calls=%async_computation.7 | async-start | bytes 2621440 | tf_op jit(solution)/shard_map/all_gather | solution.py:77
  9.4 228.5 %reduce-scatter.16.cloned.1.call-start = ((), (), s32[]{:S(2)}) async-start(), calls=%async_computation.13 | async-start | bytes 1966080
  10.8 69.2 %copy-start.32 = (f32[512]{0:T(512)}, f32[512]{0:T(512)S(1)}, u32[]{:S(2)}) copy-start(f32[512]{0:T(512)S(1)} %convert_element_type.202) | copy-start | bytes 6148
  12.2 67.9 %copy-start.37 = (f32[512]{0:T(512)}, f32[512]{0:T(512)S(1)}, u32[]{:S(2)}) copy-start(f32[512]{0:T(512)S(1)} %convert_element_type.203) | copy-start | bytes 6148
  27.0 129.0 %copy-start.30 = (f32[800]{0:T(1024)}, f32[800]{0:T(1024)S(1)}, u32[]{:S(2)}) copy-start(f32[800]{0:T(1024)S(1)} %fusion.61) | copy-start | bytes 9604
  28.4 51.6 %copy-start.25 = (f32[800]{0:T(1024)}, f32[800]{0:T(1024)S(1)}, u32[]{:S(2)}) copy-start(f32[800]{0:T(1024)S(1)} %broadcast_multiply_fusion.5) | copy-start | bytes 9604
  30.0 50.1 %copy-start.27 = (f32[800]{0:T(1024)}, f32[800]{0:T(1024)S(1)}, u32[]{:S(2)}) copy-start(f32[800]{0:T(1024)S(1)} %add_rsqrt_fusion.1) | copy-start | bytes 9604
  58.0 18.9 %copy-start.23 = (s32[10000]{0:T(1024)}, s32[10000]{0:T(1024)S(1)}, u32[]{:S(2)}) copy-start(s32[10000]{0:T(1024)S(1)} %eq.15) | copy-start | bytes 120004
  87.4 14.3 %copy-start.10 = (bf16[8,100,16,32]{1,0,3,2:T(8,128)(2,1)}, bf16[8,100,16,32]{1,0,3,2:T(8,128)(2,1)S(1)}, u32[]{:S(2)}) copy-start(bf16[8,100,16,32]{1,0,3,2:T(8,128)(2,1)S(1)} %convert_element_type.208) | copy-start | bytes 2457604
  111.1 22.1 %copy-start.13 = (bf16[800,512]{0,1:T(8,128)(2,1)}, bf16[800,512]{0,1:T(8,128)(2,1)S(1)}, u32[]{:S(2)}) copy-start(bf16[800,512]{0,1:T(8,128)(2,1)S(1)} %convert_element_type.214) | copy-start | bytes 2457604
  113.5 42.6 %copy-start.3 = (f32[800,512]{1,0:T(8,128)}, f32[800,512]{1,0:T(8,128)S(1)}, u32[]{:S(2)}) copy-start(f32[800,512]{1,0:T(8,128)S(1)} %get-tuple-element.50) | copy-start | bytes 4915204
  159.8 13.0 %slice-start = ((s8[6815744]{0:T(1024)(128)(4,1)}), s8[2621440]{0:T(1024)(128)(4,1)S(1)}, s32[]{:S(2)}) async-start(s8[6815744]{0:T(1024)(128)(4,1)} %bitcast.84), calls=%async_computation.16 | async-start | bytes 5242880
  203.6 57.7 %reduce-scatter.10.cloned.1.call-start = ((), (), s32[]{:S(2)}) async-start(), calls=%async_computation.10 | async-start | bytes 655360 | tf_op jit(solution)/shard_map/reduce_scatter | solution.py:208
  205.2 100.4 %reduce-scatter.14.cloned.1.call-start = ((), (), s32[]{:S(2)}) async-start(), calls=%async_computation.12 | async-start | bytes 2621440 | tf_op jit(solution)/shard_map/reduce_scatter | solution.py:208
  211.3 139.8 %reduce-scatter.12.cloned.1.call-start = ((), (), s32[]{:S(2)}) async-start(), calls=%async_computation.11 | async-start | bytes 2621440 | tf_op jit(solution)/shard_map/reduce_scatter | solution.py:208
  217.3 203.3 %reduce-scatter.18.cloned.1.call-start = ((), (), s32[]{:S(2)}) async-start(), calls=%async_computation.14 | async-start | bytes 163840
  218.4 220.7 %all-gather.14.cloned.1.call-start = ((), (), s32[]{:S(2)}) async-start(), calls=%async_computation.8 | async-start | bytes 4096000 | tf_op jit(solution)/shard_map/all_gather | solution.py:201
  223.9 281.7 %all-gather.16.cloned.1.call-start = ((), (), s32[]{:S(2)}) async-start(), calls=%async_computation.9 | async-start | bytes 4096000 | tf_op jit(solution)/shard_map/all_gather | solution.py:202
  231.1 120.1 %copy-start.43 = (u32[32]{0:T(128)S(1)}, u32[32]{0:T(128)}, u32[]{:S(2)}) copy-start(u32[32]{0:T(128)} %constant.111) | copy-start | bytes 388
  231.1 122.0 %copy-start.15 = (f32[16,100,100]{1,2,0:T(8,128)S(1)}, f32[16,100,100]{1,2,0:T(8,128)}, u32[]{:S(2)}) copy-start(f32[16,100,100]{1,2,0:T(8,128)} %get-tuple-element.40) | copy-start | bytes 1920004
  231.1 122.6 %copy-start.34 = (bf16[512]{0:T(512)(128)(2,1)S(1)}, bf16[512]{0:T(512)(128)(2,1)}, u32[]{:S(2)}) copy-start(bf16[512]{0:T(512)(128)(2,1)} %get-tuple-element.42) | copy-start | bytes 3076
  231.2 122.6 %copy-start.35 = (bf16[512]{0:T(512)(128)(2,1)S(1)}, bf16[512]{0:T(512)(128)(2,1)}, u32[]{:S(2)}) copy-start(bf16[512]{0:T(512)(128)(2,1)} %get-tuple-element.46) | copy-start | bytes 3076
  231.2 122.6 %copy-start.40 = (bf16[512]{0:T(512)(128)(2,1)S(1)}, bf16[512]{0:T(512)(128)(2,1)}, u32[]{:S(2)}) copy-start(bf16[512]{0:T(512)(128)(2,1)} %get-tuple-element.17) | copy-start | bytes 3076
  231.2 122.6 %copy-start.41 = (bf16[512]{0:T(512)(128)(2,1)S(1)}, bf16[512]{0:T(512)(128)(2,1)}, u32[]{:S(2)}) copy-start(bf16[512]{0:T(512)(128)(2,1)} %get-tuple-element.21) | copy-start | bytes 3076
  231.2 165.8 %copy-start.24 = (s32[10000]{0:T(1024)S(1)}, s32[10000]{0:T(1024)}, u32[]{:S(2)}) copy-start(s32[10000]{0:T(1024)} %copy-done.23) | copy-start | bytes 120004
  231.2 336.9 %all-reduce.8.cloned.1.call-start = ((), (), s32[]{:S(2)}) async-start(), calls=%async_computation.15 | async-start | bytes 3145728 | tf_op jit(solution)/shard_map/psum | solution.py:209
  353.4 48.7 %copy-start.36 = (bf16[2048]{0:T(1024)(128)(2,1)S(1)}, bf16[2048]{0:T(1024)(128)(2,1)}, u32[]{:S(2)}) copy-start(bf16[2048]{0:T(1024)(128)(2,1)} %get-tuple-element.61) | copy-start | bytes 12292
  439.1 136.9 %copy-start.17 = (bf16[3200,512]{1,0:T(8,128)(2,1)S(1)}, bf16[3200,512]{1,0:T(8,128)(2,1)}, u32[]{:S(2)}) copy-start(bf16[3200,512]{1,0:T(8,128)(2,1)} %all-gather.14.cloned.1.call-done) | copy-start | bytes 9830404
  (25 other events, 95.4 us)
Sparse Core Ops, SparseCore 0:
  9.6 40.6 all-gather.7
  51.9 47.5 all-gather.9
  101.1 44.6 all-gather.11
  203.7 34.2 reduce-scatter.15
  240.6 20.6 reduce-scatter.9
  263.4 42.0 reduce-scatter.13
  308.0 43.1 reduce-scatter.11
  354.0 18.4 reduce-scatter.17
  374.7 64.3 all-gather.13
  441.2 64.3 all-gather.15
  510.1 57.9 all-reduce.7

commit v2 on v0

v2 whole, which is shorter than its diff:
```python
import functools
import math
import jax
import jax.numpy as jnp
from jax import lax
from jax.experimental import pallas as pl
from jax.experimental.pallas import tpu as pltpu
from jax.sharding import PartitionSpec as P

AREA = 100
PAD = 104
HEAD = 32
LANES = 128
PACK = LANES // HEAD
BATCH = 4
CHUNK = BATCH * AREA
ROWS = BATCH * PAD
EPSILON = 1e-05
DENSITY = 0.3989422804014327
LOG2E = 1.4426950408889634
F32 = jnp.float32
BF16 = jnp.bfloat16
MESH = pl.DeviceIdType.MESH
VMEM_LIMIT = 60 * 2**20


def dot(a, b):
    return jnp.dot(a, b, preferred_element_type=F32)


def dot_nt(a, b):
    return lax.dot_general(a, b, (((1,), (1,)), ((), ())), preferred_element_type=F32)


def dot_tn(a, b):
    return lax.dot_general(a, b, (((0,), (0,)), ((), ())), preferred_element_type=F32)


def normalize(values):
    centered = values - jnp.mean(values, axis=-1, keepdims=True)
    inv = lax.rsqrt(jnp.mean(centered * centered, axis=-1, keepdims=True) + EPSILON)
    return centered * inv, inv


def norm_back(grad, hat, inv):
    return inv * (
        grad
        - jnp.mean(grad, axis=-1, keepdims=True)
        - hat * jnp.mean(grad * hat, axis=-1, keepdims=True)
    )


def normal_cdf(hidden):
    z = jnp.abs(hidden) * 0.7071067811865476
    t = 1.0 / (1.0 + 0.3275911 * z)
    poly = t * (
        0.127414796 + t * (-0.142248368 + t * (0.7107068705 + t * (-0.7265760135 + t * 0.5307027145)))
    )
    bell = jnp.exp2(hidden * hidden * (-0.5 * LOG2E))
    tail = poly * bell
    return jnp.where(hidden > 0.0, 1.0 - tail, tail), bell


def head_of(shape, axis):
    return lax.broadcasted_iota(jnp.int32, shape, axis) // HEAD


def pad_rows(v):
    return jnp.concatenate([v, jnp.zeros((LANES - PAD, v.shape[1]), v.dtype)], axis=0)


def spread_rows(v):
    head = head_of((LANES, LANES), 1)
    full = pad_rows(v)
    return jnp.concatenate([jnp.where(head == h, full, 0.0) for h in range(PACK)], axis=0).astype(BF16)


def spread_columns(v):
    head = head_of((LANES, LANES), 0)
    turned = pad_rows(v).T
    return jnp.concatenate([jnp.where(head == h, turned, 0.0) for h in range(PACK)], axis=1).astype(BF16)


def diagonal(full):
    head = head_of((LANES, LANES), 0)
    out = full[:, 0:LANES]
    for h in range(1, PACK):
        out = jnp.where(head == h, full[:, h * LANES : (h + 1) * LANES], out)
    return out


def span(w, size=PAD):
    return pl.ds(pl.multiple_of(w * PAD, 8), size)


def load_rows(source, wide, padded):
    wide[...] = source.astype(F32)
    for w in range(BATCH):
        padded[w * PAD : w * PAD + AREA, :] = wide[w * AREA : (w + 1) * AREA, :]


def store_rows(padded, wide, target, scales=None):
    for w in range(BATCH):
        rows = padded[w * PAD : w * PAD + AREA, :]
        wide[w * AREA : (w + 1) * AREA, :] = rows if scales is None else rows * scales[w]
    target[...] = wide[...].astype(BF16)


class Sizes:
    def __init__(self, shards, loc, units):
        self.shards, self.loc, self.units = shards, loc, units
        self.width = shards * loc
        self.groups = self.width // LANES
        self.columns = 4 * loc + 2 * units

    def attention_part(self, weights, c):
        at = slice(c * self.loc, (c + 1) * self.loc)
        return jnp.concatenate([weights[z, at, :] for z in range(self.shards)], axis=0)

    def expand_part(self, weights, i):
        return weights[i, pl.ds(4 * self.loc, self.units), :]

    def shrink_part(self, weights, i):
        return weights[i, pl.ds(4 * self.loc + self.units, self.units), :]

    def add_attention(self, dw, c, value):
        for z in range(self.shards):
            at = slice(c * self.loc, (c + 1) * self.loc)
            dw[z, :, at] += value[:, z * self.loc : (z + 1) * self.loc]


def attention(sizes, bias, vecs, wide_bias, weights, xs, work, low, qkv, mixed, middle, keep):
    width, groups = sizes.width, sizes.groups
    scale = HEAD ** (-0.5) * LOG2E
    for w in range(BATCH):
        hat, _ = normalize(xs[span(w), :])
        work[span(w), :] = hat * vecs[0:1, :] + vecs[1:2, :]
    low[...] = work[...].astype(BF16)
    for c in range(3):
        at = slice(c * width, (c + 1) * width)
        qkv[:, at] = dot_nt(low[...], sizes.attention_part(weights, c)) + wide_bias[:, at]

    def attend(w, _):
        row = span(w)
        for g in range(groups):
            col = g * LANES
            q = qkv[row, pl.ds(col, LANES)].astype(BF16)
            k = qkv[row, pl.ds(width + col, LANES)]
            v = qkv[row, pl.ds(2 * width + col, LANES)]
            scores = dot(q, spread_columns(k))
            parts = []
            for h in range(PACK):
                s = scores[:, h * LANES : (h + 1) * LANES] * scale + bias[g * PACK + h]
                e = jnp.exp2(s - jnp.max(s, axis=-1, keepdims=True))
                parts.append(e * (1.0 / jnp.sum(e, axis=-1, keepdims=True)))
            probs = jnp.concatenate(parts, axis=1).astype(BF16)
            if keep is not None:
                keep[w * groups + g] = probs
            mixed[row, pl.ds(col, LANES)] = dot(probs, spread_rows(v))
        return 0

    lax.fori_loop(0, BATCH, attend, 0)
    middle[...] = xs[...] + dot(mixed[...].astype(BF16), sizes.attention_part(weights, 3)) + vecs[2:3, :]


def second_norm(vecs, middle, work, low):
    for w in range(BATCH):
        hat, _ = normalize(middle[span(w), :])
        work[span(w), :] = hat * vecs[3:4, :] + vecs[4:5, :]
    low[...] = work[...].astype(BF16)


def feed(sizes, hid_bias, vecs, weights, middle, low, acc):
    acc[...] = middle[...] + vecs[5:6, :]

    def block(i, _):
        hidden = dot_nt(low[...], sizes.expand_part(weights, i)) + hid_bias[i]
        cdf, _ = normal_cdf(hidden)
        acc[...] += dot((hidden * cdf).astype(BF16), sizes.shrink_part(weights, i))
        return 0

    lax.fori_loop(0, sizes.shards, block, 0, unroll=4)


def column_sum(v):
    return jnp.sum(v, axis=0, keepdims=True)


def feed_both(sizes, hid_bias, vecs, weights, middle, low, glow, acc, back, dw, unit_sums):
    base, units = 4 * sizes.loc, sizes.units
    acc[...] = middle[...] + vecs[5:6, :]
    back[...] = jnp.zeros_like(back)

    def block(i, _):
        w_in, w_out = sizes.expand_part(weights, i), sizes.shrink_part(weights, i)
        hidden = dot_nt(low[...], w_in) + hid_bias[i]
        cdf, bell = normal_cdf(hidden)
        active = (hidden * cdf).astype(BF16)
        grad = (dot_nt(glow[...], w_out) * (cdf + hidden * bell * DENSITY))
        unit_sums[i] += column_sum(grad)
        grad = grad.astype(BF16)
        acc[...] += dot(active, w_out)
        back[...] += dot(grad, w_in)
        dw[i, :, base : base + units] += dot_tn(low[...], grad)
        dw[i, :, base + units : base + 2 * units] += dot_tn(glow[...], active)
        return 0

    lax.fori_loop(0, sizes.shards, block, 0, unroll=2)


def backward(sizes, vecs, weights, xs, work, low, qkv, mixed, middle, glow, back, gmid, gmix, dqkv, keep, dw, dbias, sums):
    width, groups = sizes.width, sizes.groups
    scale = HEAD ** (-0.5)
    for w in range(BATCH):
        hat, inv = normalize(middle[span(w), :])
        grad = back[span(w), :]
        sums[3:4, :] += column_sum(grad * hat)
        sums[4:5, :] += column_sum(grad)
        gmid[span(w), :] += norm_back(grad * vecs[3:4, :], hat, inv)
    branch = gmid[...].astype(BF16)
    sums[5:6, :] += column_sum(gmid[...])
    sizes.add_attention(dw, 3, dot_tn(branch, mixed[...].astype(BF16)))
    gmix[...] = dot_nt(branch, sizes.attention_part(weights, 3))

    def attend(w, _):
        row = span(w)
        for g in range(groups):
            col = g * LANES
            q = qkv[row, pl.ds(col, LANES)]
            k = qkv[row, pl.ds(width + col, LANES)]
            v = qkv[row, pl.ds(2 * width + col, LANES)]
            grad = gmix[row, pl.ds(col, LANES)]
            probs = keep[w * groups + g]
            wide_grad = dot(grad.astype(BF16), spread_columns(v))
            parts = []
            for h in range(PACK):
                p = probs[:, h * LANES : (h + 1) * LANES].astype(F32)
                t = wide_grad[:, h * LANES : (h + 1) * LANES]
                s = p * (t - jnp.sum(p * t, axis=-1, keepdims=True))
                dbias[g * PACK + h] += s
                parts.append(s)
            score = jnp.concatenate(parts, axis=1).astype(BF16)
            dqkv[row, pl.ds(col, LANES)] = dot(score, spread_rows(k)) * scale
            turned = pad_rows(q).T[:, :PAD].astype(BF16)
            dqkv[row, pl.ds(width + col, LANES)] = diagonal(dot(turned, score)).T[:PAD] * scale
            turned = pad_rows(grad).T[:, :PAD].astype(BF16)
            dqkv[row, pl.ds(2 * width + col, LANES)] = diagonal(dot(turned, probs)).T[:PAD]
        return 0

    lax.fori_loop(0, BATCH, attend, 0)
    for w in range(BATCH):
        hat, _ = normalize(xs[span(w), :])
        work[span(w), :] = hat * vecs[0:1, :] + vecs[1:2, :]
    low[...] = work[...].astype(BF16)
    back[...] = jnp.zeros_like(back)
    for c in range(3):
        at = slice(c * width, (c + 1) * width)
        grad = dqkv[:, at]
        if c != 1:
            sums[c // 2 : c // 2 + 1, :] += column_sum(grad)
        grad = grad.astype(BF16)
        back[...] += dot(grad, sizes.attention_part(weights, c))
        sizes.add_attention(dw, c, dot_tn(low[...], grad))
    for w in range(BATCH):
        hat, inv = normalize(xs[span(w), :])
        grad = back[span(w), :]
        sums[6:7, :] += column_sum(grad * hat)
        sums[7:8, :] += column_sum(grad)
        gmid[span(w), :] += norm_back(grad * vecs[0:1, :], hat, inv)


def live_scales(first, live):
    return [jnp.where(first + w < live[0], 1.0, 0.0).astype(F32) for w in range(BATCH)]


def forward_kernel(sizes, order, live, tok_ref, held, bias, vecs, wide_bias, hid_bias, weights, out_ref,
                   wide, xs, work, low, qkv, mixed, middle):
    @pl.when(pl.program_id(0) == 0)
    def _():
        xs[...] = jnp.zeros_like(xs)

    load_rows(tok_ref[...], wide, xs)
    attention(sizes, bias, vecs, wide_bias, weights, xs, work, low, qkv, mixed, middle, None)
    second_norm(vecs, middle, work, low)
    feed(sizes, hid_bias, vecs, weights, middle, low, work)
    store_rows(work, wide, out_ref, live_scales(order[pl.program_id(0)] * BATCH, live))


def own_kernel(sizes, order, live, tok_ref, cot_ref, bias, vecs, wide_bias, hid_bias, weights,
               out_ref, gtok_ref, dw_ref, dbias, sums, unit_sums,
               wide, xs, work, low, qkv, mixed, middle, glow, back, gmid, gmix, dqkv, keep, dw):
    @pl.when(pl.program_id(0) == 0)
    def _():
        xs[...] = jnp.zeros_like(xs)
        dw[...] = jnp.zeros_like(dw)
        dbias[...] = jnp.zeros_like(dbias)
        sums[...] = jnp.zeros_like(sums)
        unit_sums[...] = jnp.zeros_like(unit_sums)

    scales = live_scales(order[pl.program_id(0)] * BATCH, live)
    load_rows(tok_ref[...], wide, xs)
    attention(sizes, bias, vecs, wide_bias, weights, xs, work, low, qkv, mixed, middle, keep)
    second_norm(vecs, middle, work, low)
    wide[...] = cot_ref[...].astype(F32)
    for w in range(BATCH):
        gmid[w * PAD : w * PAD + AREA, :] = wide[w * AREA : (w + 1) * AREA, :] * scales[w]
        gmid[w * PAD + AREA : (w + 1) * PAD, :] = jnp.zeros((PAD - AREA, gmid.shape[1]), F32)
    sums[2:3, :] += column_sum(gmid[...])
    glow[...] = gmid[...].astype(BF16)
    feed_both(sizes, hid_bias, vecs, weights, middle, low, glow, work, back, dw, unit_sums)
    store_rows(work, wide, out_ref, scales)
    backward(sizes, vecs, weights, xs, work, low, qkv, mixed, middle, glow, back, gmid, gmix, dqkv, keep, dw, dbias, sums)
    store_rows(gmid, wide, gtok_ref)

    @pl.when(pl.program_id(0) == pl.num_programs(0) - 1)
    def _():
        def cast(z, _):
            dw_ref[z] = dw[z].astype(BF16)
            return 0

        lax.fori_loop(0, sizes.shards, cast, 0)


def whole_block(a):
    return pl.BlockSpec(a.shape, lambda *_: (0,) * len(a.shape), pipeline_mode=pl.Buffered(1))


def forward_scratch(sizes, d):
    return [
        pltpu.VMEM((CHUNK, d), F32),
        pltpu.VMEM((ROWS, d), F32),
        pltpu.VMEM((ROWS, d), F32),
        pltpu.VMEM((ROWS, d), BF16),
        pltpu.VMEM((ROWS, 3 * sizes.width), F32),
        pltpu.VMEM((ROWS, sizes.width), F32),
        pltpu.VMEM((ROWS, d), F32),
    ]


def run_forward(sizes, order, live, tokens, held, *params):
    d = tokens.shape[1]
    block = pl.BlockSpec((CHUNK, d), lambda i, order, live: (order[i], 0))
    return pl.pallas_call(
        functools.partial(forward_kernel, sizes),
        out_shape=jax.ShapeDtypeStruct(tokens.shape, BF16),
        grid_spec=pltpu.PrefetchScalarGridSpec(
            num_scalar_prefetch=2,
            grid=(order.shape[0],),
            in_specs=[block, pl.BlockSpec(memory_space=pl.ANY)] + [whole_block(a) for a in params],
            out_specs=block,
            scratch_shapes=forward_scratch(sizes, d),
        ),
        input_output_aliases={3: 0},
        compiler_params=pltpu.CompilerParams(vmem_limit_bytes=VMEM_LIMIT),
    )(order, live, tokens, held, *params)


def run_own(sizes, order, live, tokens, cotangent, *params):
    d = tokens.shape[1]
    chunks = order.shape[0]
    block = pl.BlockSpec((CHUNK, d), lambda i, order, live: (order[i], 0))
    outs = (
        jax.ShapeDtypeStruct(tokens.shape, BF16),
        jax.ShapeDtypeStruct((chunks * CHUNK, d), BF16),
        jax.ShapeDtypeStruct((sizes.shards, d, sizes.columns), BF16),
        jax.ShapeDtypeStruct(params[0].shape, F32),
        jax.ShapeDtypeStruct((8, d), F32),
        jax.ShapeDtypeStruct((sizes.shards, 1, sizes.units), F32),
    )
    return pl.pallas_call(
        functools.partial(own_kernel, sizes),
        out_shape=outs,
        grid_spec=pltpu.PrefetchScalarGridSpec(
            num_scalar_prefetch=2,
            grid=(chunks,),
            in_specs=[block, block] + [whole_block(a) for a in params],
            out_specs=[block, pl.BlockSpec((CHUNK, d), lambda i, *_: (i, 0))] + [whole_block(o) for o in outs[2:]],
            scratch_shapes=forward_scratch(sizes, d)
            + [
                pltpu.VMEM((ROWS, d), BF16),
                pltpu.VMEM((ROWS, d), F32),
                pltpu.VMEM((ROWS, d), F32),
                pltpu.VMEM((ROWS, sizes.width), F32),
                pltpu.VMEM((ROWS, 3 * sizes.width), F32),
                pltpu.VMEM((BATCH * sizes.groups, PAD, PACK * LANES), BF16),
                pltpu.VMEM((sizes.shards, d, sizes.columns), F32),
            ],
        ),
        compiler_params=pltpu.CompilerParams(vmem_limit_bytes=VMEM_LIMIT),
    )(order, live, tokens, cotangent, *params)


class Place:
    def __init__(self, mesh_shape):
        self.shards, self.n_dp = mesh_shape["mp"], mesh_shape["dp"]
        self.chips = self.n_dp // 2
        self.bits = int(math.log2(self.chips))
        self.dp, self.z = lax.axis_index("dp"), lax.axis_index("mp")
        self.core, self.chip = lax.rem(self.dp, 2), lax.div(self.dp, 2)

    def mate(self):
        return (self.dp + 1 - 2 * self.core, self.z)

    def flip(self, m):
        chip = self.chip
        for b in range(self.bits):
            if m >> b & 1:
                chip = chip + (1 << b) * (1 - 2 * lax.rem(lax.div(self.chip, 1 << b), 2))
        return chip

    def across(self, m):
        return (2 * self.flip(m) + self.core, self.z)

    def bit(self, b):
        return lax.rem(lax.div(self.chip, 1 << b), 2)

    def along(self, k):
        return (self.dp, lax.rem(self.z + k, self.shards))

    def greet(self, targets):
        barrier = pltpu.get_barrier_semaphore()
        for target in targets:
            pl.semaphore_signal(barrier, inc=1, device_id=target, device_id_type=MESH)
        pl.semaphore_wait(barrier, len(targets))

    def everyone(self):
        return (
            [self.mate()]
            + [self.across(m) for m in range(1, self.chips)]
            + [self.along(k) for k in range(1, self.shards)]
        )


def remote(source, target, sent, received, device):
    return pltpu.make_async_remote_copy(source, target, sent, received, device_id=device, device_id_type=MESH)


def gather_kernel(mesh_shape, shard, small, out, out_small, own_sem, z_sem, s_sem, p_sem, m_sem):
    here = Place(mesh_shape)
    rows = shard.shape[0] // here.n_dp

    def piece(dp):
        return pl.ds(pl.multiple_of(dp * rows, 16), rows)

    here.greet(here.everyone())
    keep = [
        pltpu.make_async_copy(shard, out.at[here.z], own_sem.at[0]),
        pltpu.make_async_copy(small, out_small.at[here.z], own_sem.at[1]),
    ]
    for copy in keep:
        copy.start()
    sends = []
    for k in range(1, here.shards):
        copy = remote(small, out_small.at[here.z], s_sem.at[0, k], s_sem.at[1, k], here.along(k))
        copy.start()
        sends.append(copy)
        copy = remote(
            shard.at[piece(here.dp)], out.at[here.z, piece(here.dp)], z_sem.at[0, k], z_sem.at[1, k], here.along(k)
        )
        copy.start()
        sends.append(copy)

    def from_shard(k):
        return lax.rem(here.z - k + here.shards, here.shards)

    def arrival(slot, k):
        block = out.at[from_shard(k), piece(here.dp)]
        return remote(block, block, slot.at[0], slot.at[1], here.mate())

    def spread(k):
        block = out.at[from_shard(k), piece(here.dp)]
        remote(block, block, z_sem.at[0, k], z_sem.at[1, k], here.along(k)).wait_recv()
        for m in range(1, here.chips):
            copy = remote(block, block, p_sem.at[0, k, m], p_sem.at[1, k, m], here.across(m))
            copy.start()
            sends.append(copy)
        copy = remote(block, block, m_sem.at[0, k, 0], m_sem.at[1, k, 0], here.mate())
        copy.start()
        sends.append(copy)

    def relay(k):
        for m in range(1, here.chips):
            block = out.at[from_shard(k), piece(2 * here.flip(m) + here.core)]
            remote(block, block, p_sem.at[0, k, m], p_sem.at[1, k, m], here.across(m)).wait_recv()
            copy = remote(block, block, m_sem.at[0, k, m], m_sem.at[1, k, m], here.mate())
            copy.start()
            sends.append(copy)

    order = sorted(range(1, here.shards), key=lambda k: min(k, here.shards - k))
    for k in order:
        spread(k)
    for k in order:
        relay(k)
    for k in order:
        for m in range(here.chips):
            block = out.at[from_shard(k), piece(2 * here.flip(m) + 1 - here.core)]
            remote(block, block, m_sem.at[0, k, m], m_sem.at[1, k, m], here.mate()).wait_recv()
        block = out_small.at[from_shard(k)]
        remote(block, block, s_sem.at[0, k], s_sem.at[1, k], here.along(k)).wait_recv()
    for copy in sends:
        copy.wait_send()
    for copy in keep:
        copy.wait()


def run_gather(mesh_shape, shard, small):
    shards, chips = mesh_shape["mp"], mesh_shape["dp"] // 2
    anywhere = pl.BlockSpec(memory_space=pl.ANY)
    dma = pltpu.SemaphoreType.DMA
    return pl.pallas_call(
        functools.partial(gather_kernel, mesh_shape),
        out_shape=(
            jax.ShapeDtypeStruct((shards, *shard.shape), shard.dtype),
            jax.ShapeDtypeStruct((shards, *small.shape), small.dtype),
        ),
        in_specs=[anywhere] * 2,
        out_specs=(anywhere, anywhere),
        scratch_shapes=[dma((2,)), dma((2, shards)), dma((2, shards)), dma((2, shards, chips)), dma((2, shards, chips))],
        compiler_params=pltpu.CompilerParams(collective_id=0, has_side_effects=True, vmem_limit_bytes=VMEM_LIMIT),
    )(shard, small)


def reduce_kernel(mesh_shape, gtok, dw, small, gout, final, small_out,
                  acc, half, part_a, part_b, last_a, last_b, sums, sums_in,
                  own_sem, line_sem, h_sem, q_sem, l_sem, f_sem, g_sem, t_sem):
    here = Place(mesh_shape)
    shards, chips, bits = here.shards, here.chips, here.bits
    d, columns = dw.shape[1], dw.shape[2]
    split = columns // 2
    side_a, side_b = pl.ds(0, split), pl.ds(split, split)
    sends = []

    def start(copy, when=None):
        sends.append((copy, when))
        if when is None:
            copy.start()
        else:
            pl.when(when)(copy.start)

    here.greet(here.everyone())

    block_rows = gtok.shape[0]

    def block(z):
        return gout.at[pl.ds(pl.multiple_of(z * block_rows, 16), block_rows)]

    own = pltpu.make_async_copy(gtok, block(here.z), own_sem.at[0])
    own.start()
    up, down = (here.dp, jnp.minimum(here.z + 1, shards - 1)), (here.dp, jnp.maximum(here.z - 1, 0))

    def line(step):
        for way, (target, sign) in enumerate(((up, 1), (down, -1))):
            held = here.z - sign * step
            inside = (held >= 0) & (held < shards)
            nxt = here.z + sign
            has_next = (nxt >= 0) & (nxt < shards)
            safe = jnp.clip(held, 0, shards - 1)
            if step > 0:
                arrived = remote(block(safe), block(safe), line_sem.at[0, way, step - 1], line_sem.at[1, way, step - 1], target)
                pl.when(inside)(arrived.wait_recv)
            if step < shards - 1:
                source = gtok if step == 0 else block(safe)
                copy = remote(source, block(safe), line_sem.at[0, way, step], line_sem.at[1, way, step], target)
                start(copy, inside & has_next)

    line(0)

    def rows_of(order, core, chip_bit, depth):
        size = d // 2
        first = core * size
        for b in order[:depth]:
            size //= 2
            first = first + chip_bit(b) * size
        return pl.ds(pl.multiple_of(first, 16), size)

    orders = (tuple(range(bits)), tuple(reversed(range(bits))))
    sides = (side_a, side_b)
    parts = (part_a, part_b)

    for s in range(shards):
        away = pl.ds(pl.multiple_of((1 - here.core) * (d // 2), 16), d // 2)
        start(remote(dw.at[s, away], half.at[s], h_sem.at[0, s], h_sem.at[1, s], here.mate()))

    sums[0] = small[...]
    stages = bits + 1

    def small_stage(i):
        target = here.mate() if i == 0 else here.across(1 << (i - 1))
        copy = remote(sums.at[i], sums_in.at[i], t_sem.at[0, i], t_sem.at[1, i], target)
        start(copy)

        def finish():
            copy.wait_recv()
            sums[i + 1] = sums[i] + sums_in[i]

        return finish

    small_finish = small_stage(0)

    def flipped(b):
        return lambda c: 1 - here.bit(c) if c == b else here.bit(c)

    def plane_send(s, depth):
        for side in range(2):
            b = orders[side][depth]
            rows = rows_of(orders[side], here.core, flipped(b), depth + 1)
            size = d >> (depth + 2)
            target = parts[side].at[depth, s, pl.ds(0, size)]
            start(remote(acc.at[s, rows, sides[side]], target, q_sem.at[0, side, depth, s], q_sem.at[1, side, depth, s], here.across(1 << b)))

    def plane_add(s, depth):
        for side in range(2):
            b = orders[side][depth]
            size = d >> (depth + 2)
            rows = rows_of(orders[side], here.core, here.bit, depth + 1)
            target = parts[side].at[depth, s, pl.ds(0, size)]
            remote(target, target, q_sem.at[0, side, depth, s], q_sem.at[1, side, depth, s], here.across(1 << b)).wait_recv()
            acc[s, rows, sides[side]] = (
                acc[s, rows, sides[side]].astype(F32) + parts[side][depth, s, pl.ds(0, size), :].astype(F32)
            ).astype(BF16)

    def half_add(s):
        mine = pl.ds(pl.multiple_of(here.core * (d // 2), 16), d // 2)
        remote(half.at[s], half.at[s], h_sem.at[0, s], h_sem.at[1, s], here.mate()).wait_recv()
        acc[s, mine, :] = (dw[s, mine, :].astype(F32) + half[s].astype(F32)).astype(BF16)

    lasts = (last_a, last_b)

    def mine_rows(side):
        return rows_of(orders[side], here.core, here.bit, bits)

    def shard_send(k):
        s = lax.rem(here.z + k, shards)
        for side in range(2):
            start(remote(acc.at[s, mine_rows(side), sides[side]], lasts[side].at[k], l_sem.at[0, side, k], l_sem.at[1, side, k], here.along(k)))

    for s in range(shards):
        half_add(s)
        plane_send(s, 0)
    small_finish()
    line(1)
    for depth in range(1, bits):
        small_finish = small_stage(depth)
        for s in range(shards):
            plane_add(s, depth - 1)
            plane_send(s, depth)
        small_finish()
        if depth + 1 < shards:
            line(depth + 1)
    small_finish = small_stage(bits)
    for s in range(shards):
        plane_add(s, bits - 1)
    small_finish()
    for k in range(1, shards):
        shard_send(k)
    for k in range(1, shards):
        start(remote(sums.at[stages], sums_in.at[stages + k - 1], t_sem.at[0, stages + k - 1], t_sem.at[1, stages + k - 1], here.along(k)))
    for step in range(bits + 1, shards):
        line(step)
    total = sums[stages]
    for k in range(1, shards):
        slot = stages + k - 1
        remote(sums.at[stages], sums_in.at[slot], t_sem.at[0, slot], t_sem.at[1, slot], here.along(k)).wait_recv()
        total = total + sums_in[slot]
    small_out[...] = total
    for side in range(2):
        rows = mine_rows(side)
        total = acc[here.z, rows, sides[side]].astype(F32)
        for k in range(1, shards):
            slot = lasts[side].at[k]
            remote(slot, slot, l_sem.at[0, side, k], l_sem.at[1, side, k], here.along(k)).wait_recv()
            total = total + lasts[side][k].astype(F32)
        final[rows, sides[side]] = total.astype(BF16)
    for side in range(2):
        for m in range(1, chips):
            rows = mine_rows(side)
            spot = final.at[rows, sides[side]]
            start(remote(spot, spot, f_sem.at[0, side, m], f_sem.at[1, side, m], here.across(m)))
        spot = final.at[mine_rows(side), sides[side]]
        start(remote(spot, spot, g_sem.at[0, side, 0], g_sem.at[1, side, 0], here.mate()))

    def theirs(side, m, core):
        return final.at[rows_of(orders[side], core, lambda b: 1 - here.bit(b) if m >> b & 1 else here.bit(b), bits), sides[side]]

    for side in range(2):
        for m in range(1, chips):
            spot = theirs(side, m, here.core)
            remote(spot, spot, f_sem.at[0, side, m], f_sem.at[1, side, m], here.across(m)).wait_recv()
            start(remote(spot, spot, g_sem.at[0, side, m], g_sem.at[1, side, m], here.mate()))
    for side in range(2):
        for m in range(chips):
            spot = theirs(side, m, 1 - here.core)
            remote(spot, spot, g_sem.at[0, side, m], g_sem.at[1, side, m], here.mate()).wait_recv()
    for copy, when in sends:
        if when is None:
            copy.wait_send()
        else:
            pl.when(when)(copy.wait_send)
    own.wait()


def run_reduce(mesh_shape, gtok, dw, small):
    shards, chips = mesh_shape["mp"], mesh_shape["dp"] // 2
    bits = int(math.log2(chips))
    anywhere = pl.BlockSpec(memory_space=pl.ANY)
    here = pl.BlockSpec(memory_space=pltpu.VMEM)
    dma = pltpu.SemaphoreType.DMA
    _, d, columns = dw.shape
    split = columns // 2
    finish = d // (2 * chips)
    return pl.pallas_call(
        functools.partial(reduce_kernel, mesh_shape),
        out_shape=(
            jax.ShapeDtypeStruct((shards * gtok.shape[0], d), gtok.dtype),
            jax.ShapeDtypeStruct((d, columns), BF16),
            jax.ShapeDtypeStruct(small.shape, F32),
        ),
        in_specs=[anywhere, here, here],
        out_specs=(anywhere, here, here),
        scratch_shapes=[
            pltpu.VMEM((shards, d, columns), BF16),
            pltpu.VMEM((shards, d // 2, columns), BF16),
            pltpu.VMEM((bits, shards, d // 4, split), BF16),
            pltpu.VMEM((bits, shards, d // 4, split), BF16),
            pltpu.VMEM((shards, finish, split), BF16),
            pltpu.VMEM((shards, finish, split), BF16),
            pltpu.VMEM((bits + 2, *small.shape), F32),
            pltpu.VMEM((bits + shards, *small.shape), F32),
            dma((1,)),
            dma((2, 2, shards)),
            dma((2, shards)),
            dma((2, 2, bits, shards)),
            dma((2, 2, shards)),
            dma((2, 2, chips)),
            dma((2, 2, chips)),
            dma((2, bits + shards)),
        ],
        compiler_params=pltpu.CompilerParams(collective_id=1, has_side_effects=True, vmem_limit_bytes=VMEM_LIMIT),
    )(gtok, dw, small)


def relative_bias(table, offset_index):
    onehot = (offset_index.reshape(1, AREA * AREA) == lax.broadcasted_iota(jnp.int32, (table.shape[1], 1), 0)).astype(BF16)
    values = jnp.dot(table.astype(BF16), onehot, preferred_element_type=F32) * LOG2E
    values = jnp.pad(values.reshape(-1, AREA, AREA), ((0, 0), (0, PAD - AREA), (0, 0)))
    return jnp.pad(values, ((0, 0), (0, 0), (0, LANES - AREA)), constant_values=-1e30)


def table_grad(scores, offset_index, table_rows):
    onehot = (offset_index.reshape(AREA * AREA, 1) == lax.broadcasted_iota(jnp.int32, (1, table_rows), 1)).astype(BF16)
    flat = scores[:, :AREA, :AREA].reshape(-1, AREA * AREA)
    return jnp.dot(flat.astype(BF16), onehot, preferred_element_type=F32)


def local(
    mesh_shape,
    tokens,
    cotangent,
    group_windows,
    offset_index,
    first_gain,
    first_shift,
    triple_weight,
    query_value_bias,
    bias_table,
    output_weight,
    output_bias,
    second_gain,
    second_shift,
    expand_weight,
    expand_bias,
    shrink_weight,
    shrink_bias,
):
    z = lax.axis_index("mp")
    shards = mesh_shape["mp"]
    d, _, loc = triple_weight.shape
    units = expand_weight.shape[1]
    table_rows, loc_heads = bias_table.shape
    sizes = Sizes(shards, loc, units)
    shard = jnp.concatenate(
        [triple_weight.transpose(1, 2, 0).reshape(3 * loc, d), output_weight, expand_weight.T, shrink_weight], axis=0
    )

    def widen(v):
        return jnp.pad(v, ((0, 0), (0, 512 - v.shape[1])))

    small = jnp.concatenate(
        [widen(expand_bias[None]), widen(query_value_bias.reshape(1, 2 * loc)), widen(bias_table.T)], axis=0
    ).astype(F32)
    small = jnp.pad(small, ((0, 8 - small.shape[0]), (0, 0)))
    weights, small = run_gather(mesh_shape, shard, small)
    hid_bias = small[:, 0:1, :units]
    pair = small[:, 1, : 2 * loc].reshape(shards, 2, loc)
    wide_bias = jnp.concatenate([pair[:, 0].reshape(1, -1), jnp.zeros((1, sizes.width), F32), pair[:, 1].reshape(1, -1)], axis=1)
    table = small[:, 2 : 2 + loc_heads, :table_rows].reshape(shards * loc_heads, table_rows)
    bias = relative_bias(table, offset_index)
    blank = jnp.zeros_like(first_gain)
    vecs = jnp.stack([first_gain, first_shift, output_bias, second_gain, second_shift, shrink_bias, blank, blank]).astype(F32)
    params = (bias, vecs, wide_bias, hid_bias, weights)
    chunks = tokens.shape[0] // CHUNK
    own = chunks // shards
    order = lax.rem(z * own + jnp.arange(chunks, dtype=jnp.int32), chunks)
    result, gtok, dw, dbias, sums, unit_sums = run_own(sizes, order[:own], group_windows, tokens, cotangent, *params)
    result = run_forward(sizes, order[own:], group_windows, tokens, result, *params)
    grads = table_grad(dbias, offset_index, table_rows)
    grads = jnp.pad(grads, ((0, 0), (0, 384 - table_rows)))
    packed = jnp.concatenate([sums, unit_sums.reshape(-1, d), grads.reshape(-1, d)], axis=0)
    grad_tokens, final, packed = run_reduce(mesh_shape, gtok, dw, packed)
    sums, rest = packed[:8], packed[8:]
    count = shards * units // d
    unit_total = lax.dynamic_slice_in_dim(rest[:count].reshape(-1), z * units, units)
    table_total = rest[count:].reshape(shards * loc_heads, 384)[:, :table_rows]
    table_total = lax.dynamic_slice_in_dim(table_total, z * loc_heads, loc_heads, 0).T
    pair_total = lax.dynamic_slice_in_dim(sums[0:2], z * loc, loc, 1)
    final = final.astype(F32)
    return (
        result,
        grad_tokens,
        sums[6],
        sums[7],
        final[:, : 3 * loc].reshape(d, 3, loc),
        pair_total,
        table_total,
        final[:, 3 * loc : 4 * loc].T,
        sums[5],
        sums[3],
        sums[4],
        final[:, 4 * loc : 4 * loc + units],
        unit_total,
        final[:, 4 * loc + units :].T,
        sums[2],
    )


def solution(mesh):
    in_specs = (
        P("dp", None),
        P("dp", None),
        P("dp"),
        P(),
        P(),
        P(),
        P(None, None, "mp"),
        P(None, "mp"),
        P(None, "mp"),
        P("mp", None),
        P(),
        P(),
        P(),
        P(None, "mp"),
        P("mp"),
        P("mp", None),
        P(),
    )
    out_specs = (
        P("dp", None),
        P("dp", None),
        P(),
        P(),
        P(None, None, "mp"),
        P(None, "mp"),
        P(None, "mp"),
        P("mp", None),
        P(),
        P(),
        P(),
        P(None, "mp"),
        P("mp"),
        P("mp", None),
        P(),
    )
    step = functools.partial(local, dict(mesh.shape))
    return jax.shard_map(step, mesh=mesh, in_specs=in_specs, out_specs=out_specs, check_vma=False)
```

time: 770 us -> 299 us (0.39)
  waiting for transfers between devices: 512 us -> 0 us
  Pallas kernels: 0 us -> 262 us
  matrix products: 83.9 us -> 5.22 us
  other arithmetic: 74.7 us -> 6.17 us
  local copies, waits for them, and re-layouts: 53.7 us -> 23.2 us
  blocking collectives: 24 us -> 0 us
  between operations: 15.2 us -> 1.71 us
    psum x4 -> x0, waiting for transfers between devices: 512 us -> none  [the longest x1 226 us: local(): lax.psum(shrink_term.astype(jnp.bfloat16), 'mp').astype(jnp.float32)]
    pallas_call x0 -> x4, Pallas kernels: none -> 262 us  [the longest x1 88.6 us: run_reduce(): pl.pallas_call(functools.partial(reduce_kernel, mesh_shape), out_shape=(j...]
    dot_general x20 -> x2, matrix products: 83.9 us -> 5.22 us  [the longest x1 2.75 us: table_grad(): return jnp.dot(flat.astype(BF16), onehot, preferred_element_type=F32)]
    reduce_sum x10 -> x0, other arithmetic: 42.6 us -> none  [the longest x1 8.86 us: local(): second_gain_term = jnp.sum(grad_second * second_hat, axis=0)]
    convert_element_type x26 -> x2, other arithmetic: 32 us -> 1 us  [the longest x1 0.61 us: local(): jnp.stack([first_gain, first_shift, output_bias, second_gain, second_shif...]
    psum x1 -> x0, blocking collectives: 24 us -> none  [local(): lax.psum(first_gain_term.astype(jnp.bfloat16), 'dp').astype(jnp.float32)]
    squeeze x2 -> x0, local copies, waits for them, and re-layouts: 12.4 us -> none  [the longest x1 6.3 us: local(): triple[:, 0] + bias_wide[0]]
    convert_element_type x7 -> x2, local copies, waits for them, and re-layouts: 12.2 us -> 0.33 us  [the longest x1 0.31 us: table_grad(): return jnp.dot(flat.astype(BF16), onehot, preferred_element_type=F32)]
  transfers between devices with their start and end apart: 4 -> 0, of which waited for: 4 -> 0; matrix products, arithmetic and copies ran while one was open for 4% -> 0% of each run, Pallas kernels for 0% -> 0%
where the time goes in v2:
time: 299 us; the launch traced here: 298 us
  Pallas kernels  262 us (88%)
  local copies, waits for them, and re-layouts  23.2 us (8%)
  other arithmetic  6.17 us (2%)
  matrix products  5.22 us (2%)
    pallas_call x1, Pallas kernels, run_reduce(): pl.pallas_call(functools.partial(reduce_kernel, mesh_shape), out_shape=(j...  88.6 us
    pallas_call x1, Pallas kernels, run_forward(): pl.pallas_call(functools.partial(forward_kernel, sizes), out_shape=jax.Sh...  59.8 us
    pallas_call x1, Pallas kernels, run_own(): pl.pallas_call(functools.partial(own_kernel, sizes), out_shape=outs, grid...  58.4 us
    pallas_call x1, Pallas kernels, run_gather(): pl.pallas_call(functools.partial(gather_kernel, mesh_shape), out_shape=(j...  55 us
    unnamed x43, local copies, waits for them, and re-layouts  10.2 us

profile of v2, /device:TPU:0, one launch (start us, length us, event | category | flops | bytes accessed | tf_op | source)
XLA Modules:
  0.0 298.1 jit_solution(2143552675289109533)
XLA Ops:
  0.7 0.6 slice.79.order
  2.0 1.3 copy.41
  3.2 1.2 copy.40
  4.4 2.3 pad_maximum_fusion.shard
  6.8 0.6 pad_convert_fusion.small
  7.4 55.0 %shard_map.280 = (bf16[4,1536,512]{2,1,0:T(8,128)(2,1)}, f32[4,8,512]{2,1,0:T(8,128)}) custom-call(bf16[1536,512]{1,0:T(8,128)(2,1)} %pad_maximum_fusion.shard, f32[8,512]{1,0:T(8,128)} %pad_convert_fusion.small), custom_call_target="tpu_custom_call" | custom-call | tf_op jit(solution)/shard_map/pallas_call | solution.py:510
  62.4 0.8 slice.118
  63.4 2.5 fusion.2
  65.9 0.5 reshape.64
  66.4 1.0 pad_select_fusion.bias
  67.5 0.6 convert_element_type.28.vecs
  68.2 0.8 slice.82
  68.9 0.6 fusion.10.wide_bias
  69.5 1.4 slice.85.hid_bias
  71.0 58.4 %shard_map.281 = (bf16[3200,512]{1,0:T(8,128)(2,1)}, bf16[800,512]{1,0:T(8,128)(2,1)}, bf16[4,512,1536]{2,1,0:T(8,128)(2,1)}, f32[16,104,128]{2,1,0:T(8,128)}, f32[8,512]{1,0:T(8,128)}, /*index=5*/f32[4,1,512]{2,1,0:T(1,128)}) custom-call(s32[2]{0:T(128)} %bitcast.57, s32[1]{0:T(128)S(6)} %copy.59.live, bf16[3200,512]{1,0:T(8,128)(2,1)} %tok_ref.3, ...), custom_call_target="tpu_custom_call" | custom-call | tf_op jit(solution)/shard_map/pallas_call | solution.py:370
  129.4 59.8 %shard_map.282 = bf16[3200,512]{1,0:T(8,128)(2,1)} custom-call(s32[6]{0:T(128)} %slice.79.order, s32[1]{0:T(128)S(6)} %copy.59.live, bf16[3200,512]{1,0:T(8,128)(2,1)} %tok_ref.3, bf16[3200,512]{1,0:T(8,128)(2,1)} %get-tuple-element.28.held, f32[16,104,128]{2,1,0:T(8,128)} %pad_select_fusion.bias, ...), custom_call_target="tpu_custom_call", output_to_operand_aliasing={{}: (3, {})} | custom-call | tf_op jit(solution)/shard_map/pallas_call | solution.py:343
  189.6 2.8 fusion
  192.4 0.6 pad_maximum_fusion.1.small
  193.1 88.6 %shard_map.283 = (bf16[3200,512]{1,0:T(8,128)(2,1)}, bf16[512,1536]{1,0:T(8,128)(2,1)}, f32[24,512]{1,0:T(8,128)}) custom-call(bf16[800,512]{1,0:T(8,128)(2,1)} %get-tuple-element.29.gtok, bf16[4,512,1536]{2,1,0:T(8,128)(2,1)} %get-tuple-element.30.dw, f32[24,512]{1,0:T(8,128)} %pad_maximum_fusion.1.small), custom_call_target="tpu_custom_call" | custom-call | tf_op jit(solution)/shard_map/pallas_call | solution.py:711
  281.7 1.6 fusion.12
  283.3 1.0 slice.105
  284.6 1.1 copy.45
  285.7 0.6 constant_dynamic-slice_fusion
  286.3 0.6 dynamic-slice_bitcast_fusion
  286.9 0.4 convert_element_type.30
  287.3 1.7 copy-done.1
  289.0 0.8 copy.46
  289.9 1.1 slice.108
  291.0 0.7 dynamic_slice.11
  291.6 1.3 slice_bitcast_fusion
  292.9 1.3 copy.47
  294.2 3.8 %copy.60 = bf16[3200,512]{1,0:T(8,128)(2,1)} copy(bf16[3200,512]{1,0:T(8,128)(2,1)} %get-tuple-element.91) | data formatting | bytes 6553600
  (62 shorter events, 1.0 us)
Async XLA Ops:
  0.6 6.1 %copy-start.7 = (bf16[361,4]{0,1:T(4,128)(2,1)S(1)}, bf16[361,4]{0,1:T(4,128)(2,1)}, u32[]{:S(2)}) copy-start(bf16[361,4]{0,1:T(4,128)(2,1)} %param.25) | copy-start | bytes 8668
  0.7 6.1 %copy-start.16 = (bf16[2,128]{1,0:T(2,128)(2,1)S(1)}, bf16[2,128]{1,0:T(2,128)(2,1)}, u32[]{:S(2)}) copy-start(bf16[2,128]{1,0:T(2,128)(2,1)} %param.24) | copy-start | bytes 1540
  0.7 6.1 %copy-start.8 = (bf16[512]{0:T(512)(128)(2,1)S(1)}, bf16[512]{0:T(512)(128)(2,1)}, u32[]{:S(2)}) copy-start(bf16[512]{0:T(512)(128)(2,1)} %param.31) | copy-start | bytes 3076
  0.7 61.7 %copy-start.15 = (s32[8]{0:T(128)}, s32[8]{0:T(128)S(1)}, u32[]{:S(2)}) copy-start(s32[8]{0:T(128)S(1)} %compare_select_fusion) | copy-start | bytes 100
  1.9 61.3 %copy-start.4 = (s32[100,100]{1,0:T(8,128)S(1)}, s32[100,100]{1,0:T(8,128)}, u32[]{:S(2)}) copy-start(s32[100,100]{1,0:T(8,128)} %param.20) | copy-start | bytes 120004
  63.4 4.0 %copy-start.9 = (bf16[512]{0:T(512)(128)(2,1)S(1)}, bf16[512]{0:T(512)(128)(2,1)}, u32[]{:S(2)}) copy-start(bf16[512]{0:T(512)(128)(2,1)} %param.21) | copy-start | bytes 3076
  63.4 4.0 %copy-start.10 = (bf16[512]{0:T(512)(128)(2,1)S(1)}, bf16[512]{0:T(512)(128)(2,1)}, u32[]{:S(2)}) copy-start(bf16[512]{0:T(512)(128)(2,1)} %param.22) | copy-start | bytes 3076
  63.4 4.0 %copy-start.11 = (bf16[512]{0:T(512)(128)(2,1)S(1)}, bf16[512]{0:T(512)(128)(2,1)}, u32[]{:S(2)}) copy-start(bf16[512]{0:T(512)(128)(2,1)} %param.27) | copy-start | bytes 3076
  63.4 4.0 %copy-start.12 = (bf16[512]{0:T(512)(128)(2,1)S(1)}, bf16[512]{0:T(512)(128)(2,1)}, u32[]{:S(2)}) copy-start(bf16[512]{0:T(512)(128)(2,1)} %param.28) | copy-start | bytes 3076
  63.4 4.0 %copy-start.13 = (bf16[512]{0:T(512)(128)(2,1)S(1)}, bf16[512]{0:T(512)(128)(2,1)}, u32[]{:S(2)}) copy-start(bf16[512]{0:T(512)(128)(2,1)} %param.29) | copy-start | bytes 3076
  63.4 4.0 %copy-start.14 = (bf16[512]{0:T(512)(128)(2,1)S(1)}, bf16[512]{0:T(512)(128)(2,1)}, u32[]{:S(2)}) copy-start(bf16[512]{0:T(512)(128)(2,1)} %param.33) | copy-start | bytes 3076
  129.4 59.9 %copy-start.2 = (f32[16,104,128]{2,1,0:T(8,128)S(1)}, f32[16,104,128]{2,1,0:T(8,128)}, u32[]{:S(2)}) copy-start(f32[16,104,128]{2,1,0:T(8,128)} %get-tuple-element.33) | copy-start | bytes 2555908
  189.2 3.2 %copy-start.6 = (f32[4,1,512]{2,1,0:T(1,128)S(1)}, f32[4,1,512]{2,1,0:T(1,128)}, u32[]{:S(2)}) copy-start(f32[4,1,512]{2,1,0:T(1,128)} %get-tuple-element.32) | copy-start | bytes 24580
  189.2 3.2 %copy-start.5 = (f32[8,512]{1,0:T(8,128)S(1)}, f32[8,512]{1,0:T(8,128)}, u32[]{:S(2)}) copy-start(f32[8,512]{1,0:T(8,128)} %get-tuple-element.31) | copy-start | bytes 49156
  281.6 4.1 %copy-start.3 = (f32[24,512]{1,0:T(8,128)S(1)}, f32[24,512]{1,0:T(8,128)}, u32[]{:S(2)}) copy-start(f32[24,512]{1,0:T(8,128)} %get-tuple-element.35) | copy-start | bytes 147460
  281.7 5.3 %copy-start = (bf16[512,1536]{1,0:T(8,128)(2,1)S(1)}, bf16[512,1536]{1,0:T(8,128)(2,1)}, u32[]{:S(2)}) copy-start(bf16[512,1536]{1,0:T(8,128)(2,1)} %get-tuple-element.36) | copy-start | bytes 4718596
  287.3 1.7 copy-start.1

commit v3 on v2

--- a/solution.py
+++ b/solution.py
@@ -273,19 +273,6 @@
     return [jnp.where(first + w < live[0], 1.0, 0.0).astype(F32) for w in range(BATCH)]
 
 
-def forward_kernel(sizes, order, live, tok_ref, held, bias, vecs, wide_bias, hid_bias, weights, out_ref,
-                   wide, xs, work, low, qkv, mixed, middle):
-    @pl.when(pl.program_id(0) == 0)
-    def _():
-        xs[...] = jnp.zeros_like(xs)
-
-    load_rows(tok_ref[...], wide, xs)
-    attention(sizes, bias, vecs, wide_bias, weights, xs, work, low, qkv, mixed, middle, None)
-    second_norm(vecs, middle, work, low)
-    feed(sizes, hid_bias, vecs, weights, middle, low, work)
-    store_rows(work, wide, out_ref, live_scales(order[pl.program_id(0)] * BATCH, live))
-
-
 def own_kernel(sizes, order, live, tok_ref, cot_ref, bias, vecs, wide_bias, hid_bias, weights,
                out_ref, gtok_ref, dw_ref, dbias, sums, unit_sums,
                wide, xs, work, low, qkv, mixed, middle, glow, back, gmid, gmix, dqkv, keep, dw):
@@ -335,24 +322,6 @@
         pltpu.VMEM((ROWS, sizes.width), F32),
         pltpu.VMEM((ROWS, d), F32),
     ]
-
-
-def run_forward(sizes, order, live, tokens, held, *params):
-    d = tokens.shape[1]
-    block = pl.BlockSpec((CHUNK, d), lambda i, order, live: (order[i], 0))
-    return pl.pallas_call(
-        functools.partial(forward_kernel, sizes),
-        out_shape=jax.ShapeDtypeStruct(tokens.shape, BF16),
-        grid_spec=pltpu.PrefetchScalarGridSpec(
-            num_scalar_prefetch=2,
-            grid=(order.shape[0],),
-            in_specs=[block, pl.BlockSpec(memory_space=pl.ANY)] + [whole_block(a) for a in params],
-            out_specs=block,
-            scratch_shapes=forward_scratch(sizes, d),
-        ),
-        input_output_aliases={3: 0},
-        compiler_params=pltpu.CompilerParams(vmem_limit_bytes=VMEM_LIMIT),
-    )(order, live, tokens, held, *params)
 
 
 def run_own(sizes, order, live, tokens, cotangent, *params):
@@ -520,223 +489,357 @@
     )(shard, small)
 
 
-def reduce_kernel(mesh_shape, gtok, dw, small, gout, final, small_out,
-                  acc, half, part_a, part_b, last_a, last_b, sums, sums_in,
-                  own_sem, line_sem, h_sem, q_sem, l_sem, f_sem, g_sem, t_sem):
-    here = Place(mesh_shape)
-    shards, chips, bits = here.shards, here.chips, here.bits
-    d, columns = dw.shape[1], dw.shape[2]
-    split = columns // 2
-    side_a, side_b = pl.ds(0, split), pl.ds(split, split)
-    sends = []
-
-    def start(copy, when=None):
-        sends.append((copy, when))
+class Reduction:
+    def __init__(self, mesh_shape, gtok, gout, dw, final, small_out, scratch):
+        (self.acc, self.half, self.parts, self.lasts, self.sums, self.sums_in,
+         self.own_sem, self.line_sem, self.h_sem, self.q_sem, self.l_sem, self.f_sem, self.g_sem, self.t_sem) = scratch
+        self.gtok, self.gout, self.dw, self.final, self.small_out = gtok, gout, dw, final, small_out
+        self.here = Place(mesh_shape)
+        self.d, self.columns = dw.shape[1], dw.shape[2]
+        split = self.columns // 2
+        self.sides = (pl.ds(0, split), pl.ds(split, split))
+        bits = self.here.bits
+        self.orders = (tuple(range(bits)), tuple(reversed(range(bits))))
+        self.stages = bits + 1
+        self.sent = []
+
+    def send(self, make, when=None):
+        self.sent.append((make, when))
         if when is None:
-            copy.start()
+            make().start()
         else:
-            pl.when(when)(copy.start)
-
-    here.greet(here.everyone())
-
-    block_rows = gtok.shape[0]
-
-    def block(z):
-        return gout.at[pl.ds(pl.multiple_of(z * block_rows, 16), block_rows)]
-
-    own = pltpu.make_async_copy(gtok, block(here.z), own_sem.at[0])
-    own.start()
-    up, down = (here.dp, jnp.minimum(here.z + 1, shards - 1)), (here.dp, jnp.maximum(here.z - 1, 0))
-
-    def line(step):
-        for way, (target, sign) in enumerate(((up, 1), (down, -1))):
-            held = here.z - sign * step
-            inside = (held >= 0) & (held < shards)
-            nxt = here.z + sign
-            has_next = (nxt >= 0) & (nxt < shards)
-            safe = jnp.clip(held, 0, shards - 1)
+            pl.when(when())(lambda: make().start())
+
+    def finish_sends(self):
+        for make, when in self.sent:
+            if when is None:
+                make().wait_send()
+            else:
+                pl.when(when())(lambda make=make: make().wait_send())
+
+
+    def block(self, z):
+        rows = self.gtok.shape[0]
+        return self.gout.at[pl.ds(pl.multiple_of(z * rows, 16), rows)]
+
+    def own_copy(self):
+        return pltpu.make_async_copy(self.gtok, self.block(self.here.z), self.own_sem.at[0])
+
+    def line_copy(self, way, step, arriving=False):
+        here, sign = self.here, 1 - 2 * way
+        held = jnp.clip(here.z - sign * step, 0, here.shards - 1)
+        at = step - 1 if arriving else step
+        source = self.gtok if at == 0 and not arriving else self.block(held)
+        target = (here.dp, jnp.clip(here.z + sign, 0, here.shards - 1))
+        return remote(source, self.block(held), self.line_sem.at[0, way, at], self.line_sem.at[1, way, at], target)
+
+    def line(self, step):
+        here = self.here
+        for way in range(2):
+            sign = 1 - 2 * way
+
+            def inside(sign=sign):
+                held = here.z - sign * step
+                return (held >= 0) & (held < here.shards)
+
+            def onward(sign=sign):
+                return (here.z + sign >= 0) & (here.z + sign < here.shards)
+
             if step > 0:
-                arrived = remote(block(safe), block(safe), line_sem.at[0, way, step - 1], line_sem.at[1, way, step - 1], target)
-                pl.when(inside)(arrived.wait_recv)
-            if step < shards - 1:
-                source = gtok if step == 0 else block(safe)
-                copy = remote(source, block(safe), line_sem.at[0, way, step], line_sem.at[1, way, step], target)
-                start(copy, inside & has_next)
-
-    line(0)
-
-    def rows_of(order, core, chip_bit, depth):
-        size = d // 2
+                pl.when(inside())(lambda way=way: self.line_copy(way, step, True).wait_recv())
+            if step < here.shards - 1:
+                self.send(
+                    functools.partial(self.line_copy, way, step),
+                    lambda inside=inside, onward=onward: inside() & onward(),
+                )
+
+
+    def rows_of(self, side, core, chip_bit, depth):
+        size = self.d // 2
         first = core * size
-        for b in order[:depth]:
+        for b in self.orders[side][:depth]:
             size //= 2
             first = first + chip_bit(b) * size
         return pl.ds(pl.multiple_of(first, 16), size)
 
-    orders = (tuple(range(bits)), tuple(reversed(range(bits))))
-    sides = (side_a, side_b)
-    parts = (part_a, part_b)
-
-    for s in range(shards):
-        away = pl.ds(pl.multiple_of((1 - here.core) * (d // 2), 16), d // 2)
-        start(remote(dw.at[s, away], half.at[s], h_sem.at[0, s], h_sem.at[1, s], here.mate()))
-
-    sums[0] = small[...]
-    stages = bits + 1
-
-    def small_stage(i):
+    def half_rows(self, core):
+        return pl.ds(pl.multiple_of(core * (self.d // 2), 16), self.d // 2)
+
+    def half_copy(self, s):
+        rows = self.half_rows(1 - self.here.core)
+        return remote(self.dw.at[s, rows], self.half.at[s], self.h_sem.at[0, s], self.h_sem.at[1, s], self.here.mate())
+
+    def half_send(self, s):
+        self.send(functools.partial(self.half_copy, s))
+
+    def half_add(self, s):
+        self.half_copy(s).wait_recv()
+        mine = self.half_rows(self.here.core)
+        self.acc[s, mine, :] = (self.dw[s, mine, :].astype(F32) + self.half[s].astype(F32)).astype(BF16)
+
+    def plane_copy(self, s, depth, side):
+        here = self.here
+        b = self.orders[side][depth]
+        rows = self.rows_of(side, here.core, lambda c: 1 - here.bit(c) if c == b else here.bit(c), depth + 1)
+        target = self.parts[side].at[depth, s, pl.ds(0, self.d >> (depth + 2))]
+        sems = self.q_sem
+        return remote(
+            self.acc.at[s, rows, self.sides[side]], target, sems.at[0, side, depth, s], sems.at[1, side, depth, s], here.across(1 << b)
+        )
+
+    def plane_send(self, s, depth):
+        for side in range(2):
+            self.send(functools.partial(self.plane_copy, s, depth, side))
+
+    def plane_add(self, s, depth):
+        for side in range(2):
+            self.plane_copy(s, depth, side).wait_recv()
+            rows = self.rows_of(side, self.here.core, self.here.bit, depth + 1)
+            arrived = self.parts[side][depth, s, pl.ds(0, self.d >> (depth + 2)), :]
+            here = self.acc[s, rows, self.sides[side]]
+            self.acc[s, rows, self.sides[side]] = (here.astype(F32) + arrived.astype(F32)).astype(BF16)
+
+    def mine(self, side):
+        return self.rows_of(side, self.here.core, self.here.bit, self.here.bits)
+
+    def shard_copy(self, side, k):
+        here = self.here
+        s = lax.rem(here.z + k, here.shards)
+        return remote(
+            self.acc.at[s, self.mine(side), self.sides[side]], self.lasts[side].at[k], self.l_sem.at[0, side, k], self.l_sem.at[1, side, k], here.along(k)
+        )
+
+    def shard_sends(self):
+        for k in range(1, self.here.shards):
+            for side in range(2):
+                self.send(functools.partial(self.shard_copy, side, k))
+
+    def shard_adds(self):
+        for side in range(2):
+            rows = self.mine(side)
+            total = self.acc[self.here.z, rows, self.sides[side]].astype(F32)
+            for k in range(1, self.here.shards):
+                self.shard_copy(side, k).wait_recv()
+                total = total + self.lasts[side][k].astype(F32)
+            self.final[rows, self.sides[side]] = total.astype(BF16)
+
+    def final_spot(self, side, m, core):
+        here = self.here
+        rows = self.rows_of(side, core, lambda b: 1 - here.bit(b) if m >> b & 1 else here.bit(b), here.bits)
+        return self.final.at[rows, self.sides[side]]
+
+    def final_copy(self, side, m, arriving=False):
+        here = self.here
+        spot = self.final_spot(side, m if arriving else 0, here.core)
+        return remote(spot, spot, self.f_sem.at[0, side, m], self.f_sem.at[1, side, m], here.across(m))
+
+    def final_relay(self, side, m, arriving=False):
+        here = self.here
+        spot = self.final_spot(side, m, 1 - here.core if arriving else here.core)
+        return remote(spot, spot, self.g_sem.at[0, side, m], self.g_sem.at[1, side, m], here.mate())
+
+    def final_spread(self):
+        chips = self.here.chips
+        for side in range(2):
+            for m in range(1, chips):
+                self.send(functools.partial(self.final_copy, side, m))
+            self.send(functools.partial(self.final_relay, side, 0))
+        for side in range(2):
+            for m in range(1, chips):
+                self.final_copy(side, m, True).wait_recv()
+                self.send(functools.partial(self.final_relay, side, m))
+        for side in range(2):
+            for m in range(chips):
+                self.final_relay(side, m, True).wait_recv()
+
+
+    def small_copy(self, i):
+        here = self.here
         target = here.mate() if i == 0 else here.across(1 << (i - 1))
-        copy = remote(sums.at[i], sums_in.at[i], t_sem.at[0, i], t_sem.at[1, i], target)
-        start(copy)
-
-        def finish():
-            copy.wait_recv()
-            sums[i + 1] = sums[i] + sums_in[i]
-
-        return finish
-
-    small_finish = small_stage(0)
-
-    def flipped(b):
-        return lambda c: 1 - here.bit(c) if c == b else here.bit(c)
-
-    def plane_send(s, depth):
-        for side in range(2):
-            b = orders[side][depth]
-            rows = rows_of(orders[side], here.core, flipped(b), depth + 1)
-            size = d >> (depth + 2)
-            target = parts[side].at[depth, s, pl.ds(0, size)]
-            start(remote(acc.at[s, rows, sides[side]], target, q_sem.at[0, side, depth, s], q_sem.at[1, side, depth, s], here.across(1 << b)))
-
-    def plane_add(s, depth):
-        for side in range(2):
-            b = orders[side][depth]
-            size = d >> (depth + 2)
-            rows = rows_of(orders[side], here.core, here.bit, depth + 1)
-            target = parts[side].at[depth, s, pl.ds(0, size)]
-            remote(target, target, q_sem.at[0, side, depth, s], q_sem.at[1, side, depth, s], here.across(1 << b)).wait_recv()
-            acc[s, rows, sides[side]] = (
-                acc[s, rows, sides[side]].astype(F32) + parts[side][depth, s, pl.ds(0, size), :].astype(F32)
-            ).astype(BF16)
-
-    def half_add(s):
-        mine = pl.ds(pl.multiple_of(here.core * (d // 2), 16), d // 2)
-        remote(half.at[s], half.at[s], h_sem.at[0, s], h_sem.at[1, s], here.mate()).wait_recv()
-        acc[s, mine, :] = (dw[s, mine, :].astype(F32) + half[s].astype(F32)).astype(BF16)
-
-    lasts = (last_a, last_b)
-
-    def mine_rows(side):
-        return rows_of(orders[side], here.core, here.bit, bits)
-
-    def shard_send(k):
-        s = lax.rem(here.z + k, shards)
-        for side in range(2):
-            start(remote(acc.at[s, mine_rows(side), sides[side]], lasts[side].at[k], l_sem.at[0, side, k], l_sem.at[1, side, k], here.along(k)))
-
-    for s in range(shards):
-        half_add(s)
-        plane_send(s, 0)
-    small_finish()
-    line(1)
-    for depth in range(1, bits):
-        small_finish = small_stage(depth)
-        for s in range(shards):
-            plane_add(s, depth - 1)
-            plane_send(s, depth)
-        small_finish()
-        if depth + 1 < shards:
-            line(depth + 1)
-    small_finish = small_stage(bits)
-    for s in range(shards):
-        plane_add(s, bits - 1)
-    small_finish()
-    for k in range(1, shards):
-        shard_send(k)
-    for k in range(1, shards):
-        start(remote(sums.at[stages], sums_in.at[stages + k - 1], t_sem.at[0, stages + k - 1], t_sem.at[1, stages + k - 1], here.along(k)))
-    for step in range(bits + 1, shards):
-        line(step)
-    total = sums[stages]
-    for k in range(1, shards):
-        slot = stages + k - 1
-        remote(sums.at[stages], sums_in.at[slot], t_sem.at[0, slot], t_sem.at[1, slot], here.along(k)).wait_recv()
-        total = total + sums_in[slot]
-    small_out[...] = total
-    for side in range(2):
-        rows = mine_rows(side)
-        total = acc[here.z, rows, sides[side]].astype(F32)
-        for k in range(1, shards):
-            slot = lasts[side].at[k]
-            remote(slot, slot, l_sem.at[0, side, k], l_sem.at[1, side, k], here.along(k)).wait_recv()
-            total = total + lasts[side][k].astype(F32)
-        final[rows, sides[side]] = total.astype(BF16)
-    for side in range(2):
-        for m in range(1, chips):
-            rows = mine_rows(side)
-            spot = final.at[rows, sides[side]]
-            start(remote(spot, spot, f_sem.at[0, side, m], f_sem.at[1, side, m], here.across(m)))
-        spot = final.at[mine_rows(side), sides[side]]
-        start(remote(spot, spot, g_sem.at[0, side, 0], g_sem.at[1, side, 0], here.mate()))
-
-    def theirs(side, m, core):
-        return final.at[rows_of(orders[side], core, lambda b: 1 - here.bit(b) if m >> b & 1 else here.bit(b), bits), sides[side]]
-
-    for side in range(2):
-        for m in range(1, chips):
-            spot = theirs(side, m, here.core)
-            remote(spot, spot, f_sem.at[0, side, m], f_sem.at[1, side, m], here.across(m)).wait_recv()
-            start(remote(spot, spot, g_sem.at[0, side, m], g_sem.at[1, side, m], here.mate()))
-    for side in range(2):
-        for m in range(chips):
-            spot = theirs(side, m, 1 - here.core)
-            remote(spot, spot, g_sem.at[0, side, m], g_sem.at[1, side, m], here.mate()).wait_recv()
-    for copy, when in sends:
-        if when is None:
-            copy.wait_send()
-        else:
-            pl.when(when)(copy.wait_send)
-    own.wait()
-
-
-def run_reduce(mesh_shape, gtok, dw, small):
+        return remote(self.sums.at[i], self.sums_in.at[i], self.t_sem.at[0, i], self.t_sem.at[1, i], target)
+
+    def small_send(self, i):
+        self.send(functools.partial(self.small_copy, i))
+
+    def small_add(self, i):
+        self.small_copy(i).wait_recv()
+        self.sums[i + 1] = self.sums[i] + self.sums_in[i]
+
+    def small_along(self, k):
+        slot = self.stages + k - 1
+        return remote(
+            self.sums.at[self.stages], self.sums_in.at[slot], self.t_sem.at[0, slot], self.t_sem.at[1, slot], self.here.along(k)
+        )
+
+    def small_sends(self):
+        for k in range(1, self.here.shards):
+            self.send(functools.partial(self.small_along, k))
+
+    def small_total(self):
+        total = self.sums[self.stages]
+        for k in range(1, self.here.shards):
+            self.small_along(k).wait_recv()
+            total = total + self.sums_in[self.stages + k - 1]
+        self.small_out[...] = total
+
+    def steps(self):
+        here = self.here
+        shards, bits = here.shards, here.bits
+        steps = []
+
+        def first():
+            self.small_add(0)
+            self.small_send(1)
+            for s in range(shards):
+                self.half_add(s)
+                self.plane_send(s, 0)
+
+        steps.append(first)
+        for depth in range(1, bits):
+
+            def middle(depth=depth):
+                self.small_add(depth)
+                self.small_send(depth + 1)
+                for s in range(shards):
+                    self.plane_add(s, depth - 1)
+                    self.plane_send(s, depth)
+
+            steps.append(middle)
+
+        def last():
+            self.small_add(bits)
+            self.small_sends()
+            for s in range(shards):
+                self.plane_add(s, bits - 1)
+            self.shard_sends()
+
+        steps.append(last)
+        return steps
+
+    def start(self):
+        self.own_copy().start()
+        self.line(0)
+        self.small_send(0)
+        for s in range(self.here.shards):
+            self.half_send(s)
+
+    def end(self):
+        self.small_total()
+        self.shard_adds()
+        self.final_spread()
+        self.finish_sends()
+        self.own_copy().wait()
+
+
+def reduce_scratch(mesh_shape, d, columns, small_shape):
     shards, chips = mesh_shape["mp"], mesh_shape["dp"] // 2
     bits = int(math.log2(chips))
+    split, finish = columns // 2, d // (2 * chips)
+    dma = pltpu.SemaphoreType.DMA
+    return [
+        pltpu.VMEM((shards, d, columns), BF16),
+        pltpu.VMEM((shards, d // 2, columns), BF16),
+        [pltpu.VMEM((bits, shards, d // 4, split), BF16)] * 2,
+        [pltpu.VMEM((shards, finish, split), BF16)] * 2,
+        pltpu.VMEM((bits + 2, *small_shape), F32),
+        pltpu.VMEM((bits + shards, *small_shape), F32),
+        dma((1,)),
+        dma((2, 2, shards)),
+        dma((2, shards)),
+        dma((2, 2, bits, shards)),
+        dma((2, 2, shards)),
+        dma((2, 2, chips)),
+        dma((2, 2, chips)),
+        dma((2, bits + shards)),
+    ]
+
+
+def rest_kernel(sizes, mesh_shape, live, tokens, held, bias, vecs, wide_bias, hid_bias, weights, gtok, dw, small,
+                result, gout, final, small_out, rows_in, rows_out, in_sem, out_sem, forward, reduction):
+    wide, xs, work, low, qkv, mixed, middle = forward
+    here = Place(mesh_shape)
+    red = Reduction(mesh_shape, gtok, gout, dw, final, small_out, reduction)
+    own = gtok.shape[0] // CHUNK
+    chunks = sizes.shards * own
+    extra = chunks - own
+    here.greet(here.everyone())
+
+    def chunk_of(i):
+        return lax.rem((here.z + 1) * own + i, chunks)
+
+    def rows(i):
+        return pl.ds(pl.multiple_of(chunk_of(i) * CHUNK, 16), CHUNK)
+
+    def fetch(i):
+        return pltpu.make_async_copy(tokens.at[rows(i)], rows_in.at[lax.rem(i, 2)], in_sem.at[lax.rem(i, 2)])
+
+    def put(i):
+        return pltpu.make_async_copy(rows_out.at[lax.rem(i, 2)], result.at[rows(i)], out_sem.at[lax.rem(i, 2)])
+
+    fetch(0).start()
+    red.sums[0] = small[...]
+    red.start()
+    xs[...] = jnp.zeros_like(xs)
+    steps = red.steps()
+    count = len(steps) + sizes.shards - 1
+    moves = {}
+    for n, step in enumerate(steps):
+        moves.setdefault(min(n * extra // len(steps), extra - 1), []).append(step)
+    for n in range(1, sizes.shards):
+        moves.setdefault(min(1 + 2 * (n - 1), extra - 1), []).append(functools.partial(red.line, n))
+
+    def chunk(i, _):
+        fetch(i).wait()
+        pl.when(i + 1 < extra)(lambda: fetch(i + 1).start())
+        slot = lax.rem(i, 2)
+        load_rows(rows_in[slot], wide, xs)
+        attention(sizes, bias, vecs, wide_bias, weights, xs, work, low, qkv, mixed, middle, None)
+        second_norm(vecs, middle, work, low)
+        feed(sizes, hid_bias, vecs, weights, middle, low, work)
+        pl.when(i >= 2)(lambda: put(i - 2).wait())
+        store_rows(work, wide, rows_out.at[slot], live_scales(chunk_of(i) * BATCH, live))
+        put(i).start()
+        for at in sorted(moves):
+
+            def run(at=at):
+                for move in moves[at]:
+                    move()
+
+            pl.when(i == at)(run)
+        return 0
+
+    lax.fori_loop(0, extra, chunk, 0)
+    red.end()
+    for i in range(max(extra - 2, 0), extra):
+        put(i).wait()
+
+
+def run_rest(sizes, mesh_shape, live, tokens, held, params, gtok, dw, small):
+    d = tokens.shape[1]
     anywhere = pl.BlockSpec(memory_space=pl.ANY)
     here = pl.BlockSpec(memory_space=pltpu.VMEM)
     dma = pltpu.SemaphoreType.DMA
-    _, d, columns = dw.shape
-    split = columns // 2
-    finish = d // (2 * chips)
     return pl.pallas_call(
-        functools.partial(reduce_kernel, mesh_shape),
+        functools.partial(rest_kernel, sizes, mesh_shape),
         out_shape=(
-            jax.ShapeDtypeStruct((shards * gtok.shape[0], d), gtok.dtype),
-            jax.ShapeDtypeStruct((d, columns), BF16),
+            jax.ShapeDtypeStruct(tokens.shape, BF16),
+            jax.ShapeDtypeStruct(tokens.shape, BF16),
+            jax.ShapeDtypeStruct((d, sizes.columns), BF16),
             jax.ShapeDtypeStruct(small.shape, F32),
         ),
-        in_specs=[anywhere, here, here],
-        out_specs=(anywhere, here, here),
+        in_specs=[pl.BlockSpec(memory_space=pltpu.SMEM), anywhere, anywhere] + [here] * len(params) + [anywhere, here, here],
+        out_specs=(anywhere, anywhere, here, here),
         scratch_shapes=[
-            pltpu.VMEM((shards, d, columns), BF16),
-            pltpu.VMEM((shards, d // 2, columns), BF16),
-            pltpu.VMEM((bits, shards, d // 4, split), BF16),
-            pltpu.VMEM((bits, shards, d // 4, split), BF16),
-            pltpu.VMEM((shards, finish, split), BF16),
-            pltpu.VMEM((shards, finish, split), BF16),
-            pltpu.VMEM((bits + 2, *small.shape), F32),
-            pltpu.VMEM((bits + shards, *small.shape), F32),
-            dma((1,)),
-            dma((2, 2, shards)),
-            dma((2, shards)),
-            dma((2, 2, bits, shards)),
-            dma((2, 2, shards)),
-            dma((2, 2, chips)),
-            dma((2, 2, chips)),
-            dma((2, bits + shards)),
+            pltpu.VMEM((2, CHUNK, d), BF16),
+            pltpu.VMEM((2, CHUNK, d), BF16),
+            dma((2,)),
+            dma((2,)),
+            forward_scratch(sizes, d),
+            reduce_scratch(mesh_shape, d, sizes.columns, small.shape),
         ],
+        input_output_aliases={2: 0},
         compiler_params=pltpu.CompilerParams(collective_id=1, has_side_effects=True, vmem_limit_bytes=VMEM_LIMIT),
-    )(gtok, dw, small)
+    )(live, tokens, held, *params, gtok, dw, small)
 
 
 def relative_bias(table, offset_index):
@@ -802,11 +905,10 @@
     own = chunks // shards
     order = lax.rem(z * own + jnp.arange(chunks, dtype=jnp.int32), chunks)
     result, gtok, dw, dbias, sums, unit_sums = run_own(sizes, order[:own], group_windows, tokens, cotangent, *params)
-    result = run_forward(sizes, order[own:], group_windows, tokens, result, *params)
     grads = table_grad(dbias, offset_index, table_rows)
     grads = jnp.pad(grads, ((0, 0), (0, 384 - table_rows)))
     packed = jnp.concatenate([sums, unit_sums.reshape(-1, d), grads.reshape(-1, d)], axis=0)
-    grad_tokens, final, packed = run_reduce(mesh_shape, gtok, dw, packed)
+    result, grad_tokens, final, packed = run_rest(sizes, mesh_shape, group_windows, tokens, result, params, gtok, dw, packed)
     sums, rest = packed[:8], packed[8:]
     count = shards * units // d
     unit_total = lax.dynamic_slice_in_dim(rest[:count].reshape(-1), z * units, units)

time: 299 us -> 251 us (0.84)
  Pallas kernels: 262 us -> 207 us
  local copies, waits for them, and re-layouts: 23.2 us -> 28.3 us
    pallas_call x2 -> x1, Pallas kernels: 148 us -> 93.2 us  [run_rest(): pl.pallas_call(functools.partial(rest_kernel, sizes, mesh_shape), out_sha...]
    slice x2, local copies, waits for them, and re-layouts: 1.31 us -> 4.36 us  [local(): final[:, :3 * loc].reshape(d, 3, loc)]
    unnamed x43 -> x40, local copies, waits for them, and re-layouts: 10.2 us -> 11.8 us
where the time goes in v3:
time: 251 us; the launch traced here: 250 us
  Pallas kernels  207 us (82%)
  local copies, waits for them, and re-layouts  28.3 us (11%)
  other arithmetic  8.09 us (3%)
  matrix products  5.22 us (2%)
    pallas_call x1, Pallas kernels, run_rest(): pl.pallas_call(functools.partial(rest_kernel, sizes, mesh_shape), out_sha...  93.2 us
    pallas_call x1, Pallas kernels, run_own(): pl.pallas_call(functools.partial(own_kernel, sizes), out_shape=outs, grid...  58.4 us
    pallas_call x1, Pallas kernels, run_gather(): pl.pallas_call(functools.partial(gather_kernel, mesh_shape), out_shape=(j...  55 us
    unnamed x40, local copies, waits for them, and re-layouts  11.8 us

profile of v3, /device:TPU:0, one launch (start us, length us, event | category | flops | bytes accessed | tf_op | source)
XLA Modules:
  0.0 249.8 jit_solution(16825954908462336601)
XLA Ops:
  0.7 1.3 copy.41
  2.0 1.2 copy.40
  3.2 2.3 pad_maximum_fusion.shard
  5.5 0.6 pad_convert_fusion.small
  6.1 55.0 %shard_map.280 = (bf16[4,1536,512]{2,1,0:T(8,128)(2,1)}, f32[4,8,512]{2,1,0:T(8,128)}) custom-call(bf16[1536,512]{1,0:T(8,128)(2,1)} %pad_maximum_fusion.shard, f32[8,512]{1,0:T(8,128)} %pad_convert_fusion.small), custom_call_target="tpu_custom_call" | custom-call | tf_op jit(solution)/shard_map/pallas_call | solution.py:479
  61.2 0.8 slice.78
  62.0 0.6 fusion.10.wide_bias
  62.6 0.8 slice.114
  63.6 2.5 fusion.2
  66.5 1.0 pad_select_fusion.bias
  67.5 1.4 slice.81.hid_bias
  69.6 0.6 convert_element_type.28.vecs
  70.9 58.4 %shard_map.281 = (bf16[3200,512]{1,0:T(8,128)(2,1)}, bf16[800,512]{1,0:T(8,128)(2,1)}, bf16[4,512,1536]{2,1,0:T(8,128)(2,1)}, f32[16,104,128]{2,1,0:T(8,128)}, f32[8,512]{1,0:T(8,128)}, /*index=5*/f32[4,1,512]{2,1,0:T(1,128)}) custom-call(s32[2]{0:T(128)} %bitcast.57, s32[1]{0:T(128)S(6)} %copy.60.live, bf16[3200,512]{1,0:T(8,128)(2,1)} %tokens.1, ...), custom_call_target="tpu_custom_call" | custom-call | tf_op jit(solution)/shard_map/pallas_call | solution.py:339
  129.3 1.2 slice.113
  130.9 2.8 %fusion = f32[16,361]{1,0:T(8,128)S(1)} fusion(bf16[16,10000]{1,0:T(8,128)(2,1)S(1)} %convert_element_type.29, s32[10000]{0:T(1024)S(1)} %eq.28), kind=kOutput, calls=%fused_computation.1 | convolution fusion | flops 119130000 | bytes 383104 | tf_op jit(solution)/shard_map/dot_general | solution.py:855
  133.7 0.6 pad_maximum_fusion.1.small
  134.3 93.2 %shard_map.282 = (bf16[3200,512]{1,0:T(8,128)(2,1)}, bf16[3200,512]{1,0:T(8,128)(2,1)}, bf16[512,1536]{1,0:T(8,128)(2,1)}, f32[24,512]{1,0:T(8,128)}) custom-call(s32[1]{0:T(128)S(6)} %copy.60.live, bf16[3200,512]{1,0:T(8,128)(2,1)} %tokens.1, bf16[3200,512]{1,0:T(8,128)(2,1)} %get-tuple-element.29.held, ...), custom_call_target="tpu_custom_call", output_to_operand_aliasing={{0}: (2, {})} | custom-call | tf_op jit(solution)/shard_map/pallas_call | solution.py:822
  227.5 1.8 convert_element_type.30
  229.3 1.0 slice_bitcast_fusion
  230.3 2.5 %copy.47 = f32[512,512]{1,0:T(8,128)} copy(f32[512,512]{0,1:T(8,128)} %slice_bitcast_fusion) | data formatting | bytes 2097152
  232.9 0.8 copy.46
  233.7 2.1 slice.101
  235.8 2.3 copy.44
  238.1 2.3 copy.45
  240.4 2.1 slice.104
  242.6 0.6 dynamic-slice_bitcast_fusion
  243.2 0.7 dynamic_slice.11
  243.8 0.6 constant_dynamic-slice_fusion
  244.4 0.6 fusion.12
  245.0 1.7 copy.61
  246.7 1.4 copy-done.1
  248.1 1.7 copy.62
  (57 shorter events, 1.7 us)
Async XLA Ops:
  0.6 4.8 %copy-start.7 = (bf16[512]{0:T(512)(128)(2,1)S(1)}, bf16[512]{0:T(512)(128)(2,1)}, u32[]{:S(2)}) copy-start(bf16[512]{0:T(512)(128)(2,1)} %param.31) | copy-start | bytes 3076
  0.7 4.8 %copy-start.14 = (bf16[2,128]{1,0:T(2,128)(2,1)S(1)}, bf16[2,128]{1,0:T(2,128)(2,1)}, u32[]{:S(2)}) copy-start(bf16[2,128]{1,0:T(2,128)(2,1)} %param.24) | copy-start | bytes 1540
  0.7 4.8 %copy-start.6 = (bf16[361,4]{0,1:T(4,128)(2,1)S(1)}, bf16[361,4]{0,1:T(4,128)(2,1)}, u32[]{:S(2)}) copy-start(bf16[361,4]{0,1:T(4,128)(2,1)} %param.25) | copy-start | bytes 8668
  0.7 62.7 %copy-start.3 = (s32[100,100]{1,0:T(8,128)S(1)}, s32[100,100]{1,0:T(8,128)}, u32[]{:S(2)}) copy-start(s32[100,100]{1,0:T(8,128)} %param.20) | copy-start | bytes 120004
  63.5 6.0 %copy-start.8 = (bf16[512]{0:T(512)(128)(2,1)S(1)}, bf16[512]{0:T(512)(128)(2,1)}, u32[]{:S(2)}) copy-start(bf16[512]{0:T(512)(128)(2,1)} %param.21) | copy-start | bytes 3076
  63.5 6.0 %copy-start.9 = (bf16[512]{0:T(512)(128)(2,1)S(1)}, bf16[512]{0:T(512)(128)(2,1)}, u32[]{:S(2)}) copy-start(bf16[512]{0:T(512)(128)(2,1)} %param.22) | copy-start | bytes 3076
  63.5 6.0 %copy-start.10 = (bf16[512]{0:T(512)(128)(2,1)S(1)}, bf16[512]{0:T(512)(128)(2,1)}, u32[]{:S(2)}) copy-start(bf16[512]{0:T(512)(128)(2,1)} %param.27) | copy-start | bytes 3076
  63.5 6.0 %copy-start.11 = (bf16[512]{0:T(512)(128)(2,1)S(1)}, bf16[512]{0:T(512)(128)(2,1)}, u32[]{:S(2)}) copy-start(bf16[512]{0:T(512)(128)(2,1)} %param.28) | copy-start | bytes 3076
  63.5 6.0 %copy-start.12 = (bf16[512]{0:T(512)(128)(2,1)S(1)}, bf16[512]{0:T(512)(128)(2,1)}, u32[]{:S(2)}) copy-start(bf16[512]{0:T(512)(128)(2,1)} %param.29) | copy-start | bytes 3076
  63.6 6.0 %copy-start.13 = (bf16[512]{0:T(512)(128)(2,1)S(1)}, bf16[512]{0:T(512)(128)(2,1)}, u32[]{:S(2)}) copy-start(bf16[512]{0:T(512)(128)(2,1)} %param.33) | copy-start | bytes 3076
  129.3 4.4 %copy-start.5 = (f32[4,1,512]{2,1,0:T(1,128)S(1)}, f32[4,1,512]{2,1,0:T(1,128)}, u32[]{:S(2)}) copy-start(f32[4,1,512]{2,1,0:T(1,128)} %get-tuple-element.33) | copy-start | bytes 24580
  129.3 4.4 %copy-start.4 = (f32[8,512]{1,0:T(8,128)S(1)}, f32[8,512]{1,0:T(8,128)}, u32[]{:S(2)}) copy-start(f32[8,512]{1,0:T(8,128)} %get-tuple-element.32) | copy-start | bytes 49156
  233.7 8.8 %copy-start.2 = (f32[24,512]{1,0:T(8,128)S(1)}, f32[24,512]{1,0:T(8,128)}, u32[]{:S(2)}) copy-start(f32[24,512]{1,0:T(8,128)} %get-tuple-element.37) | copy-start | bytes 147460
  233.7 11.3 %copy-start = (bf16[3200,512]{1,0:T(8,128)(2,1)S(1)}, bf16[3200,512]{1,0:T(8,128)(2,1)}, u32[]{:S(2)}) copy-start(bf16[3200,512]{1,0:T(8,128)(2,1)} %get-tuple-element.92) | copy-start | bytes 9830404
  245.0 3.1 %copy-start.1 = (bf16[3200,512]{1,0:T(8,128)(2,1)S(1)}, bf16[3200,512]{1,0:T(8,128)(2,1)}, u32[]{:S(2)}) copy-start(bf16[3200,512]{1,0:T(8,128)(2,1)} %get-tuple-element.93) | copy-start | bytes 9830404

commit v4 on v3

v4 whole, which is shorter than its diff:
```python
import functools
import math
import jax
import jax.numpy as jnp
from jax import lax
from jax.experimental import pallas as pl
from jax.experimental.pallas import tpu as pltpu
from jax.sharding import PartitionSpec as P

AREA = 100
PAD = 104
HEAD = 32
LANES = 128
PACK = LANES // HEAD
BATCH = 4
CHUNK = BATCH * AREA
ROWS = BATCH * PAD
EPSILON = 1e-05
DENSITY = 0.3989422804014327
LOG2E = 1.4426950408889634
F32 = jnp.float32
BF16 = jnp.bfloat16
MESH = pl.DeviceIdType.MESH
VMEM_LIMIT = 63 * 2**20


def dot(a, b):
    return jnp.dot(a, b, preferred_element_type=F32)


def dot_nt(a, b):
    return lax.dot_general(a, b, (((1,), (1,)), ((), ())), preferred_element_type=F32)


def dot_tn(a, b):
    return lax.dot_general(a, b, (((0,), (0,)), ((), ())), preferred_element_type=F32)


def normalize(values):
    centered = values - jnp.mean(values, axis=-1, keepdims=True)
    inv = lax.rsqrt(jnp.mean(centered * centered, axis=-1, keepdims=True) + EPSILON)
    return centered * inv, inv


def norm_back(grad, hat, inv):
    return inv * (
        grad
        - jnp.mean(grad, axis=-1, keepdims=True)
        - hat * jnp.mean(grad * hat, axis=-1, keepdims=True)
    )


def normal_cdf(hidden):
    z = jnp.abs(hidden) * 0.7071067811865476
    t = 1.0 / (1.0 + 0.3275911 * z)
    poly = t * (
        0.127414796 + t * (-0.142248368 + t * (0.7107068705 + t * (-0.7265760135 + t * 0.5307027145)))
    )
    bell = jnp.exp2(hidden * hidden * (-0.5 * LOG2E))
    tail = poly * bell
    return jnp.where(hidden > 0.0, 1.0 - tail, tail), bell


def head_of(shape, axis):
    return lax.broadcasted_iota(jnp.int32, shape, axis) // HEAD


def pad_rows(v):
    return jnp.concatenate([v, jnp.zeros((LANES - PAD, v.shape[1]), v.dtype)], axis=0)


def spread_rows(v):
    head = head_of((LANES, LANES), 1)
    full = pad_rows(v)
    return jnp.concatenate([jnp.where(head == h, full, 0.0) for h in range(PACK)], axis=0).astype(BF16)


def spread_columns(v):
    head = head_of((LANES, LANES), 0)
    turned = pad_rows(v).T
    return jnp.concatenate([jnp.where(head == h, turned, 0.0) for h in range(PACK)], axis=1).astype(BF16)


def diagonal(full):
    head = head_of((LANES, LANES), 0)
    out = full[:, 0:LANES]
    for h in range(1, PACK):
        out = jnp.where(head == h, full[:, h * LANES : (h + 1) * LANES], out)
    return out


def span(w, size=PAD):
    return pl.ds(pl.multiple_of(w * PAD, 8), size)


def load_rows(source, wide, padded):
    wide[...] = source.astype(F32)
    for w in range(BATCH):
        padded[w * PAD : w * PAD + AREA, :] = wide[w * AREA : (w + 1) * AREA, :]


def store_rows(padded, wide, target, scales=None):
    for w in range(BATCH):
        rows = padded[w * PAD : w * PAD + AREA, :]
        wide[w * AREA : (w + 1) * AREA, :] = rows if scales is None else rows * scales[w]
    target[...] = wide[...].astype(BF16)


class Sizes:
    def __init__(self, shards, loc, units):
        self.shards, self.loc, self.units = shards, loc, units
        self.width = shards * loc
        self.groups = self.width // LANES
        self.columns = 4 * loc + 2 * units

    def attention_part(self, weights, c):
        at = slice(c * self.loc, (c + 1) * self.loc)
        return jnp.concatenate([weights[z, at, :] for z in range(self.shards)], axis=0)

    def expand_part(self, weights, i):
        return weights[i, pl.ds(4 * self.loc, self.units), :]

    def shrink_part(self, weights, i):
        return weights[i, pl.ds(4 * self.loc + self.units, self.units), :]

    def add_attention(self, dw, c, value):
        for z in range(self.shards):
            at = slice(c * self.loc, (c + 1) * self.loc)
            dw[z, :, at] += value[:, z * self.loc : (z + 1) * self.loc]


def attention(sizes, bias, vecs, wide_bias, weights, xs, work, low, qkv, mixed, middle, keep, between=None):
    width, groups = sizes.width, sizes.groups
    scale = HEAD ** (-0.5) * LOG2E
    for w in range(BATCH):
        hat, _ = normalize(xs[span(w), :])
        work[span(w), :] = hat * vecs[0:1, :] + vecs[1:2, :]
    low[...] = work[...].astype(BF16)
    for c in range(3):
        at = slice(c * width, (c + 1) * width)
        qkv[:, at] = dot_nt(low[...], sizes.attention_part(weights, c)) + wide_bias[:, at]

    if between is not None:
        between()

    def attend(w, _):
        row = span(w)
        for g in range(groups):
            col = g * LANES
            q = qkv[row, pl.ds(col, LANES)].astype(BF16)
            k = qkv[row, pl.ds(width + col, LANES)]
            v = qkv[row, pl.ds(2 * width + col, LANES)]
            scores = dot(q, spread_columns(k))
            parts = []
            for h in range(PACK):
                s = scores[:, h * LANES : (h + 1) * LANES] * scale + bias[g * PACK + h]
                e = jnp.exp2(s - jnp.max(s, axis=-1, keepdims=True))
                parts.append(e * (1.0 / jnp.sum(e, axis=-1, keepdims=True)))
            probs = jnp.concatenate(parts, axis=1).astype(BF16)
            if keep is not None:
                keep[w * groups + g] = probs
            mixed[row, pl.ds(col, LANES)] = dot(probs, spread_rows(v))
        return 0

    lax.fori_loop(0, BATCH, attend, 0)
    middle[...] = xs[...] + dot(mixed[...].astype(BF16), sizes.attention_part(weights, 3)) + vecs[2:3, :]


def second_norm(vecs, middle, work, low):
    for w in range(BATCH):
        hat, _ = normalize(middle[span(w), :])
        work[span(w), :] = hat * vecs[3:4, :] + vecs[4:5, :]
    low[...] = work[...].astype(BF16)


def feed(sizes, hid_bias, vecs, weights, middle, low, acc):
    acc[...] = middle[...] + vecs[5:6, :]

    def block(i, _):
        hidden = dot_nt(low[...], sizes.expand_part(weights, i)) + hid_bias[i, 0:1, 0 : sizes.units]
        cdf, _ = normal_cdf(hidden)
        acc[...] += dot((hidden * cdf).astype(BF16), sizes.shrink_part(weights, i))
        return 0

    lax.fori_loop(0, sizes.shards, block, 0, unroll=4)


def column_sum(v):
    return jnp.sum(v, axis=0, keepdims=True)


def feed_both(sizes, hid_bias, vecs, weights, middle, low, glow, acc, back, dw, unit_sums):
    base, units = 4 * sizes.loc, sizes.units
    acc[...] = middle[...] + vecs[5:6, :]
    back[...] = jnp.zeros_like(back)

    def block(i, _):
        w_in, w_out = sizes.expand_part(weights, i), sizes.shrink_part(weights, i)
        hidden = dot_nt(low[...], w_in) + hid_bias[i, 0:1, 0 : sizes.units]
        cdf, bell = normal_cdf(hidden)
        active = (hidden * cdf).astype(BF16)
        grad = (dot_nt(glow[...], w_out) * (cdf + hidden * bell * DENSITY))
        unit_sums[i] += column_sum(grad)
        grad = grad.astype(BF16)
        acc[...] += dot(active, w_out)
        back[...] += dot(grad, w_in)
        dw[i, :, base : base + units] += dot_tn(low[...], grad)
        dw[i, :, base + units : base + 2 * units] += dot_tn(glow[...], active)
        return 0

    lax.fori_loop(0, sizes.shards, block, 0, unroll=2)


def backward(sizes, vecs, weights, xs, work, low, qkv, mixed, middle, glow, back, gmid, keep, dw, dbias, sums, between):
    width, groups = sizes.width, sizes.groups
    scale = HEAD ** (-0.5)
    gmix, dqkv = work, qkv
    for w in range(BATCH):
        hat, inv = normalize(middle[span(w), :])
        grad = back[span(w), :]
        sums[3:4, :] += column_sum(grad * hat)
        sums[4:5, :] += column_sum(grad)
        gmid[span(w), :] += norm_back(grad * vecs[3:4, :], hat, inv)
    branch = gmid[...].astype(BF16)
    sums[5:6, :] += column_sum(gmid[...])
    sizes.add_attention(dw, 3, dot_tn(branch, mixed[...].astype(BF16)))
    gmix[...] = dot_nt(branch, sizes.attention_part(weights, 3))
    between()

    def attend(w, _):
        row = span(w)
        for g in range(groups):
            col = g * LANES
            q = qkv[row, pl.ds(col, LANES)]
            k = qkv[row, pl.ds(width + col, LANES)]
            v = qkv[row, pl.ds(2 * width + col, LANES)]
            grad = gmix[row, pl.ds(col, LANES)]
            probs = keep[w * groups + g]
            wide_grad = dot(grad.astype(BF16), spread_columns(v))
            parts = []
            for h in range(PACK):
                p = probs[:, h * LANES : (h + 1) * LANES].astype(F32)
                t = wide_grad[:, h * LANES : (h + 1) * LANES]
                s = p * (t - jnp.sum(p * t, axis=-1, keepdims=True))
                dbias[g * PACK + h] += s
                parts.append(s)
            score = jnp.concatenate(parts, axis=1).astype(BF16)
            turned = pad_rows(q).T[:, :PAD].astype(BF16)
            dqkv[row, pl.ds(col, LANES)] = dot(score, spread_rows(k)) * scale
            dqkv[row, pl.ds(width + col, LANES)] = diagonal(dot(turned, score)).T[:PAD] * scale
            turned = pad_rows(grad).T[:, :PAD].astype(BF16)
            dqkv[row, pl.ds(2 * width + col, LANES)] = diagonal(dot(turned, probs)).T[:PAD]
        return 0

    lax.fori_loop(0, BATCH, attend, 0)
    for w in range(BATCH):
        hat, _ = normalize(xs[span(w), :])
        work[span(w), :] = hat * vecs[0:1, :] + vecs[1:2, :]
    low[...] = work[...].astype(BF16)
    back[...] = jnp.zeros_like(back)
    for c in range(3):
        at = slice(c * width, (c + 1) * width)
        grad = dqkv[:, at]
        if c != 1:
            sums[c // 2 : c // 2 + 1, :] += column_sum(grad)
        grad = grad.astype(BF16)
        back[...] += dot(grad, sizes.attention_part(weights, c))
        sizes.add_attention(dw, c, dot_tn(low[...], grad))
    for w in range(BATCH):
        hat, inv = normalize(xs[span(w), :])
        grad = back[span(w), :]
        sums[6:7, :] += column_sum(grad * hat)
        sums[7:8, :] += column_sum(grad)
        gmid[span(w), :] += norm_back(grad * vecs[0:1, :], hat, inv)


def live_scales(first, live):
    return [jnp.where(first + w < live[0], 1.0, 0.0).astype(F32) for w in range(BATCH)]


class Place:
    def __init__(self, mesh_shape):
        self.shards, self.n_dp = mesh_shape["mp"], mesh_shape["dp"]
        self.chips = self.n_dp // 2
        self.bits = int(math.log2(self.chips))
        self.dp, self.z = lax.axis_index("dp"), lax.axis_index("mp")
        self.core, self.chip = lax.rem(self.dp, 2), lax.div(self.dp, 2)

    def mate(self):
        return (self.dp + 1 - 2 * self.core, self.z)

    def flip(self, m):
        chip = self.chip
        for b in range(self.bits):
            if m >> b & 1:
                chip = chip + (1 << b) * (1 - 2 * lax.rem(lax.div(self.chip, 1 << b), 2))
        return chip

    def across(self, m):
        return (2 * self.flip(m) + self.core, self.z)

    def bit(self, b):
        return lax.rem(lax.div(self.chip, 1 << b), 2)

    def along(self, k):
        return (self.dp, lax.rem(self.z + k, self.shards))

    def greet(self, targets):
        barrier = pltpu.get_barrier_semaphore()
        for target in targets:
            pl.semaphore_signal(barrier, inc=1, device_id=target, device_id_type=MESH)
        pl.semaphore_wait(barrier, len(targets))

    def everyone(self):
        return (
            [self.mate()]
            + [self.across(m) for m in range(1, self.chips)]
            + [self.along(k) for k in range(1, self.shards)]
        )


def remote(source, target, sent, received, device):
    return pltpu.make_async_remote_copy(source, target, sent, received, device_id=device, device_id_type=MESH)


class Sends:
    def __init__(self):
        self.sent = []

    def send(self, make, when=None):
        self.sent.append((make, when))
        if when is None:
            make().start()
        else:
            pl.when(when())(lambda: make().start())

    def finish(self):
        for make, when in self.sent:
            if when is None:
                make().wait_send()
            else:
                pl.when(when())(lambda make=make: make().wait_send())


class Gather:
    def __init__(self, here, sends, out, parts, small, scratch):
        self.here, self.sends, self.out, self.parts, self.small = here, sends, out, parts, small
        self.z_sem, self.s_sem, self.p_sem, self.m_sem = scratch
        self.order = sorted(range(1, here.shards), key=lambda k: min(k, here.shards - k))

    def spot(self, part, shard, dp):
        first, rows = self.parts[part]
        rows //= self.here.n_dp
        return self.out.at[shard, pl.ds(pl.multiple_of(first + dp * rows, 16), rows)]

    def origin(self, k):
        return lax.rem(self.here.z - k + self.here.shards, self.here.shards)

    def along(self, part, k, arriving=False):
        here = self.here
        spot = self.spot(part, self.origin(k) if arriving else here.z, here.dp)
        return remote(spot, spot, self.z_sem.at[0, part, k], self.z_sem.at[1, part, k], here.along(k))

    def small_along(self, k, arriving=False):
        spot = self.small.at[self.origin(k) if arriving else self.here.z]
        return remote(spot, spot, self.s_sem.at[0, k], self.s_sem.at[1, k], self.here.along(k))

    def start(self):
        for k in self.order:
            self.sends.send(functools.partial(self.small_along, k))
        self.start_part(0)

    def start_part(self, part):
        for k in self.order:
            self.sends.send(functools.partial(self.along, part, k))

    def across(self, part, k, m, arriving=False):
        here = self.here
        spot = self.spot(part, self.origin(k), 2 * here.flip(m if arriving else 0) + here.core)
        return remote(spot, spot, self.p_sem.at[0, part, k, m], self.p_sem.at[1, part, k, m], here.across(m))

    def mate(self, part, k, m, arriving=False):
        here = self.here
        spot = self.spot(part, self.origin(k), 2 * here.flip(m) + (1 - here.core if arriving else here.core))
        return remote(spot, spot, self.m_sem.at[0, part, k, m], self.m_sem.at[1, part, k, m], here.mate())

    def spread(self, part):
        for k in self.order:
            self.along(part, k, True).wait_recv()
            for m in range(1, self.here.chips):
                self.sends.send(functools.partial(self.across, part, k, m))
            self.sends.send(functools.partial(self.mate, part, k, 0))

    def relay(self, part):
        for k in self.order:
            for m in range(1, self.here.chips):
                self.across(part, k, m, True).wait_recv()
                self.sends.send(functools.partial(self.mate, part, k, m))

    def wait(self, part):
        for k in self.order:
            for m in range(self.here.chips):
                self.mate(part, k, m, True).wait_recv()

    def wait_small(self):
        for k in self.order:
            self.small_along(k, True).wait_recv()


def gather_scratch(mesh_shape, parts):
    shards, chips = mesh_shape["mp"], mesh_shape["dp"] // 2
    dma = pltpu.SemaphoreType.DMA
    return [dma((2, parts, shards)), dma((2, shards)), dma((2, parts, shards, chips)), dma((2, parts, shards, chips))]


class Lines:
    def __init__(self, here, sends, source, target, sem, reach):
        self.here, self.sends, self.source, self.target, self.sem, self.reach = here, sends, source, target, sem, reach

    def block(self, z, c):
        chunks = self.source.shape[0]
        return self.target.at[pl.ds(pl.multiple_of((z * chunks + c) * CHUNK, 16), CHUNK)]

    def local(self, c):
        return pltpu.make_async_copy(self.source.at[c], self.block(self.here.z, c), self.sem.at[0, c, 0, self.reach])

    def copy(self, c, way, step, reach, arriving=False):
        here, sign = self.here, 1 - 2 * way
        held = jnp.clip(here.z - sign * step, 0, here.shards - 1)
        at = step - 1 if arriving else step + reach - 1
        source = self.source.at[c] if step == 0 else self.block(held, c)
        target = (here.dp, jnp.clip(here.z + sign * reach, 0, here.shards - 1))
        return remote(source, self.block(held, c), self.sem.at[0, c, way, at], self.sem.at[1, c, way, at], target)

    def there(self, way, step, reach):
        here, sign = self.here, 1 - 2 * way
        held, onward = here.z - sign * step, here.z + sign * reach
        return (held >= 0) & (held < here.shards) & (onward >= 0) & (onward < here.shards)

    def send(self, c, step, reach):
        for way in range(2):
            self.sends.send(
                functools.partial(self.copy, c, way, step, reach), functools.partial(self.there, way, step, reach)
            )

    def start(self, c):
        for reach in range(1, min(2, self.reach) + 1):
            self.send(c, 0, reach)

    def arrive(self, c, step):
        for way in range(2):
            pl.when(self.there(way, step, 0))(lambda way=way: self.copy(c, way, step, 1, True).wait_recv())

    def forward(self, c, step):
        self.arrive(c, step)
        self.send(c, step, 1)


class Reduction:
    def __init__(self, here, sends, dw, final, span, scratch):
        (self.acc, self.half, self.parts, self.lasts, self.h_sem, self.q_sem, self.l_sem, self.f_sem, self.g_sem) = scratch
        self.dw, self.final, self.here, self.sends = dw, final, here, sends
        self.d = dw.shape[1]
        self.first, self.columns = span
        split = self.columns // 2
        self.sides = (pl.ds(0, split), pl.ds(split, split))
        self.orders = (tuple(range(here.bits)), tuple(reversed(range(here.bits))))

    def send(self, make):
        self.sends.send(make)

    def rows_of(self, side, core, chip_bit, depth):
        size = self.d // 2
        first = core * size
        for b in self.orders[side][:depth]:
            size //= 2
            first = first + chip_bit(b) * size
        return pl.ds(pl.multiple_of(first, 16), size)

    def half_rows(self, core):
        return pl.ds(pl.multiple_of(core * (self.d // 2), 16), self.d // 2)

    def half_copy(self, s):
        rows = self.half_rows(1 - self.here.core)
        return remote(self.acc.at[s, rows], self.half.at[s], self.h_sem.at[0, s], self.h_sem.at[1, s], self.here.mate())

    def half_send(self, s):
        rows = self.half_rows(1 - self.here.core)
        self.acc[s, rows, :] = self.dw[s, rows, pl.ds(self.first, self.columns)].astype(BF16)
        self.send(functools.partial(self.half_copy, s))

    def half_add(self, s):
        self.half_copy(s).wait_recv()
        mine = self.half_rows(self.here.core)
        self.acc[s, mine, :] = (self.dw[s, mine, pl.ds(self.first, self.columns)] + self.half[s].astype(F32)).astype(BF16)

    def plane_copy(self, s, depth, side):
        here = self.here
        b = self.orders[side][depth]
        rows = self.rows_of(side, here.core, lambda c: 1 - here.bit(c) if c == b else here.bit(c), depth + 1)
        target = self.parts[side][depth].at[s]
        sems = self.q_sem
        return remote(
            self.acc.at[s, rows, self.sides[side]], target, sems.at[0, side, depth, s], sems.at[1, side, depth, s], here.across(1 << b)
        )

    def plane_send(self, s, depth):
        for side in range(2):
            self.send(functools.partial(self.plane_copy, s, depth, side))

    def plane_add(self, s, depth):
        for side in range(2):
            self.plane_copy(s, depth, side).wait_recv()
            rows = self.rows_of(side, self.here.core, self.here.bit, depth + 1)
            arrived = self.parts[side][depth][s]
            here = self.acc[s, rows, self.sides[side]]
            self.acc[s, rows, self.sides[side]] = (here.astype(F32) + arrived.astype(F32)).astype(BF16)

    def mine(self, side):
        return self.rows_of(side, self.here.core, self.here.bit, self.here.bits)

    def shard_copy(self, side, k):
        here = self.here
        s = lax.rem(here.z + k, here.shards)
        return remote(
            self.acc.at[s, self.mine(side), self.sides[side]], self.lasts[side].at[k], self.l_sem.at[0, side, k], self.l_sem.at[1, side, k], here.along(k)
        )

    def shard_sends(self):
        for k in range(1, self.here.shards):
            for side in range(2):
                self.send(functools.partial(self.shard_copy, side, k))

    def shard_adds(self):
        for side in range(2):
            rows = self.mine(side)
            total = self.acc[self.here.z, rows, self.sides[side]].astype(F32)
            for k in range(1, self.here.shards):
                self.shard_copy(side, k).wait_recv()
                total = total + self.lasts[side][k].astype(F32)
            self.final[rows, self.final_side(side)] = total.astype(BF16)

    def final_side(self, side):
        split = self.columns // 2
        return pl.ds(self.first + side * split, split)

    def final_spot(self, side, m, core):
        here = self.here
        rows = self.rows_of(side, core, lambda b: 1 - here.bit(b) if m >> b & 1 else here.bit(b), here.bits)
        return self.final.at[rows, self.final_side(side)]

    def final_copy(self, side, m, arriving=False):
        here = self.here
        spot = self.final_spot(side, m if arriving else 0, here.core)
        return remote(spot, spot, self.f_sem.at[0, side, m], self.f_sem.at[1, side, m], here.across(m))

    def final_relay(self, side, m, arriving=False):
        here = self.here
        spot = self.final_spot(side, m, 1 - here.core if arriving else here.core)
        return remote(spot, spot, self.g_sem.at[0, side, m], self.g_sem.at[1, side, m], here.mate())

    def final_spread(self):
        for side in range(2):
            for m in range(1, self.here.chips):
                self.send(functools.partial(self.final_copy, side, m))
            self.send(functools.partial(self.final_relay, side, 0))

    def final_relays(self):
        for side in range(2):
            for m in range(1, self.here.chips):
                self.final_copy(side, m, True).wait_recv()
                self.send(functools.partial(self.final_relay, side, m))

    def final_wait(self):
        for side in range(2):
            for m in range(self.here.chips):
                self.final_relay(side, m, True).wait_recv()

    def start(self):
        for s in range(self.here.shards):
            self.half_send(s)

    def plane(self, depth):
        for s in range(self.here.shards):
            if depth == 0:
                self.half_add(s)
            else:
                self.plane_add(s, depth - 1)
            if depth < self.here.bits:
                self.plane_send(s, depth)
        if depth == self.here.bits:
            self.shard_sends()

    def close(self):
        self.shard_adds()
        self.final_spread()


def reduce_scratch(mesh_shape, d, columns):
    shards, chips = mesh_shape["mp"], mesh_shape["dp"] // 2
    bits = int(math.log2(chips))
    split, finish = columns // 2, d // (2 * chips)
    dma = pltpu.SemaphoreType.DMA
    return [
        pltpu.VMEM((shards, d, columns), BF16),
        pltpu.VMEM((shards, d // 2, columns), BF16),
        [[pltpu.VMEM((shards, d >> (depth + 2), split), BF16) for depth in range(bits)]] * 2,
        [pltpu.VMEM((shards, finish, split), BF16)] * 2,
        dma((2, shards)),
        dma((2, 2, bits, shards)),
        dma((2, 2, shards)),
        dma((2, 2, chips)),
        dma((2, 2, chips)),
    ]


class Totals:
    def __init__(self, here, sends, out, scratch):
        self.here, self.sends, self.small_out = here, sends, out
        self.sums, self.sums_in, self.t_sem = scratch
        self.stages = here.bits + 1

    def send(self, make):
        self.sends.send(make)

    def small_copy(self, i):
        here = self.here
        target = here.mate() if i == 0 else here.across(1 << (i - 1))
        return remote(self.sums.at[i], self.sums_in.at[i], self.t_sem.at[0, i], self.t_sem.at[1, i], target)

    def small_send(self, i):
        self.send(functools.partial(self.small_copy, i))

    def small_add(self, i):
        self.small_copy(i).wait_recv()
        self.sums[i + 1] = self.sums[i] + self.sums_in[i]

    def small_along(self, k):
        slot = self.stages + k - 1
        return remote(
            self.sums.at[self.stages], self.sums_in.at[slot], self.t_sem.at[0, slot], self.t_sem.at[1, slot], self.here.along(k)
        )

    def small_sends(self):
        for k in range(1, self.here.shards):
            self.send(functools.partial(self.small_along, k))

    def small_total(self):
        total = self.sums[self.stages]
        for k in range(1, self.here.shards):
            self.small_along(k).wait_recv()
            total = total + self.sums_in[self.stages + k - 1]
        self.small_out[...] = total


def totals_scratch(mesh_shape, shape):
    shards, chips = mesh_shape["mp"], mesh_shape["dp"] // 2
    bits = int(math.log2(chips))
    return [
        pltpu.VMEM((bits + 2, *shape), F32),
        pltpu.VMEM((bits + shards, *shape), F32),
        pltpu.SemaphoreType.DMA((2, bits + shards)),
    ]


TALL = 384
BLOCK = 8


def one_hot(index_row):
    return (lax.broadcasted_iota(jnp.int32, (TALL, LANES), 0) == index_row).astype(F32).astype(BF16)


def build_bias(index, table, bias):
    heads = table.shape[0]
    tall = jnp.broadcast_to(table[:, None, :], (heads, BLOCK, TALL)).reshape(heads * BLOCK, TALL).astype(BF16)
    row = lax.rem(lax.broadcasted_iota(jnp.int32, (heads * BLOCK, LANES), 0), BLOCK)
    blocked = jnp.where(lax.broadcasted_iota(jnp.int32, (heads * BLOCK, LANES), 1) < AREA, 0.0, -1e30)

    def block(r, _):
        at = pl.ds(pl.multiple_of(r * BLOCK, BLOCK), BLOCK)
        rows = index[at, :]
        out = blocked
        for i in range(BLOCK):
            values = dot(tall, one_hot(rows[i : i + 1, :]))
            out = jnp.where(row == i, values * LOG2E + blocked, out)
        bias[:, at, :] = out.reshape(heads, BLOCK, LANES)
        return 0

    lax.fori_loop(0, PAD // BLOCK, block, 0)


def sum_table(index, dbias, turned):
    heads = dbias.shape[0]
    row = lax.rem(lax.broadcasted_iota(jnp.int32, (heads * BLOCK, LANES), 0), BLOCK)
    turned[...] = jnp.zeros_like(turned)

    def block(r, _):
        at = pl.ds(pl.multiple_of(r * BLOCK, BLOCK), BLOCK)
        rows = index[at, :]
        values = dbias[:, at, :].reshape(heads * BLOCK, LANES)
        left = jnp.concatenate([one_hot(rows[i : i + 1, :]) for i in range(BLOCK)], axis=1)
        right = jnp.concatenate([jnp.where(row == i, values, 0.0) for i in range(BLOCK)], axis=1).astype(BF16)
        turned[...] += dot_nt(left, right)
        return 0

    lax.fori_loop(0, PAD // BLOCK, block, 0)


def block_kernel(sizes, mesh_shape, exchange, live, index, vecs, tokens, cotangent, shard, small,
                 result, gtok, final, small_out,
                 weights, smalls, wide_bias, bias, dbias, dw, xs, qkv, mixed, middle, keep,
                 wide, work, low, glow, back, gmid, sums, unit_sums, turned,
                 tok_in, cot_in, rows_in, rows_out,
                 own_sem, tok_sem, cot_sem, in_sem, out_sem, result_sem, gtok_sem,
                 gather_refs, feed_refs, attn_refs, total_refs):
    here = Place(mesh_shape)
    sends = Sends()
    own_out, own_grad = tok_in, cot_in
    shards, own = sizes.shards, tok_in.shape[0]
    chunks = shards * own
    loc, units = sizes.loc, sizes.units
    gather = Gather(here, sends, weights, ((0, 4 * loc), (4 * loc, 2 * units)), smalls, gather_refs)
    feed_sum = Reduction(here, sends, dw, final, (4 * loc, 2 * units), feed_refs)
    attn_sum = Reduction(here, sends, dw, final, (0, 4 * loc), attn_refs)
    totals = Totals(here, sends, small_out, total_refs)
    results = Lines(here, sends, own_out, result, result_sem, 1)
    grads = Lines(here, sends, own_grad, gtok, gtok_sem, shards - 1)

    def own_rows(c):
        return pl.ds(pl.multiple_of((here.z * own + c) * CHUNK, 16), CHUNK)

    def own_tokens(c):
        return pltpu.make_async_copy(tokens.at[own_rows(c)], tok_in.at[c], tok_sem.at[c])

    def own_cotangent(c):
        return pltpu.make_async_copy(cotangent.at[own_rows(c)], cot_in.at[c], cot_sem.at[c])

    mine = [
        pltpu.make_async_copy(shard, weights.at[here.z], own_sem.at[0]),
        pltpu.make_async_copy(small, smalls.at[here.z], own_sem.at[1]),
    ]
    for copy in mine:
        copy.start()
    for c in range(own):
        own_tokens(c).start()
    for c in range(own):
        own_cotangent(c).start()
    here.greet(here.everyone())
    for copy in mine:
        copy.wait()
    gather.start()
    xs[...] = jnp.zeros_like(xs)
    dbias[...] = jnp.zeros_like(dbias)
    sums[...] = jnp.zeros_like(sums)
    unit_sums[...] = jnp.zeros_like(unit_sums)
    gather.wait_small()
    heads = sizes.width // HEAD
    count = heads // shards
    for z in range(shards):
        at = slice(z * loc, (z + 1) * loc)
        wide_bias[:, at] = smalls[z, 1:2, 0:loc]
        wide_bias[:, slice(2 * sizes.width + z * loc, 2 * sizes.width + (z + 1) * loc)] = smalls[z, 1:2, loc : 2 * loc]
    wide_bias[:, sizes.width : 2 * sizes.width] = jnp.zeros((1, sizes.width), F32)
    gather.spread(0)
    gather.start_part(1)
    table = jnp.concatenate([smalls[z, 2 : 2 + count, 0:TALL] for z in range(shards)], axis=0)
    build_bias(index, table, bias)
    gather.relay(0)

    def clear(z, _):
        dw[z] = jnp.zeros_like(dw[z])
        return 0

    lax.fori_loop(0, shards, clear, 0)
    gather.wait(0)

    def attend(c, _):
        own_tokens(c).wait()
        load_rows(tok_in[c], wide, xs.at[c])

        def between():
            pl.when(c == 0)(lambda: gather.spread(1))

        attention(sizes, bias, vecs, wide_bias, weights, xs.at[c], work, low, qkv.at[c], mixed.at[c], middle.at[c], keep.at[c], between)
        pl.when(c == 0)(lambda: gather.relay(1))
        return 0

    lax.fori_loop(0, own, attend, 0)
    gather.wait(1)

    def finish(c, _):
        scales = live_scales((here.z * own + c) * BATCH, live)
        own_cotangent(c).wait()
        second_norm(vecs, middle.at[c], work, low)
        wide[...] = cot_in[c].astype(F32)
        for w in range(BATCH):
            gmid[w * PAD : w * PAD + AREA, :] = wide[w * AREA : (w + 1) * AREA, :] * scales[w]
            gmid[w * PAD + AREA : (w + 1) * PAD, :] = jnp.zeros((PAD - AREA, gmid.shape[1]), F32)
        sums[2:3, :] += column_sum(gmid[...])
        glow[...] = gmid[...].astype(BF16)
        feed_both(sizes, smalls, vecs, weights, middle.at[c], low, glow, work, back, dw, unit_sums)
        store_rows(work, wide, own_out.at[c], scales)
        for i in range(own):

            def fed(i=i):
                results.local(i).start()
                if i < exchange:
                    results.start(i)
                if i == own - 1:
                    feed_sum.start()

            pl.when(c == i)(fed)

        def between():
            pl.when(c == own - 1)(lambda: feed_sum.plane(0))

        backward(sizes, vecs, weights, xs.at[c], work, low, qkv.at[c], mixed.at[c], middle.at[c], glow, back, gmid, keep.at[c], dw, dbias, sums, between)
        store_rows(gmid, wide, own_grad.at[c])
        for i in range(own):

            def done(i=i):
                grads.local(i).start()
                grads.start(i)

            pl.when(c == i)(done)
        return 0

    lax.fori_loop(0, own, finish, 0)
    attn_sum.start()
    sum_table(index, dbias, turned)
    table = turned[...].T
    total = totals.sums
    total[0, 0:8, :] = sums[...]
    for z in range(shards):
        at = z * units % sizes.width
        line = 8 + z * units // sizes.width
        total[0, line : line + 1, at : at + units] = unit_sums[z]
    base = 8 + shards * units // sizes.width
    total[0, base : base + heads, 0:TALL] = jnp.sum(table.reshape(heads, BLOCK, TALL), axis=1)
    totals.small_send(0)

    extra = chunks - own
    before = jnp.int32(0)
    if exchange == own:
        before = jnp.maximum(here.z - 1, 0) * own
        after = jnp.maximum(shards - 2 - here.z, 0) * own
        extras, most = before + after, extra - own

        def chunk_of(i):
            return jnp.where(i < before, i, i - before + (here.z + 2) * own)
    else:
        extras, most = jnp.int32(extra), extra

        def chunk_of(i):
            return lax.rem((here.z + 1) * own + i, chunks)

    def rows(i):
        return pl.ds(pl.multiple_of(chunk_of(i) * CHUNK, 16), CHUNK)

    def fetch(i):
        return pltpu.make_async_copy(tokens.at[rows(i)], rows_in.at[lax.rem(i, 2)], in_sem.at[lax.rem(i, 2)])

    def put(i):
        return pltpu.make_async_copy(rows_out.at[lax.rem(i, 2)], result.at[rows(i)], out_sem.at[lax.rem(i, 2)])

    pl.when(extras > 0)(lambda: fetch(0).start())
    bits = here.bits
    points = 2 * most
    moves = {p: [] for p in range(points + 1)}

    def place(p, step):
        moves[max(0, min(p, points))].append(step)

    place(0, functools.partial(attn_sum.plane, 0))
    for depth in range(1, bits + 1):
        place(2 * depth - 1, functools.partial(feed_sum.plane, depth))
        place(2 * depth, functools.partial(attn_sum.plane, depth))
    for i in range(totals.stages):

        def small_step(i=i):
            totals.small_add(i)
            if i + 1 < totals.stages:
                totals.small_send(i + 1)
            else:
                totals.small_sends()

        place(2 * i + 1, small_step)
    for c in range(own):
        for n in range(2, shards - 1):
            place(2 * n - 2 + 6 * c, functools.partial(grads.forward, c, n))
    place(points - 4, feed_sum.close)
    place(points - 2, feed_sum.final_relays)
    place(points - 2, attn_sum.close)

    def run(i, half):
        for at in range(points):
            if at % 2 == half and moves[at]:

                def go(at=at):
                    for move in moves[at]:
                        move()

                pl.when(i == at // 2)(go)

    states = (xs.at[0], work, low, qkv.at[0], mixed.at[0], middle.at[0])

    def other(i, _):
        @pl.when(i < extras)
        def _():
            fetch(i).wait()
            pl.when(i + 1 < extras)(lambda: fetch(i + 1).start())
            load_rows(rows_in[lax.rem(i, 2)], wide, xs.at[0])
            attention(sizes, bias, vecs, wide_bias, weights, *states, None)

        run(i, 0)

        @pl.when(i < extras)
        def _():
            second_norm(vecs, middle.at[0], work, low)
            feed(sizes, smalls, vecs, weights, middle.at[0], low, work)
            pl.when(i >= 2)(lambda: put(i - 2).wait())
            store_rows(work, wide, rows_out.at[lax.rem(i, 2)], live_scales(chunk_of(i) * BATCH, live))
            put(i).start()

        run(i, 1)
        return 0

    lax.fori_loop(0, most, other, 0)
    for move in moves[points]:
        move()
    attn_sum.final_relays()
    totals.small_total()
    for c in range(exchange):
        results.arrive(c, 1)
    for c in range(own):
        for n in range(1, shards):
            if n < 2 or n == shards - 1:
                grads.arrive(c, n)
    attn_sum.final_wait()
    feed_sum.final_wait()
    sends.finish()
    for c in range(own):
        results.local(c).wait()
        grads.local(c).wait()
    for back_by in (2, 1):
        pl.when(extras >= back_by)(lambda back_by=back_by: put(extras - back_by).wait())


def run_block(sizes, mesh_shape, exchange, live, index, vecs, tokens, cotangent, shard, small):
    d = tokens.shape[1]
    shards, width, units, groups = sizes.shards, sizes.width, sizes.units, sizes.groups
    heads = width // HEAD
    own = tokens.shape[0] // CHUNK // shards
    anywhere = pl.BlockSpec(memory_space=pl.ANY)
    here = pl.BlockSpec(memory_space=pltpu.VMEM)
    dma = pltpu.SemaphoreType.DMA
    total_shape = (8 + shards * units // d + heads, d)
    return pl.pallas_call(
        functools.partial(block_kernel, sizes, mesh_shape, exchange),
        out_shape=(
            jax.ShapeDtypeStruct(tokens.shape, BF16),
            jax.ShapeDtypeStruct(tokens.shape, BF16),
            jax.ShapeDtypeStruct((d, sizes.columns), BF16),
            jax.ShapeDtypeStruct(total_shape, F32),
        ),
        in_specs=[pl.BlockSpec(memory_space=pltpu.SMEM), here, here, anywhere, anywhere, anywhere, anywhere],
        out_specs=(anywhere, anywhere, here, here),
        scratch_shapes=[
            pltpu.VMEM((shards, sizes.columns, d), BF16),
            pltpu.VMEM((shards, *small.shape), F32),
            pltpu.VMEM((1, 3 * width), F32),
            pltpu.VMEM((heads, PAD, LANES), F32),
            pltpu.VMEM((heads, PAD, LANES), F32),
            pltpu.VMEM((shards, d, sizes.columns), F32),
            pltpu.VMEM((own, ROWS, d), F32),
            pltpu.VMEM((own, ROWS, 3 * width), F32),
            pltpu.VMEM((own, ROWS, width), F32),
            pltpu.VMEM((own, ROWS, d), F32),
            pltpu.VMEM((own, BATCH * groups, PAD, PACK * LANES), BF16),
            pltpu.VMEM((CHUNK, d), F32),
            pltpu.VMEM((ROWS, d), F32),
            pltpu.VMEM((ROWS, d), BF16),
            pltpu.VMEM((ROWS, d), BF16),
            pltpu.VMEM((ROWS, d), F32),
            pltpu.VMEM((ROWS, d), F32),
            pltpu.VMEM((8, d), F32),
            pltpu.VMEM((shards, 1, units), F32),
            pltpu.VMEM((TALL, heads * BLOCK), F32),
            pltpu.VMEM((own, CHUNK, d), BF16),
            pltpu.VMEM((own, CHUNK, d), BF16),
            pltpu.VMEM((2, CHUNK, d), BF16),
            pltpu.VMEM((2, CHUNK, d), BF16),
            dma((2,)),
            dma((own,)),
            dma((own,)),
            dma((2,)),
            dma((2,)),
            dma((2, own, 2, 2)),
            dma((2, own, 2, shards)),
            gather_scratch(mesh_shape, 2),
            reduce_scratch(mesh_shape, d, 2 * units),
            reduce_scratch(mesh_shape, d, 4 * sizes.loc),
            totals_scratch(mesh_shape, total_shape),
        ],
        compiler_params=pltpu.CompilerParams(collective_id=0, has_side_effects=True, vmem_limit_bytes=VMEM_LIMIT),
    )(live, index, vecs, tokens, cotangent, shard, small)


def finish_kernel(sizes, z, final, packed, triple, output, expand, shrink, pair, table, unit, *singles):
    loc, units = sizes.loc, sizes.units
    d = final.shape[0]
    count = sizes.width // HEAD // sizes.shards
    triple[...] = final[:, : 3 * loc].astype(F32)
    output[...] = final[:, 3 * loc : 4 * loc].astype(F32).T
    expand[...] = final[:, 4 * loc : 4 * loc + units].astype(F32)
    shrink[...] = final[:, 4 * loc + units :].astype(F32).T
    base = 8 + sizes.shards * units // d
    for s in range(sizes.shards):

        def take(s=s):
            pair[...] = packed[0:2, s * loc : (s + 1) * loc]
            table[...] = packed[base + s * count : base + (s + 1) * count, 0:TALL]
            at = s * units % d
            line = 8 + s * units // d
            unit[...] = packed[line : line + 1, at : at + units]

        pl.when(z[0] == s)(take)
    for ref, line in zip(singles, (6, 7, 5, 3, 4, 2)):
        ref[...] = packed[line : line + 1, :]


def run_finish(sizes, z, final, packed):
    loc, units, d = sizes.loc, sizes.units, final.shape[0]
    count = sizes.width // HEAD // sizes.shards
    shapes = [(d, 3 * loc), (loc, d), (d, units), (units, d), (2, loc), (count, TALL), (1, units)] + [(1, d)] * 6
    here = pl.BlockSpec(memory_space=pltpu.VMEM)
    return pl.pallas_call(
        functools.partial(finish_kernel, sizes),
        out_shape=tuple(jax.ShapeDtypeStruct(shape, F32) for shape in shapes),
        in_specs=[pl.BlockSpec(memory_space=pltpu.SMEM), here, here],
        out_specs=tuple([here] * len(shapes)),
        compiler_params=pltpu.CompilerParams(vmem_limit_bytes=32 * 2**20),
    )(z, final, packed)


def local(
    mesh_shape,
    tokens,
    cotangent,
    group_windows,
    offset_index,
    first_gain,
    first_shift,
    triple_weight,
    query_value_bias,
    bias_table,
    output_weight,
    output_bias,
    second_gain,
    second_shift,
    expand_weight,
    expand_bias,
    shrink_weight,
    shrink_bias,
):
    z = lax.axis_index("mp")
    shards = mesh_shape["mp"]
    d, _, loc = triple_weight.shape
    units = expand_weight.shape[1]
    table_rows, loc_heads = bias_table.shape
    heads = shards * loc_heads
    sizes = Sizes(shards, loc, units)
    shard = jnp.concatenate(
        [triple_weight.transpose(1, 2, 0).reshape(3 * loc, d), output_weight, expand_weight.T, shrink_weight], axis=0
    )

    def widen(v):
        return jnp.pad(v, ((0, 0), (0, 512 - v.shape[1])))

    small = jnp.concatenate(
        [widen(expand_bias[None]), widen(query_value_bias.reshape(1, 2 * loc)), widen(bias_table.T)], axis=0
    ).astype(F32)
    small = jnp.pad(small, ((0, 8 - small.shape[0]), (0, 0)))
    blank = jnp.zeros_like(first_gain)
    vecs = jnp.stack([first_gain, first_shift, output_bias, second_gain, second_shift, shrink_bias, blank, blank]).astype(F32)
    index = jnp.pad(offset_index, ((0, PAD - AREA), (0, LANES - AREA)), constant_values=-1)
    result, grad_tokens, final, packed = run_block(
        sizes, mesh_shape, EXCHANGE, group_windows, index, vecs, tokens, cotangent, shard, small
    )
    triple, output, expand, shrink, pair, table, unit, *singles = run_finish(sizes, z.reshape(1), final, packed)
    first_gain, first_shift, output_sum, second_gain, second_shift, shrink_sum = (v.reshape(d) for v in singles)
    return (
        result,
        grad_tokens,
        first_gain,
        first_shift,
        triple.reshape(d, 3, loc),
        pair,
        table[:, :table_rows].T,
        output,
        output_sum,
        second_gain,
        second_shift,
        expand,
        unit.reshape(units),
        shrink,
        shrink_sum,
    )


EXCHANGE = 0


def solution(mesh):
    in_specs = (
        P("dp", None),
        P("dp", None),
        P("dp"),
        P(),
        P(),
        P(),
        P(None, None, "mp"),
        P(None, "mp"),
        P(None, "mp"),
        P("mp", None),
        P(),
        P(),
        P(),
        P(None, "mp"),
        P("mp"),
        P("mp", None),
        P(),
    )
    out_specs = (
        P("dp", None),
        P("dp", None),
        P(),
        P(),
        P(None, None, "mp"),
        P(None, "mp"),
        P(None, "mp"),
        P("mp", None),
        P(),
        P(),
        P(),
        P(None, "mp"),
        P("mp"),
        P("mp", None),
        P(),
    )
    step = functools.partial(local, dict(mesh.shape))
    return jax.shard_map(step, mesh=mesh, in_specs=in_specs, out_specs=out_specs, check_vma=False)
```

time: 251 us -> 191 us (0.76)
  Pallas kernels: 207 us -> 167 us
  local copies, waits for them, and re-layouts: 28.3 us -> 18 us
  matrix products: 5.22 us -> 0 us
  other arithmetic: 8.09 us -> 3.54 us
    pallas_call x3 -> x2, Pallas kernels: 207 us -> 167 us  [the longest x1 165 us: run_block(): pl.pallas_call(functools.partial(block_kernel, sizes, mesh_shape, exchang...]
    slice x10 -> x0, local copies, waits for them, and re-layouts: 11.3 us -> none  [the longest x2 4.36 us: local(): final[:, :3 * loc].reshape(d, 3, loc)]
    dot_general x2 -> x0, matrix products: 5.22 us -> none  [the longest x1 2.75 us: table_grad(): return jnp.dot(flat.astype(BF16), onehot, preferred_element_type=F32)]
    another operation x8, local copies, waits for them, and re-layouts: 0.07 us -> 4.13 us  [local(): jnp.stack([first_gain, first_shift, output_bias, second_gain, second_shif...]
    unnamed x40 -> x17, local copies, waits for them, and re-layouts: 11.8 us -> 10.4 us
where the time goes in v4:
time: 191 us; the launch traced here: 190 us
  Pallas kernels  167 us (87%)
  local copies, waits for them, and re-layouts  18 us (9%)
  other arithmetic  3.54 us (2%)
    pallas_call x1, Pallas kernels, run_block(): pl.pallas_call(functools.partial(block_kernel, sizes, mesh_shape, exchang...  165 us
    unnamed x17, local copies, waits for them, and re-layouts  10.4 us
    another operation x8, local copies, waits for them, and re-layouts, local(): jnp.stack([first_gain, first_shift, output_bias, second_gain, second_shif...  4.13 us

profile of v4, /device:TPU:0, one launch (start us, length us, event | category | flops | bytes accessed | tf_op | source)
XLA Modules:
  0.0 190.0 jit_solution(15793018569631135900)
XLA Ops:
  0.6 0.0 copy-start.3
  0.7 0.0 copy-start.5
  0.7 0.0 copy-start.4
  1.3 1.4 pad.18.index
  2.8 0.7 stack.24
  3.5 0.7 stack.25
  4.2 0.7 stack.26
  4.8 0.7 stack.27
  5.5 0.7 stack.28
  6.2 0.7 stack.29
  6.9 0.6 convert_element_type.10.vecs
  7.5 1.3 copy.36
  8.8 1.2 copy.35
  10.0 2.3 %pad_maximum_fusion.shard = bf16[1536,512]{1,0:T(8,128)(2,1)} fusion(bf16[512,512]{1,0:T(8,128)(2,1)} %param.32, bf16[512,512]{1,0:T(8,128)(2,1)S(1)} %bitcast.21, bf16[128,512]{1,0:T(8,128)(2,1)} %param.26, bf16[384,512]{1,0:T(8,128)(2,1)S(1)} %bitcast.22), kind=kLoop, calls=%fused_computation | loop fusion | flops 6291456 | bytes 3145728 | tf_op jit(solution)/shard_map/concatenate | solution.py:1074
  12.3 0.0 copy-done.5
  12.3 0.0 copy-done.4
  12.3 0.0 copy-done.3
  12.3 0.6 pad_convert_fusion.small
  12.9 165.3 %shard_map.280 = (bf16[3200,512]{1,0:T(8,128)(2,1)}, bf16[3200,512]{1,0:T(8,128)(2,1)}, bf16[512,1536]{1,0:T(8,128)(2,1)}, f32[28,512]{1,0:T(8,128)}) custom-call(s32[1]{0:T(128)S(6)} %copy.44.live, s32[104,128]{1,0:T(8,128)} %pad.18.index, f32[8,512]{1,0:T(8,128)} %convert_element_type.10.vecs, bf16[3200,512]{1,0:T(8,128)(2,1)} %tokens.1, ...), custom_call_target="tpu_custom_call" | custom-call | tf_op jit(solution)/shard_map/pallas_call | solution.py:959
  178.2 0.0 copy-start
  178.2 1.4 copy-done
  179.6 0.0 copy-start.1
  179.6 0.8 copy-done.1
  180.5 1.8 shard_map.281
  182.3 0.3 copy.37
  182.5 1.1 copy.38
  183.7 0.6 slice_bitcast_fusion
  184.3 0.0 copy-start.2
  184.3 4.0 %copy.45 = bf16[3200,512]{1,0:T(8,128)(2,1)} copy(bf16[3200,512]{1,0:T(8,128)(2,1)} %get-tuple-element.94) | data formatting | bytes 6553600
  188.3 0.0 copy-done.2
  188.3 1.7 copy.46
  (5 shorter events, 0.1 us)
Async XLA Ops:
  0.6 11.6 %copy-start.3 = (bf16[361,4]{0,1:T(4,128)(2,1)S(1)}, bf16[361,4]{0,1:T(4,128)(2,1)}, u32[]{:S(2)}) copy-start(bf16[361,4]{0,1:T(4,128)(2,1)} %param.25) | copy-start | bytes 8668
  0.7 11.6 %copy-start.5 = (bf16[2,128]{1,0:T(2,128)(2,1)S(1)}, bf16[2,128]{1,0:T(2,128)(2,1)}, u32[]{:S(2)}) copy-start(bf16[2,128]{1,0:T(2,128)(2,1)} %param.24) | copy-start | bytes 1540
  0.7 11.6 %copy-start.4 = (bf16[512]{0:T(512)(128)(2,1)S(1)}, bf16[512]{0:T(512)(128)(2,1)}, u32[]{:S(2)}) copy-start(bf16[512]{0:T(512)(128)(2,1)} %param.31) | copy-start | bytes 3076
  178.2 1.4 copy-start
  179.6 0.8 copy-start.1
  184.3 4.0 %copy-start.2 = (bf16[3200,512]{1,0:T(8,128)(2,1)S(1)}, bf16[3200,512]{1,0:T(8,128)(2,1)}, u32[]{:S(2)}) copy-start(bf16[3200,512]{1,0:T(8,128)(2,1)} %get-tuple-element.95) | copy-start | bytes 9830404

commit v5 on v4

--- a/solution.py
+++ b/solution.py
@@ -285,25 +285,27 @@
         self.bits = int(math.log2(self.chips))
         self.dp, self.z = lax.axis_index("dp"), lax.axis_index("mp")
         self.core, self.chip = lax.rem(self.dp, 2), lax.div(self.dp, 2)
+        self.bit_values = [lax.rem(lax.div(self.chip, 1 << b), 2) for b in range(self.bits)]
+        self.flips = [
+            self.chip + sum((1 << b) * (1 - 2 * self.bit_values[b]) for b in range(self.bits) if m >> b & 1)
+            for m in range(self.chips)
+        ]
+        self.rounds = [lax.rem(self.z + k, self.shards) for k in range(self.shards)]
 
     def mate(self):
         return (self.dp + 1 - 2 * self.core, self.z)
 
     def flip(self, m):
-        chip = self.chip
-        for b in range(self.bits):
-            if m >> b & 1:
-                chip = chip + (1 << b) * (1 - 2 * lax.rem(lax.div(self.chip, 1 << b), 2))
-        return chip
+        return self.flips[m]
 
     def across(self, m):
         return (2 * self.flip(m) + self.core, self.z)
 
     def bit(self, b):
-        return lax.rem(lax.div(self.chip, 1 << b), 2)
+        return self.bit_values[b]
 
     def along(self, k):
-        return (self.dp, lax.rem(self.z + k, self.shards))
+        return (self.dp, self.rounds[k])
 
     def greet(self, targets):
         barrier = pltpu.get_barrier_semaphore()
@@ -346,71 +348,137 @@
     def __init__(self, here, sends, out, parts, small, scratch):
         self.here, self.sends, self.out, self.parts, self.small = here, sends, out, parts, small
         self.z_sem, self.s_sem, self.p_sem, self.m_sem = scratch
-        self.order = sorted(range(1, here.shards), key=lambda k: min(k, here.shards - k))
 
     def spot(self, part, shard, dp):
         first, rows = self.parts[part]
         rows //= self.here.n_dp
         return self.out.at[shard, pl.ds(pl.multiple_of(first + dp * rows, 16), rows)]
 
-    def origin(self, k):
-        return lax.rem(self.here.z - k + self.here.shards, self.here.shards)
-
-    def along(self, part, k, arriving=False):
+    def origin(self, way, step):
+        return jnp.clip(self.here.z - (1 - 2 * way) * step, 0, self.here.shards - 1)
+
+    def there(self, way, step, reach=0):
+        held, onward = self.here.z - (1 - 2 * way) * step, self.here.z + (1 - 2 * way) * reach
+        return (held >= 0) & (held < self.here.shards) & (onward >= 0) & (onward < self.here.shards)
+
+    def along(self, part, way, step, arriving=False):
         here = self.here
-        spot = self.spot(part, self.origin(k) if arriving else here.z, here.dp)
-        return remote(spot, spot, self.z_sem.at[0, part, k], self.z_sem.at[1, part, k], here.along(k))
+        spot = self.spot(part, self.origin(way, step), here.dp)
+        at = step - 1 if arriving else step
+        target = (here.dp, jnp.clip(here.z + 1 - 2 * way, 0, here.shards - 1))
+        return remote(spot, spot, self.z_sem.at[0, part, way, at], self.z_sem.at[1, part, way, at], target)
+
+    def along_send(self, part, way, step):
+        self.sends.send(functools.partial(self.along, part, way, step), functools.partial(self.there, way, step, 1))
 
     def small_along(self, k, arriving=False):
-        spot = self.small.at[self.origin(k) if arriving else self.here.z]
-        return remote(spot, spot, self.s_sem.at[0, k], self.s_sem.at[1, k], self.here.along(k))
+        here = self.here
+        spot = self.small.at[here.rounds[here.shards - k] if arriving else here.z]
+        return remote(spot, spot, self.s_sem.at[0, k], self.s_sem.at[1, k], here.along(k))
 
     def start(self):
-        for k in self.order:
+        for k in range(1, self.here.shards):
             self.sends.send(functools.partial(self.small_along, k))
-        self.start_part(0)
+
+    def wait_small(self):
+        for k in range(1, self.here.shards):
+            self.small_along(k, True).wait_recv()
 
     def start_part(self, part):
-        for k in self.order:
-            self.sends.send(functools.partial(self.along, part, k))
-
-    def across(self, part, k, m, arriving=False):
+        for way in range(2):
+            self.along_send(part, way, 0)
+
+    def piece(self, part, way, step, m, core, side=None):
+        spot = self.spot(part, self.origin(way, step), 2 * self.here.flip(m) + core)
+        if side is None:
+            return spot
+        half = self.out.shape[2] // 2
+        return spot.at[:, pl.ds(side * half, half)]
+
+    def hop(self, part, way, step, m, side, bit, arriving=False):
         here = self.here
-        spot = self.spot(part, self.origin(k), 2 * here.flip(m if arriving else 0) + here.core)
-        return remote(spot, spot, self.p_sem.at[0, part, k, m], self.p_sem.at[1, part, k, m], here.across(m))
-
-    def mate(self, part, k, m, arriving=False):
+        spot = self.piece(part, way, step, m | bit if arriving else m, here.core, side)
+        slot = (part, way, step, m | bit, side or 0)
+        return remote(spot, spot, self.p_sem.at[0, *slot], self.p_sem.at[1, *slot], here.across(bit))
+
+    def mate(self, part, way, step, m, side, arriving=False):
         here = self.here
-        spot = self.spot(part, self.origin(k), 2 * here.flip(m) + (1 - here.core if arriving else here.core))
-        return remote(spot, spot, self.m_sem.at[0, part, k, m], self.m_sem.at[1, part, k, m], here.mate())
-
-    def spread(self, part):
-        for k in self.order:
-            self.along(part, k, True).wait_recv()
-            for m in range(1, self.here.chips):
-                self.sends.send(functools.partial(self.across, part, k, m))
-            self.sends.send(functools.partial(self.mate, part, k, 0))
-
-    def relay(self, part):
-        for k in self.order:
-            for m in range(1, self.here.chips):
-                self.across(part, k, m, True).wait_recv()
-                self.sends.send(functools.partial(self.mate, part, k, m))
+        spot = self.piece(part, way, step, m, 1 - here.core if arriving else here.core, side)
+        slot = (part, way, step, m, side or 0)
+        return remote(spot, spot, self.m_sem.at[0, *slot], self.m_sem.at[1, *slot], here.mate())
+
+    def both(self, step, body):
+        for way in range(2):
+            makes = []
+
+            def run(way=way, makes=makes):
+                for make in body(way):
+                    if make is not None:
+                        make().start()
+                        makes.append(make)
+
+            pl.when(self.there(way, step))(run)
+            for make in makes:
+                self.sends.sent.append((make, functools.partial(self.there, way, step)))
+
+    def advance(self, part, step):
+        for way in range(2):
+            pl.when(self.there(way, step))(lambda way=way: self.along(part, way, step, True).wait_recv())
+            if step < self.here.shards - 1:
+                self.along_send(part, way, step)
+
+        def body(way):
+            for b in range(self.here.bits):
+                yield functools.partial(self.hop, part, way, step, 0, None, 1 << b)
+            yield functools.partial(self.mate, part, way, step, 0, None)
+
+        self.both(step, body)
+
+    def pieces(self):
+        bits = self.here.bits
+        orders = (tuple(range(bits)), tuple(reversed(range(bits))))
+        for m in sorted(range(1, self.here.chips), key=lambda m: m.bit_count()):
+            if m.bit_count() == 1:
+                yield m, None, m, [(s, [1 << b for b in o[o.index(m.bit_length() - 1) + 1 :]]) for s, o in enumerate(orders)]
+            else:
+                for s, o in enumerate(orders):
+                    last = max(o.index(b) for b in range(bits) if m >> b & 1)
+                    yield m, s, 1 << o[last], [(s, [1 << b for b in o[last + 1 :]])]
+
+    def relay(self, part, step, far):
+        def body(way):
+            for m, side, bit, onward in self.pieces():
+                if (m.bit_count() > 1) != far:
+                    continue
+                self.hop(part, way, step, m - bit, side, bit, True).wait_recv()
+                for s, later in onward:
+                    for nxt in later:
+                        yield functools.partial(self.hop, part, way, step, m, s, nxt)
+                yield functools.partial(self.mate, part, way, step, m, side)
+
+        self.both(step, body)
 
     def wait(self, part):
-        for k in self.order:
-            for m in range(self.here.chips):
-                self.mate(part, k, m, True).wait_recv()
-
-    def wait_small(self):
-        for k in self.order:
-            self.small_along(k, True).wait_recv()
+        for step in range(1, self.here.shards):
+
+            def body(way, step=step):
+                self.mate(part, way, step, 0, None, True).wait_recv()
+                for m, side, _, _ in self.pieces():
+                    self.mate(part, way, step, m, side, True).wait_recv()
+                return ()
+
+            self.both(step, body)
 
 
 def gather_scratch(mesh_shape, parts):
     shards, chips = mesh_shape["mp"], mesh_shape["dp"] // 2
     dma = pltpu.SemaphoreType.DMA
-    return [dma((2, parts, shards)), dma((2, shards)), dma((2, parts, shards, chips)), dma((2, parts, shards, chips))]
+    return [
+        dma((2, parts, 2, shards)),
+        dma((2, shards)),
+        dma((2, parts, 2, shards, chips, 2)),
+        dma((2, parts, 2, shards, chips, 2)),
+    ]
 
 
 class Lines:
@@ -521,7 +589,7 @@
 
     def shard_copy(self, side, k):
         here = self.here
-        s = lax.rem(here.z + k, here.shards)
+        s = here.rounds[k]
         return remote(
             self.acc.at[s, self.mine(side), self.sides[side]], self.lasts[side].at[k], self.l_sem.at[0, side, k], self.l_sem.at[1, side, k], here.along(k)
         )
@@ -707,9 +775,10 @@
     lax.fori_loop(0, PAD // BLOCK, block, 0)
 
 
-def block_kernel(sizes, mesh_shape, exchange, live, index, vecs, tokens, cotangent, shard, small,
+def block_kernel(sizes, mesh_shape, exchange, early, live, offsets, singles, pair, table_in, unit_in, tokens, cotangent,
+                 triple_in, output_in, expand_in, shrink_in,
                  result, gtok, final, small_out,
-                 weights, smalls, wide_bias, bias, dbias, dw, xs, qkv, mixed, middle, keep,
+                 index, vecs, saved, weights, smalls, wide_bias, bias, dbias, dw, xs, qkv, mixed, middle, keep,
                  wide, work, low, glow, back, gmid, sums, unit_sums, turned,
                  tok_in, cot_in, rows_in, rows_out,
                  own_sem, tok_sem, cot_sem, in_sem, out_sem, result_sem, gtok_sem,
@@ -737,8 +806,8 @@
         return pltpu.make_async_copy(cotangent.at[own_rows(c)], cot_in.at[c], cot_sem.at[c])
 
     mine = [
-        pltpu.make_async_copy(shard, weights.at[here.z], own_sem.at[0]),
-        pltpu.make_async_copy(small, smalls.at[here.z], own_sem.at[1]),
+        pltpu.make_async_copy(output_in, weights.at[here.z, pl.ds(3 * loc, loc)], own_sem.at[0]),
+        pltpu.make_async_copy(shrink_in, weights.at[here.z, pl.ds(4 * loc + units, units)], own_sem.at[1]),
     ]
     for copy in mine:
         copy.start()
@@ -746,47 +815,125 @@
         own_tokens(c).start()
     for c in range(own):
         own_cotangent(c).start()
+    for c in range(3):
+        weights[here.z, c * loc : (c + 1) * loc, :] = triple_in[c].astype(F32).T.astype(BF16)
+    heads = sizes.width // HEAD
+    count = heads // shards
+    smalls[here.z, 0:1, 0:units] = unit_in[...].astype(F32).reshape(1, units)
+    smalls[here.z, 1:2, 0:loc] = pair[0:1, :].astype(F32)
+    smalls[here.z, 1:2, loc : 2 * loc] = pair[1:2, :].astype(F32)
+    smalls[here.z, 2 : 2 + count, 0:TALL] = jnp.zeros((count, TALL), F32)
+    smalls[here.z, 2 : 2 + count, 0 : table_in.shape[1]] = table_in[...].astype(F32)
     here.greet(here.everyone())
-    for copy in mine:
-        copy.wait()
+    mine[0].wait()
+    gather.start_part(0)
     gather.start()
+    weights[here.z, 4 * loc : 4 * loc + units, :] = expand_in[...].astype(F32).T.astype(BF16)
+    mine[1].wait()
+    index[...] = jnp.full(index.shape, -1, jnp.int32)
+    index[0:AREA, 0:AREA] = offsets[...]
+    for line, single in enumerate(singles):
+        vecs[line : line + 1, :] = single[...].astype(F32).reshape(1, vecs.shape[1])
+    steps = range(1, shards)
+    for step in steps:
+        gather.advance(0, step)
+        if step == 1:
+            gather.start_part(1)
+    for step in steps:
+        gather.relay(0, step, False)
+    gather.advance(1, 1)
     xs[...] = jnp.zeros_like(xs)
     dbias[...] = jnp.zeros_like(dbias)
     sums[...] = jnp.zeros_like(sums)
     unit_sums[...] = jnp.zeros_like(unit_sums)
     gather.wait_small()
-    heads = sizes.width // HEAD
-    count = heads // shards
     for z in range(shards):
         at = slice(z * loc, (z + 1) * loc)
         wide_bias[:, at] = smalls[z, 1:2, 0:loc]
         wide_bias[:, slice(2 * sizes.width + z * loc, 2 * sizes.width + (z + 1) * loc)] = smalls[z, 1:2, loc : 2 * loc]
     wide_bias[:, sizes.width : 2 * sizes.width] = jnp.zeros((1, sizes.width), F32)
-    gather.spread(0)
-    gather.start_part(1)
     table = jnp.concatenate([smalls[z, 2 : 2 + count, 0:TALL] for z in range(shards)], axis=0)
     build_bias(index, table, bias)
-    gather.relay(0)
-
+    for step in steps:
+        gather.relay(0, step, True)
+    for step in steps[1:-1]:
+        gather.advance(1, step)
+    gather.wait(0)
+    jobs = {}
+    if shards > 2:
+        jobs.setdefault(0, []).append(functools.partial(gather.advance, 1, shards - 1))
+    for step in steps:
+        at = min((step - 1) // 2, 2 * own - 2)
+        jobs.setdefault(at, []).append(functools.partial(gather.relay, 1, step, False))
+        jobs.setdefault(at + 1, []).append(functools.partial(gather.relay, 1, step, True))
+
+    extra = chunks - own
+    before = jnp.int32(0)
+    if exchange == own:
+        before = jnp.maximum(here.z - 1, 0) * own
+        after = jnp.maximum(shards - 2 - here.z, 0) * own
+        extras, most = before + after, extra - own
+
+        def chunk_of(i):
+            return jnp.where(i < before, i, i - before + (here.z + 2) * own)
+    else:
+        extras, most = jnp.int32(extra), extra
+
+        def chunk_of(i):
+            return lax.rem((here.z + 1) * own + i, chunks)
+
+    def rows(i):
+        return pl.ds(pl.multiple_of(chunk_of(i) * CHUNK, 16), CHUNK)
+
+    def fetch(i):
+        return pltpu.make_async_copy(tokens.at[rows(i)], rows_in.at[lax.rem(i, 2)], in_sem.at[lax.rem(i, 2)])
+
+    def put(i):
+        return pltpu.make_async_copy(rows_out.at[lax.rem(i, 2)], result.at[rows(i)], out_sem.at[lax.rem(i, 2)])
+
+    def attend(c, _):
+        own_tokens(c).wait()
+        load_rows(tok_in[c], wide, xs.at[c])
+
+        def relays(point):
+            for at in sorted(jobs):
+                if at % 2 == point:
+
+                    def run(at=at):
+                        for job in jobs[at]:
+                            job()
+
+                    pl.when(c == at // 2)(run)
+
+        attention(
+            sizes, bias, vecs, wide_bias, weights, xs.at[c], work, low, qkv.at[c], mixed.at[c], middle.at[c], keep.at[c],
+            functools.partial(relays, 0),
+        )
+        relays(1)
+        return 0
+
+    lax.fori_loop(0, own, attend, 0)
     def clear(z, _):
         dw[z] = jnp.zeros_like(dw[z])
         return 0
 
     lax.fori_loop(0, shards, clear, 0)
-    gather.wait(0)
-
-    def attend(c, _):
-        own_tokens(c).wait()
-        load_rows(tok_in[c], wide, xs.at[c])
-
-        def between():
-            pl.when(c == 0)(lambda: gather.spread(1))
-
-        attention(sizes, bias, vecs, wide_bias, weights, xs.at[c], work, low, qkv.at[c], mixed.at[c], middle.at[c], keep.at[c], between)
-        pl.when(c == 0)(lambda: gather.relay(1))
-        return 0
-
-    lax.fori_loop(0, own, attend, 0)
+
+
+    if early:
+        first = dw.at[0, pl.ds(0, ROWS)], dw.at[1, pl.ds(0, ROWS), pl.ds(0, 512)], dw.at[1, pl.ds(0, ROWS), pl.ds(512, 512)]
+
+        def ahead(e, _):
+            at = most - early + e
+            fetch(at).start()
+            fetch(at).wait()
+            load_rows(rows_in[lax.rem(at, 2)], wide, first[1])
+            attention(sizes, bias, vecs, wide_bias, weights, first[1], work, low, first[0], first[2], saved.at[e], None)
+            return 0
+
+        lax.fori_loop(0, early, ahead, 0)
+        for z in range(2):
+            dw[z] = jnp.zeros_like(dw[z])
     gather.wait(1)
 
     def finish(c, _):
@@ -821,7 +968,8 @@
 
             def done(i=i):
                 grads.local(i).start()
-                grads.start(i)
+                grads.send(i, 0, 1)
+                grads.send(i, 0, 2)
 
             pl.when(c == i)(done)
         return 0
@@ -840,30 +988,6 @@
     total[0, base : base + heads, 0:TALL] = jnp.sum(table.reshape(heads, BLOCK, TALL), axis=1)
     totals.small_send(0)
 
-    extra = chunks - own
-    before = jnp.int32(0)
-    if exchange == own:
-        before = jnp.maximum(here.z - 1, 0) * own
-        after = jnp.maximum(shards - 2 - here.z, 0) * own
-        extras, most = before + after, extra - own
-
-        def chunk_of(i):
-            return jnp.where(i < before, i, i - before + (here.z + 2) * own)
-    else:
-        extras, most = jnp.int32(extra), extra
-
-        def chunk_of(i):
-            return lax.rem((here.z + 1) * own + i, chunks)
-
-    def rows(i):
-        return pl.ds(pl.multiple_of(chunk_of(i) * CHUNK, 16), CHUNK)
-
-    def fetch(i):
-        return pltpu.make_async_copy(tokens.at[rows(i)], rows_in.at[lax.rem(i, 2)], in_sem.at[lax.rem(i, 2)])
-
-    def put(i):
-        return pltpu.make_async_copy(rows_out.at[lax.rem(i, 2)], result.at[rows(i)], out_sem.at[lax.rem(i, 2)])
-
     pl.when(extras > 0)(lambda: fetch(0).start())
     bits = here.bits
     points = 2 * most
@@ -874,8 +998,8 @@
 
     place(0, functools.partial(attn_sum.plane, 0))
     for depth in range(1, bits + 1):
-        place(2 * depth - 1, functools.partial(feed_sum.plane, depth))
-        place(2 * depth, functools.partial(attn_sum.plane, depth))
+        place(3 * depth - 2, functools.partial(feed_sum.plane, depth))
+        place(3 * depth - 1, functools.partial(attn_sum.plane, depth))
     for i in range(totals.stages):
 
         def small_step(i=i):
@@ -886,9 +1010,9 @@
                 totals.small_sends()
 
         place(2 * i + 1, small_step)
-    for c in range(own):
-        for n in range(2, shards - 1):
-            place(2 * n - 2 + 6 * c, functools.partial(grads.forward, c, n))
+    for n in range(2, shards - 1):
+        for c in range(own):
+            place(2 * n - 2 + 8 * c, functools.partial(grads.forward, c, n))
     place(points - 4, feed_sum.close)
     place(points - 2, feed_sum.final_relays)
     place(points - 2, attn_sum.close)
@@ -906,14 +1030,19 @@
     states = (xs.at[0], work, low, qkv.at[0], mixed.at[0], middle.at[0])
 
     def other(i, _):
-        @pl.when(i < extras)
+        @pl.when(i < extras - early)
         def _():
             fetch(i).wait()
-            pl.when(i + 1 < extras)(lambda: fetch(i + 1).start())
+            pl.when(i + 1 < extras - early)(lambda: fetch(i + 1).start())
             load_rows(rows_in[lax.rem(i, 2)], wide, xs.at[0])
             attention(sizes, bias, vecs, wide_bias, weights, *states, None)
 
         run(i, 0)
+        if early:
+
+            @pl.when(i >= most - early)
+            def _():
+                middle[0] = saved[i - (most - early)]
 
         @pl.when(i < extras)
         def _():
@@ -947,7 +1076,7 @@
         pl.when(extras >= back_by)(lambda back_by=back_by: put(extras - back_by).wait())
 
 
-def run_block(sizes, mesh_shape, exchange, live, index, vecs, tokens, cotangent, shard, small):
+def run_block(sizes, mesh_shape, exchange, early, live, offsets, singles, pair, table, unit, tokens, cotangent, *raw):
     d = tokens.shape[1]
     shards, width, units, groups = sizes.shards, sizes.width, sizes.units, sizes.groups
     heads = width // HEAD
@@ -957,18 +1086,21 @@
     dma = pltpu.SemaphoreType.DMA
     total_shape = (8 + shards * units // d + heads, d)
     return pl.pallas_call(
-        functools.partial(block_kernel, sizes, mesh_shape, exchange),
+        functools.partial(block_kernel, sizes, mesh_shape, exchange, early),
         out_shape=(
             jax.ShapeDtypeStruct(tokens.shape, BF16),
             jax.ShapeDtypeStruct(tokens.shape, BF16),
             jax.ShapeDtypeStruct((d, sizes.columns), BF16),
             jax.ShapeDtypeStruct(total_shape, F32),
         ),
-        in_specs=[pl.BlockSpec(memory_space=pltpu.SMEM), here, here, anywhere, anywhere, anywhere, anywhere],
+        in_specs=[pl.BlockSpec(memory_space=pltpu.SMEM), here, [here] * 6, here, here, here, anywhere, anywhere, here, anywhere, here, anywhere],
         out_specs=(anywhere, anywhere, here, here),
         scratch_shapes=[
+            pltpu.VMEM((PAD, LANES), jnp.int32),
+            pltpu.VMEM((8, d), F32),
+            pltpu.VMEM((max(early, 1), ROWS, d) if early else (1, 8, LANES), F32),
             pltpu.VMEM((shards, sizes.columns, d), BF16),
-            pltpu.VMEM((shards, *small.shape), F32),
+            pltpu.VMEM((shards, 8, d), F32),
             pltpu.VMEM((1, 3 * width), F32),
             pltpu.VMEM((heads, PAD, LANES), F32),
             pltpu.VMEM((heads, PAD, LANES), F32),
@@ -1004,14 +1136,16 @@
             totals_scratch(mesh_shape, total_shape),
         ],
         compiler_params=pltpu.CompilerParams(collective_id=0, has_side_effects=True, vmem_limit_bytes=VMEM_LIMIT),
-    )(live, index, vecs, tokens, cotangent, shard, small)
-
-
-def finish_kernel(sizes, z, final, packed, triple, output, expand, shrink, pair, table, unit, *singles):
+    )(live, offsets, singles, pair, table, unit, tokens, cotangent, *raw)
+
+
+def finish_kernel(sizes, z, final, packed, *refs):
+    triple, output, expand, shrink, pair, table, unit, *singles = refs
     loc, units = sizes.loc, sizes.units
     d = final.shape[0]
     count = sizes.width // HEAD // sizes.shards
-    triple[...] = final[:, : 3 * loc].astype(F32)
+    for c in range(3):
+        triple[c] = final[:, c * loc : (c + 1) * loc].astype(F32)
     output[...] = final[:, 3 * loc : 4 * loc].astype(F32).T
     expand[...] = final[:, 4 * loc : 4 * loc + units].astype(F32)
     shrink[...] = final[:, 4 * loc + units :].astype(F32).T
@@ -1020,7 +1154,7 @@
 
         def take(s=s):
             pair[...] = packed[0:2, s * loc : (s + 1) * loc]
-            table[...] = packed[base + s * count : base + (s + 1) * count, 0:TALL]
+            table[...] = packed[base + s * count : base + (s + 1) * count, 0 : table.shape[1]]
             at = s * units % d
             line = 8 + s * units // d
             unit[...] = packed[line : line + 1, at : at + units]
@@ -1030,17 +1164,17 @@
         ref[...] = packed[line : line + 1, :]
 
 
-def run_finish(sizes, z, final, packed):
+def run_finish(sizes, table_rows, z, final, packed):
     loc, units, d = sizes.loc, sizes.units, final.shape[0]
     count = sizes.width // HEAD // sizes.shards
-    shapes = [(d, 3 * loc), (loc, d), (d, units), (units, d), (2, loc), (count, TALL), (1, units)] + [(1, d)] * 6
+    shapes = [(3, d, loc), (loc, d), (d, units), (units, d), (2, loc), (count, table_rows), (1, units)] + [(1, d)] * 6
     here = pl.BlockSpec(memory_space=pltpu.VMEM)
     return pl.pallas_call(
         functools.partial(finish_kernel, sizes),
         out_shape=tuple(jax.ShapeDtypeStruct(shape, F32) for shape in shapes),
         in_specs=[pl.BlockSpec(memory_space=pltpu.SMEM), here, here],
         out_specs=tuple([here] * len(shapes)),
-        compiler_params=pltpu.CompilerParams(vmem_limit_bytes=32 * 2**20),
+        compiler_params=pltpu.CompilerParams(vmem_limit_bytes=VMEM_LIMIT),
     )(z, final, packed)
 
 
@@ -1071,33 +1205,36 @@
     table_rows, loc_heads = bias_table.shape
     heads = shards * loc_heads
     sizes = Sizes(shards, loc, units)
-    shard = jnp.concatenate(
-        [triple_weight.transpose(1, 2, 0).reshape(3 * loc, d), output_weight, expand_weight.T, shrink_weight], axis=0
+    early = EARLY if sizes.columns == 3 * sizes.width else 0
+    singles = [first_gain, first_shift, output_bias, second_gain, second_shift, shrink_bias]
+    result, grad_tokens, final, packed = run_block(
+        sizes,
+        mesh_shape,
+        EXCHANGE,
+        early,
+        group_windows,
+        offset_index,
+        singles,
+        query_value_bias,
+        bias_table.T,
+        expand_bias,
+        tokens,
+        cotangent,
+        triple_weight.transpose(1, 0, 2),
+        output_weight,
+        expand_weight,
+        shrink_weight,
     )
-
-    def widen(v):
-        return jnp.pad(v, ((0, 0), (0, 512 - v.shape[1])))
-
-    small = jnp.concatenate(
-        [widen(expand_bias[None]), widen(query_value_bias.reshape(1, 2 * loc)), widen(bias_table.T)], axis=0
-    ).astype(F32)
-    small = jnp.pad(small, ((0, 8 - small.shape[0]), (0, 0)))
-    blank = jnp.zeros_like(first_gain)
-    vecs = jnp.stack([first_gain, first_shift, output_bias, second_gain, second_shift, shrink_bias, blank, blank]).astype(F32)
-    index = jnp.pad(offset_index, ((0, PAD - AREA), (0, LANES - AREA)), constant_values=-1)
-    result, grad_tokens, final, packed = run_block(
-        sizes, mesh_shape, EXCHANGE, group_windows, index, vecs, tokens, cotangent, shard, small
-    )
-    triple, output, expand, shrink, pair, table, unit, *singles = run_finish(sizes, z.reshape(1), final, packed)
+    triple, output, expand, shrink, pair, table, unit, *singles = run_finish(sizes, table_rows, z.reshape(1), final, packed)
     first_gain, first_shift, output_sum, second_gain, second_shift, shrink_sum = (v.reshape(d) for v in singles)
     return (
         result,
         grad_tokens,
         first_gain,
         first_shift,
-        triple.reshape(d, 3, loc),
+        triple.transpose(1, 0, 2),
         pair,
-        table[:, :table_rows].T,
+        table.T,
         output,
         output_sum,
         second_gain,
@@ -1110,6 +1247,7 @@
 
 
 EXCHANGE = 0
+EARLY = 0
 
 
 def solution(mesh):

time: 191 us -> 173 us (0.906)
  local copies, waits for them, and re-layouts: 18 us -> 5.72 us
  other arithmetic: 3.54 us -> 0 us
    unnamed x17 -> x4, local copies, waits for them, and re-layouts: 10.4 us -> 5.72 us
    another operation x8 -> x0, local copies, waits for them, and re-layouts: 4.13 us -> none  [local(): jnp.stack([first_gain, first_shift, output_bias, second_gain, second_shif...]
    pallas_call x1, Pallas kernels: 165 us -> 162 us  [run_block(): pl.pallas_call(functools.partial(block_kernel, sizes, mesh_shape, exchang...]
    concatenate x2 -> x0, other arithmetic: 2.32 us -> none  [the longest x1 2.31 us: local(): jnp.concatenate([triple_weight.transpose(1, 2, 0).reshape(3 * loc, d), ou...]
where the time goes in v5:
time: 173 us
  Pallas kernels  166 us (96%)
  local copies, waits for them, and re-layouts  5.72 us (3%)
    pallas_call x1, Pallas kernels, run_block(): pl.pallas_call(functools.partial(block_kernel, sizes, mesh_shape, exchang...  162 us
    unnamed x4, local copies, waits for them, and re-layouts  5.72 us
    pallas_call x1, Pallas kernels, run_finish(): pl.pallas_call(functools.partial(finish_kernel, sizes), out_shape=tuple((...  3.49 us

profile of v5, /device:TPU:0, one launch (start us, length us, event | category | flops | bytes accessed | tf_op | source)
XLA Modules:
  0.0 172.8 jit_solution(9330188554566042273)
XLA Ops:
  1.3 162.3 %shard_map.280 = (bf16[3200,512]{1,0:T(8,128)(2,1)}, bf16[3200,512]{1,0:T(8,128)(2,1)}, bf16[512,1536]{1,0:T(8,128)(2,1)}, f32[28,512]{1,0:T(8,128)}) custom-call(s32[1]{0:T(128)S(6)} %copy.34.live, s32[100,100]{1,0:T(8,128)} %offsets.1, bf16[512]{0:T(512)(128)(2,1)} %singles_0_.1, bf16[512]{0:T(512)(128)(2,1)} %singles_1_.1, bf16[512]{0:T(512)(128)(2,1)} %singles_2_.1, ...), custom_call_target="tpu_custom_call" | custom-call | tf_op jit(solution)/shard_map/pallas_call | solution.py:1088
  163.6 3.5 %shard_map.281 = (f32[3,512,128]{2,1,0:T(8,128)}, f32[128,512]{1,0:T(8,128)}, f32[512,512]{1,0:T(8,128)}, f32[512,512]{1,0:T(8,128)}, f32[2,128]{1,0:T(2,128)}, ...) custom-call(s32[1]{0:T(128)} %bitcast.2.z, ...), custom_call_target="tpu_custom_call" | custom-call | tf_op jit(solution)/shard_map/pallas_call | solution.py:1172
  167.1 0.0 copy-start
  167.1 4.0 %copy.35 = bf16[3200,512]{1,0:T(8,128)(2,1)} copy(bf16[3200,512]{1,0:T(8,128)(2,1)} %get-tuple-element.64) | data formatting | bytes 6553600
  171.1 0.0 copy-done
  171.1 1.7 copy.36
Async XLA Ops:
  167.1 4.0 %copy-start = (bf16[3200,512]{1,0:T(8,128)(2,1)S(1)}, bf16[3200,512]{1,0:T(8,128)(2,1)}, u32[]{:S(2)}) copy-start(bf16[3200,512]{1,0:T(8,128)(2,1)} %get-tuple-element.65) | copy-start | bytes 9830404

commit v6 on v5

--- a/solution.py
+++ b/solution.py
@@ -51,14 +51,8 @@
 
 
 def normal_cdf(hidden):
-    z = jnp.abs(hidden) * 0.7071067811865476
-    t = 1.0 / (1.0 + 0.3275911 * z)
-    poly = t * (
-        0.127414796 + t * (-0.142248368 + t * (0.7107068705 + t * (-0.7265760135 + t * 0.5307027145)))
-    )
     bell = jnp.exp2(hidden * hidden * (-0.5 * LOG2E))
-    tail = poly * bell
-    return jnp.where(hidden > 0.0, 1.0 - tail, tail), bell
+    return 0.5 + 0.5 * lax.erf(hidden * 0.7071067811865476), bell
 
 
 def head_of(shape, axis):
@@ -208,7 +202,7 @@
         dw[i, :, base + units : base + 2 * units] += dot_tn(glow[...], active)
         return 0
 
-    lax.fori_loop(0, sizes.shards, block, 0, unroll=2)
+    lax.fori_loop(0, sizes.shards, block, 0, unroll=4)
 
 
 def backward(sizes, vecs, weights, xs, work, low, qkv, mixed, middle, glow, back, gmid, keep, dw, dbias, sums, between):

time: 173 us -> 164 us (0.948)
  Pallas kernels: 166 us -> 157 us
    pallas_call x1, Pallas kernels: 162 us -> 153 us  [run_block(): pl.pallas_call(functools.partial(block_kernel, sizes, mesh_shape, exchang...]
where the time goes in v6:
time: 164 us
  Pallas kernels  157 us (96%)
  local copies, waits for them, and re-layouts  5.72 us (3%)
    pallas_call x1, Pallas kernels, run_block(): pl.pallas_call(functools.partial(block_kernel, sizes, mesh_shape, exchang...  153 us
    unnamed x4, local copies, waits for them, and re-layouts  5.72 us
    pallas_call x1, Pallas kernels, run_finish(): pl.pallas_call(functools.partial(finish_kernel, sizes), out_shape=tuple((...  3.49 us

profile of v6, /device:TPU:0, one launch (start us, length us, event | category | flops | bytes accessed | tf_op | source)
XLA Modules:
  0.0 163.8 jit_solution(7869706661306052839)
XLA Ops:
  1.3 153.3 %shard_map.280 = (bf16[3200,512]{1,0:T(8,128)(2,1)}, bf16[3200,512]{1,0:T(8,128)(2,1)}, bf16[512,1536]{1,0:T(8,128)(2,1)}, f32[28,512]{1,0:T(8,128)}) custom-call(s32[1]{0:T(128)S(6)} %copy.34.live, s32[100,100]{1,0:T(8,128)} %offsets.1, bf16[512]{0:T(512)(128)(2,1)} %singles_0_.1, bf16[512]{0:T(512)(128)(2,1)} %singles_1_.1, bf16[512]{0:T(512)(128)(2,1)} %singles_2_.1, ...), custom_call_target="tpu_custom_call" | custom-call | tf_op jit(solution)/shard_map/pallas_call | solution.py:1082
  154.6 3.5 %shard_map.281 = (f32[3,512,128]{2,1,0:T(8,128)}, f32[128,512]{1,0:T(8,128)}, f32[512,512]{1,0:T(8,128)}, f32[512,512]{1,0:T(8,128)}, f32[2,128]{1,0:T(2,128)}, ...) custom-call(s32[1]{0:T(128)} %bitcast.2.z, ...), custom_call_target="tpu_custom_call" | custom-call | tf_op jit(solution)/shard_map/pallas_call | solution.py:1166
  158.1 0.0 copy-start
  158.1 4.0 %copy.35 = bf16[3200,512]{1,0:T(8,128)(2,1)} copy(bf16[3200,512]{1,0:T(8,128)(2,1)} %get-tuple-element.64) | data formatting | bytes 6553600
  162.1 0.0 copy-done
  162.1 1.7 %copy.36 = bf16[3200,512]{1,0:T(8,128)(2,1)} copy(bf16[3200,512]{1,0:T(8,128)(2,1)S(1)} %copy-done) | data formatting | bytes 6553600
Async XLA Ops:
  158.1 4.0 %copy-start = (bf16[3200,512]{1,0:T(8,128)(2,1)S(1)}, bf16[3200,512]{1,0:T(8,128)(2,1)}, u32[]{:S(2)}) copy-start(bf16[3200,512]{1,0:T(8,128)(2,1)} %get-tuple-element.65) | copy-start | bytes 9830404

commit v7 on v6

--- a/solution.py
+++ b/solution.py
@@ -847,11 +847,11 @@
         wide_bias[:, slice(2 * sizes.width + z * loc, 2 * sizes.width + (z + 1) * loc)] = smalls[z, 1:2, loc : 2 * loc]
     wide_bias[:, sizes.width : 2 * sizes.width] = jnp.zeros((1, sizes.width), F32)
     table = jnp.concatenate([smalls[z, 2 : 2 + count, 0:TALL] for z in range(shards)], axis=0)
-    build_bias(index, table, bias)
     for step in steps:
         gather.relay(0, step, True)
     for step in steps[1:-1]:
         gather.advance(1, step)
+    build_bias(index, table, bias)
     gather.wait(0)
     jobs = {}
     if shards > 2:

time: 164 us -> 162 us (0.988)
  Pallas kernels: 157 us -> 155 us
    pallas_call x1, Pallas kernels: 153 us -> 151 us  [run_block(): pl.pallas_call(functools.partial(block_kernel, sizes, mesh_shape, exchang...]
where the time goes in v7:
time: 162 us
  Pallas kernels  155 us (96%)
  local copies, waits for them, and re-layouts  5.72 us (4%)
    pallas_call x1, Pallas kernels, run_block(): pl.pallas_call(functools.partial(block_kernel, sizes, mesh_shape, exchang...  151 us
    unnamed x4, local copies, waits for them, and re-layouts  5.72 us
    pallas_call x1, Pallas kernels, run_finish(): pl.pallas_call(functools.partial(finish_kernel, sizes), out_shape=tuple((...  3.49 us

profile of v7, /device:TPU:0, one launch (start us, length us, event | category | flops | bytes accessed | tf_op | source)
XLA Modules:
  0.0 162.0 jit_solution(13431856695582517270)
XLA Ops:
  1.3 151.5 %shard_map.280 = (bf16[3200,512]{1,0:T(8,128)(2,1)}, bf16[3200,512]{1,0:T(8,128)(2,1)}, bf16[512,1536]{1,0:T(8,128)(2,1)}, f32[28,512]{1,0:T(8,128)}) custom-call(s32[1]{0:T(128)S(6)} %copy.34.live, s32[100,100]{1,0:T(8,128)} %offsets.1, bf16[512]{0:T(512)(128)(2,1)} %singles_0_.1, bf16[512]{0:T(512)(128)(2,1)} %singles_1_.1, bf16[512]{0:T(512)(128)(2,1)} %singles_2_.1, ...), custom_call_target="tpu_custom_call" | custom-call | tf_op jit(solution)/shard_map/pallas_call | solution.py:1082
  152.8 3.5 %shard_map.281 = (f32[3,512,128]{2,1,0:T(8,128)}, f32[128,512]{1,0:T(8,128)}, f32[512,512]{1,0:T(8,128)}, f32[512,512]{1,0:T(8,128)}, f32[2,128]{1,0:T(2,128)}, ...) custom-call(s32[1]{0:T(128)} %bitcast.2.z, ...), custom_call_target="tpu_custom_call" | custom-call | tf_op jit(solution)/shard_map/pallas_call | solution.py:1166
  156.3 0.0 copy-start
  156.3 4.0 %copy.35 = bf16[3200,512]{1,0:T(8,128)(2,1)} copy(bf16[3200,512]{1,0:T(8,128)(2,1)} %get-tuple-element.64) | data formatting | bytes 6553600
  160.3 0.0 copy-done
  160.3 1.7 %copy.36 = bf16[3200,512]{1,0:T(8,128)(2,1)} copy(bf16[3200,512]{1,0:T(8,128)(2,1)S(1)} %copy-done) | data formatting | bytes 6553600
Async XLA Ops:
  156.3 4.0 %copy-start = (bf16[3200,512]{1,0:T(8,128)(2,1)S(1)}, bf16[3200,512]{1,0:T(8,128)(2,1)}, u32[]{:S(2)}) copy-start(bf16[3200,512]{1,0:T(8,128)(2,1)} %get-tuple-element.65) | copy-start | bytes 9830404
